TPU v7x, 128 devices: a whole 4x4x4 slice. The times are simulated.
128 devices in a mesh: sec: 2 (over core), blk: 64 (over x, y, z).
Axes of the slice: x: 4, y: 4, z: 4, core: 2. Of those that a mesh axis runs over, the one named last changes fastest.
Arguments:
- surface_state: float32 [2, 8, 65536], P('sec', None, 'blk'), may hold values from -6 to 6
- neighbours: int32 [2, 6, 65536], P('sec', None, 'blk'), may hold values from 0 to 1151, as said below
- coupling_coef: float32 [2, 2, 6, 65536], P('sec', None, None, 'blk'), may hold values from -0.6 to 0.6
- land: int32 [2, 65536], P('sec', 'blk'), may hold values 0 or 1
- tile_src: int32 [2, 64, 8, 48], P('sec', 'blk'), may hold values from 0 to 7
- dst_lists: int32 [2, 64, 8, 48], replicated, may hold values from -1 to 7
- tiles: bfloat16 [2, 64, 8, 48, 128, 128], P('sec', 'blk'), may hold values from -0.078125 to 0.078125
Outputs:
- section_out: float32 [2, 4, 65536], P('sec', None, 'blk')
Inputs may be any that keep to these rules, and one draw needn't show every extreme that they name: neighbours[s, k, g] is the place of the neighbour in its device's window of 1152 columns, whose places 64 to 1087 are the device's own columns; a neighbour lies at most 64 columns away from g in column order. `dst_lists`: -1 marks an empty slot.
All inputs are finite; a program needn't handle non-finite values. No bound on the sum of `land` on one device may be relied on, other than what follows from the above.
Results may differ from a plain program's by a relative error of at most 0.0018.
Values sent between devices are 32-bit elements; how exact they have to be, the bound alone decides.
No kernel may reach another device: no remote copies, remote signals or barrier semaphores. Data moves between devices by JAX's collectives and lax.ppermute only.
A program may use at most 128 MiB of HBM per device.

v0:
```python
import jax
import jax.numpy as jnp
from jax import lax
from jax.sharding import PartitionSpec as P

TILE = 128
BLK_DEV = 8
FLUX = 10
SURF = 4
HW = 64
SUBSTEPS = 2


def extended(cells, sides, width):
    for axis, dim in sides:
        count = lax.axis_size(axis)
        head = lax.slice_in_dim(cells, 0, width, axis=dim)
        tail = lax.slice_in_dim(cells, cells.shape[dim] - width, cells.shape[dim], axis=dim)
        cells = jnp.concatenate(
            [
                lax.ppermute(tail, axis, [(i, (i + 1) % count) for i in range(count)]),
                cells,
                lax.ppermute(head, axis, [((i + 1) % count, i) for i in range(count)]),
            ],
            axis=dim,
        )
    return cells


def partner(array, axis, stride):
    return lax.ppermute(array, axis, [(i, i ^ 1 << stride) for i in range(lax.axis_size(axis))])


def compute_fluxes(air, ocean_frac):
    wind_speed = jnp.sqrt(air[0] * air[0] + air[1] * air[1] + 1.0)
    sensible = 0.3 * wind_speed * (air[7] - air[2])
    latent = 0.3 * wind_speed * (jnp.tanh(air[7]) - air[3])
    net_short = 0.8 * jax.nn.softplus(air[4])
    net_long = jax.nn.softplus(air[5]) - jax.nn.softplus(air[7])
    rainfall = jax.nn.softplus(air[6])
    fields = jnp.stack(
        [
            0.5 * wind_speed * air[0],
            0.5 * wind_speed * air[1],
            sensible,
            latent,
            net_short,
            net_long,
            rainfall,
            0.5 * latent,
            rainfall - 0.5 * latent,
            net_short + net_long - sensible - latent,
        ]
    )
    return (fields * ocean_frac).astype(jnp.bfloat16)


def body(surface_state, neighbours, coupling_coef, land, tile_src, dst_lists, tiles):
    section = lax.axis_index("sec")
    own_index = lax.axis_index("blk")
    peer_total = lax.axis_size("blk")
    columns_in = surface_state[0]
    links = neighbours[0]
    couple = coupling_coef[0]
    wet_mask = land[0].astype(jnp.float32)
    senders = tile_src[0, 0]
    weights = tiles[0, 0]
    count_cols = columns_in.shape[1]
    recv_count = senders.shape[0]
    targets = jnp.arange(BLK_DEV, dtype=jnp.int32)
    shifts = [i - (recv_count - 1) // 2 for i in range(recv_count - 1)] + [peer_total // 2]
    shift_table = jnp.array(shifts, dtype=jnp.int32)
    peer_ids = jnp.arange(peer_total, dtype=jnp.int32)
    anchor = (own_index - shift_table) % peer_total
    offset_ids = jnp.arange(recv_count, dtype=jnp.int32)

    def spread(values):
        window = extended(values, (("blk", 1),), HW)
        return jnp.take(window, links, axis=1) - values[:, None, :]

    def route(payload):
        destination = (own_index + shift_table) % peer_total
        place = (destination[:, None] == peer_ids[None, :]).astype(jnp.float32)
        padded = jnp.einsum("in,isfp->nsfp", place, payload, precision=lax.Precision.HIGHEST)
        received = lax.all_to_all(padded, "blk", split_axis=0, concat_axis=0, tiled=True)
        pick = (anchor[:, None] == peer_ids[None, :]).astype(jnp.float32)
        return jnp.einsum("in,nsfp->isfp", pick, received, precision=lax.Precision.HIGHEST)

    def remap(make_fields, field_count, direction):
        dst_all = dst_lists[direction]
        slot_count = senders.shape[1]

        def outgoing():
            fields = make_fields()
            blocks = fields.reshape(field_count, BLK_DEV, TILE).transpose(1, 0, 2)
            picked = blocks[senders]
            partials = jnp.einsum(
                "ijpq,ijfq->ijfp", weights, picked, preferred_element_type=jnp.float32
            )
            return partials

        def silent():
            return jnp.zeros((recv_count, slot_count, field_count, TILE), jnp.float32)

        payload = lax.cond(section == direction, outgoing, silent)
        crossed = partner(payload, "sec", 0)
        dst_rows = dst_all[anchor, offset_ids]
        select = (dst_rows[..., None] == targets).astype(jnp.float32)
        result = jnp.einsum(
            "ijb,ijfp->bfp", select, route(crossed), precision=lax.Precision.HIGHEST
        )
        return result.transpose(1, 0, 2).reshape(field_count, count_cols)

    forcing = remap(lambda: compute_fluxes(columns_in, wet_mask), FLUX, 0)
    height = columns_in[0]
    flow_u = columns_in[1]
    flow_v = columns_in[2]
    depth = 1.0 + jax.nn.sigmoid(columns_in[3])
    ice_frac = jax.nn.sigmoid(columns_in[5])
    coriol = 0.3 * jnp.tanh(columns_in[6])
    mixed = 1.0 + jax.nn.softplus(columns_in[7])
    grad_wx = couple[0]
    grad_wy = couple[1]
    drag = 0.3 * (1.0 - ice_frac)
    for substep in range(SUBSTEPS):
        slopes = spread(height[None])[0]
        next_u = wet_mask * (
            flow_u - 0.5 * jnp.sum(grad_wx * slopes, axis=0) + coriol * flow_v + drag * forcing[0]
        )
        next_v = wet_mask * (
            flow_v - 0.5 * jnp.sum(grad_wy * slopes, axis=0) - coriol * flow_u + drag * forcing[1]
        )
        moved = spread(jnp.stack([depth * next_u, depth * next_v]))
        height = (
            height
            - 0.5 * jnp.sum(grad_wx * moved[0] + grad_wy * moved[1], axis=0)
            + 0.1 * forcing[8]
        )
        flow_u = next_u
        flow_v = next_v
    new_temp = columns_in[4] + 0.2 * wet_mask * forcing[9] / mixed
    surface = jnp.stack([new_temp, ice_frac, flow_u, flow_v]).astype(jnp.bfloat16)
    returned = remap(lambda: surface, SURF, 1)
    chosen = jnp.stack([couple[0], couple[0], couple[1], couple[1]])
    smoothed = returned + jnp.sum(chosen * spread(returned), axis=1)
    air_out = wet_mask * smoothed
    sea_out = jnp.stack([height, flow_u, flow_v, new_temp])
    return jnp.where(section == 0, air_out, sea_out)[None]


def solution(mesh):
    in_specs = (
        P("sec", None, "blk"),
        P("sec", None, "blk"),
        P("sec", None, None, "blk"),
        P("sec", "blk"),
        P("sec", "blk", None, None),
        P(),
        P("sec", "blk", None, None, None, None),
    )
    out_specs = P("sec", None, "blk")
    return jax.shard_map(body, mesh=mesh, in_specs=in_specs, out_specs=out_specs, check_vma=False)
```

profile of v0, /device:TPU:1, one launch (start us, length us, event | category | flops | bytes accessed | tf_op | source)
XLA Modules:
  0.0 615.8 jit_solution(2771430878442241007)
XLA Ops:
  0.0 0.3 conditional.2
  0.0 0.3 broadcast.524
  0.3 1.9 copy.108
  2.2 16.5 %collective-permute-start = (f32[8,48,10,128]{3,1,2,0:T(8,128)}, f32[8,48,10,128]{3,1,2,0:T(8,128)S(1)}, u32[]{:S(2)}, u32[]{:S(2)}) collective-permute-start(f32[8,48,10,128]{3,1,2,0:T(8,128)} %copy.108), channel_id=1, source_target_pairs={{0,64},{64,0},{1,65},{65,1},{2,66},{66,2},{3,67},{67,3},{4,68},{68... | collective-permute-start | bytes 5898248 | tf_op jit(solution)/shard_map/ppermute | solution.py:31
  18.7 3.8 collective-permute-done
  22.5 9.3 %fusion.9 = f32[64,48,10,128]{3,0,2,1:T(8,128)} fusion(f32[8,48,10,128]{3,1,2,0:T(8,128)S(1)} %collective-permute-done, s32[8]{0:T(128)S(1)} %and_select_fusion), kind=kOutput, calls=%fused_computation.40 | convolution fusion | flops 377487872 | bytes 17694752 | tf_op jit(solution)/shard_map/in,isfp->nsfp/dot_general | solution.py:84
  31.8 20.0 %copy.110 = f32[64,48,10,128]{3,1,2,0:T(8,128)} copy(f32[64,48,10,128]{3,0,2,1:T(8,128)} %fusion.9) | data formatting | bytes 31457280 | tf_op jit(solution)/shard_map/in,isfp->nsfp/dot_general | solution.py:84
  51.8 11.8 %all-to-all-start = ((f32[64,48,10,128]{3,1,2,0:T(8,128)}), f32[64,48,10,128]{3,1,2,0:T(8,128)}, u32[]{:S(2)}, u32[]{:S(2)}) async-start(f32[64,48,10,128]{3,1,2,0:T(8,128)} %copy.110), calls=%async_computation | async-start | bytes 31457280 | tf_op jit(solution)/shard_map/all_to_all | solution.py:85
  63.7 0.6 fusion.92
  64.3 0.9 collective-permute-start.1
  65.3 6.0 collective-permute-start.2
  71.3 0.1 copy.131
  71.6 0.6 gather_fusion.3
  72.2 172.1 %collective-permute-done.1 = f32[1,64]{1,0:T(1,128)S(1)} collective-permute-done((f32[1,64]{1,0:T(1,128)S(1)}, f32[1,64]{1,0:T(1,128)S(1)}, u32[]{:S(2)}, u32[]{:S(2)}) %collective-permute-start.1) | collective-permute-done | bytes 288 | tf_op jit(solution)/shard_map/ppermute | solution.py:21
  244.3 4.0 collective-permute-done.2
  248.2 0.1 concatenate.28
  248.4 34.3 %gather_fusion.5 = f32[6144]{0:T(1024)S(1)} fusion(f32[1152]{0:T(1024)S(1)} %reduce, s32[6144]{0:T(1024)S(1)} %broadcast_clamp_fusion.1), kind=kCustom, calls=%fused_computation.1.clone | custom fusion | bytes 73728 | tf_op jit(solution)/shard_map/jit(_take)/gather | solution.py:79
  282.7 21.4 %all-to-all-done = f32[64,48,10,128]{3,1,2,0:T(8,128)} async-done(((f32[64,48,10,128]{3,1,2,0:T(8,128)}), f32[64,48,10,128]{3,1,2,0:T(8,128)}, u32[]{:S(2)}, u32[]{:S(2)}) %all-to-all-start) | async-done | bytes 15728672 | tf_op jit(solution)/shard_map/all_to_all | solution.py:85
  304.2 18.4 %fusion.3 = f32[8,48,10,128]{3,0,2,1:T(8,128)S(1)} fusion(f32[64,48,10,128]{3,1,2,0:T(8,128)} %all-to-all-done, s32[8]{0:T(128)S(1)} %get-tuple-element.64), kind=kOutput, calls=%fused_computation.34 | convolution fusion | flops 377487872 | bytes 17694752 | tf_op jit(solution)/shard_map/in,nsfp->isfp/dot_general | solution.py:87
  322.6 1.3 fusion.11
  323.8 0.6 slice_multiply_fusion
  324.4 0.6 bitcast_multiply_fusion.2
  325.1 0.6 bitcast_multiply_fusion.3
  325.8 1.0 collective-permute-start.3
  326.7 5.9 collective-permute-start.4
  332.7 0.9 collective-permute-done.3
  333.6 0.1 concatenate.29
  333.7 1.1 copy.115
  334.8 17.1 %gather_fusion.6 = f32[6144,2]{1,0:T(8,128)S(1)} fusion(f32[2,1152]{0,1:T(8,128)} %copy.115, s32[6144]{0:T(1024)S(1)} %broadcast_clamp_fusion.1), kind=kCustom, calls=%fused_computation.2.clone | custom fusion | bytes 122880 | tf_op jit(solution)/shard_map/jit(_take)/gather | solution.py:79
  352.0 1.5 copy.116
  353.4 0.7 bitcast_subtract_fusion.2
  354.2 0.7 subtract_add_fusion.2
  355.0 5.8 collective-permute-start.5
  360.8 17.2 %collective-permute-start.6 = (f32[1,64]{1,0:T(1,128)S(1)}, f32[1,64]{1,0:T(1,128)S(1)}, u32[]{:S(2)}, u32[]{:S(2)}) collective-permute-start(f32[1,64]{1,0:T(1,128)S(1)} %get-tuple-element.97), channel_id=1, source_target_pairs={{1,0},{2,1},{3,2},{4,3},{5,4},{6,5},{7,6},{8,7},{9,8},{10,9},{11,1... | collective-permute-start | bytes 776 | tf_op jit(solution)/shard_map/ppermute | solution.py:23
  378.0 0.7 subtract_add_fusion.1
  378.7 0.1 concatenate.30
  378.9 34.3 %gather_fusion.7 = f32[6144]{0:T(1024)S(1)} fusion(f32[1152]{0:T(1024)S(1)} %reduce.1, s32[6144]{0:T(1024)S(1)} %broadcast_clamp_fusion.1), kind=kCustom, calls=%fused_computation.4.clone | custom fusion | bytes 73728 | tf_op jit(solution)/shard_map/jit(_take)/gather | solution.py:79
  413.5 11.6 %conditional.3 = (f32[8,48,4,128]{3,2,1,0:T(4,128)S(1)}) conditional(s32[]{:T(128)} %convert_element_type.36, () %tuple.19, (bf16[4,1024]{1,0:T(4,128)(2,1)S(1)}, s32[8,48]{1,0:T(8,128)S(1)}, bf16[8,48,128,128]{3,2,1,0:T(8,128)(2,1)}) %tuple.71), branch_computations={%region_7.10_spmd, %region_8.11_spmd} | conditional | flops 50333824 | bytes 14562312 | solution.py:105
  413.6 2.0 gather_fusion.1
  415.6 9.5 %fusion.96 = f32[8,48,4,128]{3,2,1,0:T(4,128)S(1)} fusion(bf16[8,48,4,128]{3,2,1,0:T(4,128)(2,1)S(1)} %bitcast.286, bf16[8,48,128,128]{3,2,1,0:T(8,128)(2,1)} %get-tuple-element.36), kind=kOutput, calls=%fused_computation.189 | convolution fusion | flops 50331648 | bytes 13762560 | tf_op jit(solution)/shard_map/cond/branch_1_fun/ijpq,ijfq->ijfp/dot_general | solution.py:97
  425.1 0.5 copy.117
  425.7 2.3 collective-permute-done.7
  428.0 2.8 fusion.63
  430.7 6.7 %copy.118 = f32[64,48,4,128]{3,2,1,0:T(4,128)} copy(f32[64,48,4,128]{3,0,2,1:T(8,128)S(1)} %fusion.63) | data formatting | bytes 12582912 | tf_op jit(solution)/shard_map/in,isfp->nsfp/dot_general | solution.py:84
  437.4 40.6 %all-to-all-start.1 = ((f32[64,48,4,128]{3,2,1,0:T(4,128)}), f32[64,48,4,128]{3,2,1,0:T(4,128)}, u32[]{:S(2)}, u32[]{:S(2)}) async-start(f32[64,48,4,128]{3,2,1,0:T(4,128)} %copy.118), calls=%async_computation.1 | async-start | bytes 12582912 | tf_op jit(solution)/shard_map/all_to_all | solution.py:85
  478.1 0.1 copy.130
  478.2 0.6 gather_fusion.2
  479.0 1.0 collective-permute-start.10
  479.9 6.2 collective-permute-start.11
  486.1 56.6 %collective-permute-done.10 = f32[2,64]{1,0:T(2,128)S(1)} collective-permute-done((f32[2,64]{1,0:T(2,128)S(1)}, f32[2,64]{1,0:T(2,128)S(1)}, u32[]{:S(2)}, u32[]{:S(2)}) %collective-permute-start.10) | collective-permute-done | bytes 544 | tf_op jit(solution)/shard_map/ppermute | solution.py:21
  542.6 6.1 collective-permute-done.11
  548.7 0.1 concatenate.32
  548.8 1.1 copy.123
  550.0 17.1 %gather_fusion.8 = f32[6144,2]{1,0:T(8,128)S(1)} fusion(f32[2,1152]{0,1:T(8,128)} %copy.123, s32[6144]{0:T(1024)S(1)} %broadcast_clamp_fusion.1), kind=kCustom, calls=%fused_computation.5.clone | custom fusion | bytes 122880 | tf_op jit(solution)/shard_map/jit(_take)/gather | solution.py:79
  567.1 1.5 copy.124
  568.7 8.3 %fusion.5 = f32[8,48,4,128]{3,0,2,1:T(8,128)S(1)} fusion(f32[64,48,4,128]{3,2,1,0:T(4,128)} %all-to-all-done.1, s32[8]{0:T(128)S(1)} %copy-done.23), kind=kOutput, calls=%fused_computation.36 | convolution fusion | flops 150995456 | bytes 7077920 | tf_op jit(solution)/shard_map/in,nsfp->isfp/dot_general | solution.py:87
  576.9 0.8 fusion.14
  577.9 12.1 %collective-permute-start.9 = (f32[4,64]{1,0:T(4,128)S(1)}, f32[4,64]{1,0:T(4,128)S(1)}, u32[]{:S(2)}, u32[]{:S(2)}) collective-permute-start(f32[4,64]{1,0:T(4,128)S(1)} %get-tuple-element.89), channel_id=1, source_target_pairs={{1,0},{2,1},{3,2},{4,3},{5,4},{6,5},{7,6},{8,7},{9,8},{10,9},{11,1... | collective-permute-start | bytes 3080 | tf_op jit(solution)/shard_map/ppermute | solution.py:23
  590.0 0.9 collective-permute-done.8
  590.9 0.1 concatenate.31
  591.0 0.3 copy.121
  591.3 20.9 %gather_fusion.4 = f32[6144,4]{1,0:T(8,128)} fusion(f32[4,1152]{0,1:T(8,128)S(1)} %copy.121, s32[6144]{0:T(1024)S(1)} %broadcast_clamp_fusion), kind=kCustom, calls=%fused_computation.8 | custom fusion | bytes 221184 | tf_op jit(solution)/shard_map/jit(_take)/gather | solution.py:79
  612.2 2.7 copy.122
  615.0 0.6 maximum_select_fusion
  (105 shorter events, 1.3 us)
Async XLA Ops:
  0.3 18.4 %copy-start.27 = (s32[8]{0:T(128)S(1)}, s32[8]{0:T(128)}, u32[]{:S(2)}) copy-start(s32[8]{0:T(128)} %constant.115.clone) | copy-start | bytes 100
  2.2 20.3 %collective-permute-start = (f32[8,48,10,128]{3,1,2,0:T(8,128)}, f32[8,48,10,128]{3,1,2,0:T(8,128)S(1)}, u32[]{:S(2)}, u32[]{:S(2)}) collective-permute-start(f32[8,48,10,128]{3,1,2,0:T(8,128)} %copy.108), channel_id=1, source_target_pairs={{0,64},{64,0},{1,65},{65,1},{2,66},{66,2},{3,67},{67,3},{4,68},{68... | collective-permute-start | bytes 5898248 | tf_op jit(solution)/shard_map/ppermute | solution.py:31
  18.7 3.8 copy-start.24
  51.8 11.8 %copy-start.1 = (f32[1,8,1024]{2,1,0:T(8,128)S(1)}, f32[1,8,1024]{2,1,0:T(8,128)}, u32[]{:S(2)}) copy-start(f32[1,8,1024]{2,1,0:T(8,128)} %param.16) | copy-start | bytes 98308
  51.8 19.4 %copy-start = (s32[2,64,8,48]{1,3,2,0:T(8,128)S(1)}, s32[2,64,8,48]{1,3,2,0:T(8,128)}, u32[]{:S(2)}) copy-start(s32[2,64,8,48]{1,3,2,0:T(8,128)} %param.21) | copy-start | bytes 589828
  51.8 19.6 %copy-start.2 = (s32[1,6,1024]{2,0,1:T(1,128)S(1)}, s32[1,6,1024]{2,0,1:T(1,128)}, u32[]{:S(2)}) copy-start(s32[1,6,1024]{2,0,1:T(1,128)} %param.17) | copy-start | bytes 73732
  51.8 19.6 %copy-start.26 = (s32[8]{0:T(128)S(1)}, s32[8]{0:T(128)}, u32[]{:S(2)}) copy-start(s32[8]{0:T(128)} %constant.122) | copy-start | bytes 100
  51.8 19.7 %copy-start.8 = (f32[1,2,6,1024]{3,1,2,0:T(2,128)S(1)}, f32[1,2,6,1024]{3,1,2,0:T(2,128)}, u32[]{:S(2)}) copy-start(f32[1,2,6,1024]{3,1,2,0:T(2,128)} %param.18) | copy-start | bytes 147460
  51.8 252.3 %all-to-all-start = ((f32[64,48,10,128]{3,1,2,0:T(8,128)}), f32[64,48,10,128]{3,1,2,0:T(8,128)}, u32[]{:S(2)}, u32[]{:S(2)}) async-start(f32[64,48,10,128]{3,1,2,0:T(8,128)} %copy.110), calls=%async_computation | async-start | bytes 31457280 | tf_op jit(solution)/shard_map/all_to_all | solution.py:85
  64.3 260.8 %copy-start.5 = (f32[1,1,1024]{2,1,0:T(1,128)}, f32[1,1,1024]{2,1,0:T(1,128)S(1)}, u32[]{:S(2)}) copy-start(f32[1,1,1024]{2,1,0:T(1,128)S(1)} %get-tuple-element.88) | copy-start | bytes 12292
  64.3 179.9 %collective-permute-start.1 = (f32[1,64]{1,0:T(1,128)S(1)}, f32[1,64]{1,0:T(1,128)S(1)}, u32[]{:S(2)}, u32[]{:S(2)}) collective-permute-start(f32[1,64]{1,0:T(1,128)S(1)} %get-tuple-element.100), channel_id=1, source_target_pairs={{0,1},{1,2},{2,3},{3,4},{4,5},{5,6},{6,7},{7,8},{8,9},{9,10},{10,1... | collective-permute-start | bytes 776 | tf_op jit(solution)/shard_map/ppermute | solution.py:21
  65.3 182.9 %collective-permute-start.2 = (f32[1,64]{1,0:T(1,128)S(1)}, f32[1,64]{1,0:T(1,128)S(1)}, u32[]{:S(2)}, u32[]{:S(2)}) collective-permute-start(f32[1,64]{1,0:T(1,128)S(1)} %get-tuple-element.99), channel_id=1, source_target_pairs={{1,0},{2,1},{3,2},{4,3},{5,4},{6,5},{7,6},{8,7},{9,8},{10,9},{11,1... | collective-permute-start | bytes 776 | tf_op jit(solution)/shard_map/ppermute | solution.py:23
  71.5 232.6 %copy-start.22 = (s32[8]{0:T(128)}, s32[8]{0:T(128)S(1)}, u32[]{:S(2)}) copy-start(s32[8]{0:T(128)S(1)} %get-tuple-element.64) | copy-start | bytes 100
  304.2 20.3 %copy-start.3 = (s32[1,1024]{1,0:T(1,128)S(1)}, s32[1,1024]{1,0:T(1,128)}, u32[]{:S(2)}) copy-start(s32[1,1024]{1,0:T(1,128)} %param.19) | copy-start | bytes 12292
  324.4 0.6 copy-start.15
  324.4 27.5 %copy-start.13 = (f32[1,8,128]{2,1,0:T(8,128)}, f32[1,8,128]{2,1,0:T(8,128)S(1)}, u32[]{:S(2)}) copy-start(f32[1,8,128]{2,1,0:T(8,128)S(1)} %get-tuple-element.81) | copy-start | bytes 12292
  325.1 1.7 copy-start.11
  325.8 7.9 %collective-permute-start.3 = (f32[2,64]{1,0:T(2,128)S(1)}, f32[2,64]{1,0:T(2,128)S(1)}, u32[]{:S(2)}, u32[]{:S(2)}) collective-permute-start(f32[2,64]{1,0:T(2,128)S(1)} %get-tuple-element.94), channel_id=1, source_target_pairs={{0,1},{1,2},{2,3},{3,4},{4,5},{5,6},{6,7},{7,8},{8,9},{9,10},{10,1... | collective-permute-start | bytes 1544 | tf_op jit(solution)/shard_map/ppermute | solution.py:21
  326.7 6.9 %collective-permute-start.4 = (f32[2,64]{1,0:T(2,128)S(1)}, f32[2,64]{1,0:T(2,128)S(1)}, u32[]{:S(2)}, u32[]{:S(2)}) collective-permute-start(f32[2,64]{1,0:T(2,128)S(1)} %get-tuple-element.93), channel_id=1, source_target_pairs={{1,0},{2,1},{3,2},{4,3},{5,4},{6,5},{7,6},{8,7},{9,8},{10,9},{11,1... | collective-permute-start | bytes 1544 | tf_op jit(solution)/shard_map/ppermute | solution.py:23
  332.7 19.3 %copy-start.4 = (f32[2,1024]{1,0:T(2,128)}, f32[2,1024]{1,0:T(2,128)S(1)}, u32[]{:S(2)}) copy-start(f32[2,1024]{1,0:T(2,128)S(1)} %pad_maximum_fusion) | copy-start | bytes 24580
  355.0 23.7 %collective-permute-start.5 = (f32[1,64]{1,0:T(1,128)S(1)}, f32[1,64]{1,0:T(1,128)S(1)}, u32[]{:S(2)}, u32[]{:S(2)}) collective-permute-start(f32[1,64]{1,0:T(1,128)S(1)} %get-tuple-element.98), channel_id=1, source_target_pairs={{0,1},{1,2},{2,3},{3,4},{4,5},{5,6},{6,7},{7,8},{8,9},{9,10},{10,1... | collective-permute-start | bytes 776 | tf_op jit(solution)/shard_map/ppermute | solution.py:21
  360.8 17.9 %collective-permute-start.6 = (f32[1,64]{1,0:T(1,128)S(1)}, f32[1,64]{1,0:T(1,128)S(1)}, u32[]{:S(2)}, u32[]{:S(2)}) collective-permute-start(f32[1,64]{1,0:T(1,128)S(1)} %get-tuple-element.97), channel_id=1, source_target_pairs={{1,0},{2,1},{3,2},{4,3},{5,4},{6,5},{7,6},{8,7},{9,8},{10,9},{11,1... | collective-permute-start | bytes 776 | tf_op jit(solution)/shard_map/ppermute | solution.py:23
  378.7 34.6 %copy-start.9 = (f32[1,1,1024]{2,1,0:T(1,128)}, f32[1,1,1024]{2,1,0:T(1,128)S(1)}, u32[]{:S(2)}) copy-start(f32[1,1,1024]{2,1,0:T(1,128)S(1)} %subtract_add_fusion.1) | copy-start | bytes 12292
  378.8 34.5 %copy-start.6 = (f32[1,1,1024]{2,1,0:T(1,128)S(1)}, f32[1,1,1024]{2,1,0:T(1,128)}, u32[]{:S(2)}) copy-start(f32[1,1,1024]{2,1,0:T(1,128)} %copy-done.5) | copy-start | bytes 12292
  378.8 34.5 %copy-start.14 = (f32[1,8,128]{2,1,0:T(8,128)S(1)}, f32[1,8,128]{2,1,0:T(8,128)}, u32[]{:S(2)}) copy-start(f32[1,8,128]{2,1,0:T(8,128)} %copy-done.13) | copy-start | bytes 12292
  378.8 34.5 %copy-start.16 = (f32[1,8,128]{2,1,0:T(8,128)S(1)}, f32[1,8,128]{2,1,0:T(8,128)}, u32[]{:S(2)}) copy-start(f32[1,8,128]{2,1,0:T(8,128)} %copy-done.15) | copy-start | bytes 12292
  378.9 34.5 %copy-start.17 = (f32[1,1024]{1,0:T(1,128)S(1)}, f32[1,1024]{1,0:T(1,128)}, u32[]{:S(2)}) copy-start(f32[1,1024]{1,0:T(1,128)} %get-tuple-element.61) | copy-start | bytes 12292
  378.9 34.5 %copy-start.20 = (f32[1,8,128]{2,1,0:T(8,128)S(1)}, f32[1,8,128]{2,1,0:T(8,128)}, u32[]{:S(2)}) copy-start(f32[1,8,128]{2,1,0:T(8,128)} %get-tuple-element.82) | copy-start | bytes 12292
  378.9 34.5 %copy-start.21 = (f32[1,1024]{1,0:T(1,128)S(1)}, f32[1,1024]{1,0:T(1,128)}, u32[]{:S(2)}) copy-start(f32[1,1024]{1,0:T(1,128)} %get-tuple-element.59) | copy-start | bytes 12292
  378.9 34.5 %copy-start.19 = (bf16[1,1024]{1,0:T(2,128)(2,1)S(1)}, bf16[1,1024]{1,0:T(2,128)(2,1)}, u32[]{:S(2)}) copy-start(bf16[1,1024]{1,0:T(2,128)(2,1)} %get-tuple-element.87) | copy-start | bytes 6148
  378.9 34.6 %copy-start.18 = (s32[1,1,8,48]{3,2,1,0:T(8,128)S(1)}, s32[1,1,8,48]{3,2,1,0:T(8,128)}, u32[]{:S(2)}) copy-start(s32[1,1,8,48]{3,2,1,0:T(8,128)} %param.20) | copy-start | bytes 4612
  413.5 14.5 %copy-start.25 = (s32[8]{0:T(128)S(1)}, s32[8]{0:T(128)}, u32[]{:S(2)}) copy-start(s32[8]{0:T(128)} %copy-done.24) | copy-start | bytes 100
  425.6 2.4 collective-permute-start.7
  437.4 41.4 %copy-start.12 = (f32[1,1,1024]{2,1,0:T(1,128)S(1)}, f32[1,1,1024]{2,1,0:T(1,128)}, u32[]{:S(2)}) copy-start(f32[1,1,1024]{2,1,0:T(1,128)} %copy-done.11) | copy-start | bytes 12292
  437.4 131.2 %all-to-all-start.1 = ((f32[64,48,4,128]{3,2,1,0:T(4,128)}), f32[64,48,4,128]{3,2,1,0:T(4,128)}, u32[]{:S(2)}, u32[]{:S(2)}) async-start(f32[64,48,4,128]{3,2,1,0:T(4,128)} %copy.118), calls=%async_computation.1 | async-start | bytes 12582912 | tf_op jit(solution)/shard_map/all_to_all | solution.py:85
  478.0 90.6 %copy-start.23 = (s32[8]{0:T(128)S(1)}, s32[8]{0:T(128)}, u32[]{:S(2)}) copy-start(s32[8]{0:T(128)} %copy-done.22) | copy-start | bytes 100
  479.0 63.7 %collective-permute-start.10 = (f32[2,64]{1,0:T(2,128)S(1)}, f32[2,64]{1,0:T(2,128)S(1)}, u32[]{:S(2)}, u32[]{:S(2)}) collective-permute-start(f32[2,64]{1,0:T(2,128)S(1)} %get-tuple-element.92), channel_id=1, source_target_pairs={{0,1},{1,2},{2,3},{3,4},{4,5},{5,6},{6,7},{7,8},{8,9},{9,10},{10,1... | collective-permute-start | bytes 1544 | tf_op jit(solution)/shard_map/ppermute | solution.py:21
  479.9 68.8 %collective-permute-start.11 = (f32[2,64]{1,0:T(2,128)S(1)}, f32[2,64]{1,0:T(2,128)S(1)}, u32[]{:S(2)}, u32[]{:S(2)}) collective-permute-start(f32[2,64]{1,0:T(2,128)S(1)} %get-tuple-element.91), channel_id=1, source_target_pairs={{1,0},{2,1},{3,2},{4,3},{5,4},{6,5},{7,6},{8,7},{9,8},{10,9},{11,1... | collective-permute-start | bytes 1544 | tf_op jit(solution)/shard_map/ppermute | solution.py:23
  568.6 21.4 %copy-start.7 = (f32[1,8,128]{2,1,0:T(8,128)S(1)}, f32[1,8,128]{2,1,0:T(8,128)}, u32[]{:S(2)}) copy-start(f32[1,8,128]{2,1,0:T(8,128)} %get-tuple-element.79) | copy-start | bytes 12292
  568.6 21.4 %copy-start.10 = (f32[1,1,1024]{2,1,0:T(1,128)S(1)}, f32[1,1,1024]{2,1,0:T(1,128)}, u32[]{:S(2)}) copy-start(f32[1,1,1024]{2,1,0:T(1,128)} %copy-done.9) | copy-start | bytes 12292
  577.9 13.0 %collective-permute-start.8 = (f32[4,64]{1,0:T(4,128)S(1)}, f32[4,64]{1,0:T(4,128)S(1)}, u32[]{:S(2)}, u32[]{:S(2)}) collective-permute-start(f32[4,64]{1,0:T(4,128)S(1)} %get-tuple-element.90), channel_id=1, source_target_pairs={{0,1},{1,2},{2,3},{3,4},{4,5},{5,6},{6,7},{7,8},{8,9},{9,10},{10,1... | collective-permute-start | bytes 3080 | tf_op jit(solution)/shard_map/ppermute | solution.py:21
  577.9 13.0 %collective-permute-start.9 = (f32[4,64]{1,0:T(4,128)S(1)}, f32[4,64]{1,0:T(4,128)S(1)}, u32[]{:S(2)}, u32[]{:S(2)}) collective-permute-start(f32[4,64]{1,0:T(4,128)S(1)} %get-tuple-element.89), channel_id=1, source_target_pairs={{1,0},{2,1},{3,2},{4,3},{5,4},{6,5},{7,6},{8,7},{9,8},{10,9},{11,1... | collective-permute-start | bytes 3080 | tf_op jit(solution)/shard_map/ppermute | solution.py:23
where the time goes:
time: 627 us; the launch traced here: 616 us
  waiting for transfers between devices  268 us (43%)
  local copies, waits for them, and re-layouts  166 us (26%)
  starting transfers between devices  125 us (20%)
  matrix products  50.3 us (8%)
    ppermute x5, waiting for transfers between devices, extended(): lax.ppermute(tail, axis, [(i, (i + 1) % count) for i in range(count)])  230 us
    gather x10, local copies, waits for them, and re-layouts, spread(): return jnp.take(window, links, axis=1) - values[:, None, :]  129 us
    all_to_all x2, starting transfers between devices, route(): lax.all_to_all(padded, 'blk', split_axis=0, concat_axis=0, tiled=True)  52.4 us
    ppermute x5, starting transfers between devices, extended(): lax.ppermute(head, axis, [((i + 1) % count, i) for i in range(count)])  47.4 us
    dot_general x2, local copies, waits for them, and re-layouts, route(): jnp.einsum('in,isfp->nsfp', place, payload, precision=lax.Precision.HIGHEST)  26.7 us
    dot_general x2, matrix products, route(): jnp.einsum('in,nsfp->isfp', pick, received, precision=lax.Precision.HIGHEST)  26.7 us
    all_to_all x2, waiting for transfers between devices, route(): lax.all_to_all(padded, 'blk', split_axis=0, concat_axis=0, tiled=True)  21.4 us
    ppermute x2, starting transfers between devices, partner(): lax.ppermute(array, axis, [(i, i ^ 1 << stride) for i in range(lax.axis_s...  16.6 us
  transfers between devices with their start and end apart: 14, of which 9 were waited for; matrix products, arithmetic and copies ran while one was open for 9% of the time, Pallas kernels for 0%

commit v1 on v0

v1 whole, which is shorter than its diff:
```python
import jax
import jax.numpy as jnp
from jax import lax
from jax.experimental import pallas as pl
from jax.experimental.pallas import tpu as pltpu
from jax.sharding import PartitionSpec as P

TILE = 128
BLK = 8
FLUX = 10
SURF = 4
HW = 64
SUBSTEPS = 2
AXES = ("sec", "blk")
NEAR = (-3, -2, -1, 0, 1, 2, 3)
FLUX_HALO = (0, 1, 8)
SURF_HALO = (0, 1, 2, 3)
LAND, COEF, LINK, TABLE = 8, 9, 21, 27
GROUP = 8


def offsets_of(count):
    return list(NEAR) + [count // 2]


def messages_of(count):
    offsets = offsets_of(count)
    slot = {o: i for i, o in enumerate(offsets)}
    reach = sorted({o + s for o in offsets for s in (-1, 0, 1)})
    full = [(o, slot[o], slot.get(o + 1), slot.get(o - 1)) for o in offsets]
    return full + [(o, None, slot.get(o + 1), slot.get(o - 1)) for o in reach if o not in slot]


def softplus(x):
    return jnp.maximum(x, 0.0) + jnp.log1p(jnp.exp(-jnp.abs(x)))


def sigmoid(x):
    return 1.0 / (1.0 + jnp.exp(-x))


def link_code(links, rows):
    place = links + (TILE - HW)
    return (place & (TILE - 1)) + jnp.where((place >> 7) == rows + 1, 0, TILE)


def gatherer(code):
    count = code[0].shape[0]
    lane = lax.broadcasted_iota(jnp.int32, (count, TILE), 1)
    low = lane < HW
    where = [(c & (TILE - 1), c >= TILE) for c in code]

    def take(x, index):
        return jnp.take_along_axis(x, index, axis=1, mode="promise_in_bounds")

    def spread(x):
        beside = jnp.where(low, pltpu.roll(x, count - 1, 0), pltpu.roll(x, 1, 0))
        return [jnp.where(far, take(beside, index), take(x, index)) - x for index, far in where]

    return spread


def compute_fluxes(a, ocean_frac):
    speed = jnp.sqrt(a[0] * a[0] + a[1] * a[1] + 1.0)
    sensible = 0.3 * speed * (a[7] - a[2])
    latent = 0.3 * speed * (jnp.tanh(a[7]) - a[3])
    net_short = 0.8 * softplus(a[4])
    net_long = softplus(a[5]) - softplus(a[7])
    rain = softplus(a[6])
    rows = [
        0.5 * speed * a[0],
        0.5 * speed * a[1],
        sensible,
        latent,
        net_short,
        net_long,
        rain,
        0.5 * latent,
        rain - 0.5 * latent,
        net_short + net_long - sensible - latent,
    ]
    return [r * ocean_frac for r in rows]


def start_tiles(tiles, weights, sems):
    for i in range(weights.shape[0]):
        pltpu.make_async_copy(tiles.at[0, 0, i], weights.at[i], sems.at[i]).start()


def run_tiles(fields, tiles, weights, sems, src, dst, table, sums):
    rows = len(fields) * BLK
    block = lax.broadcasted_iota(jnp.int32, (rows, TILE), 0) & (BLK - 1)
    for s in range(BLK):
        spread = jnp.concatenate([jnp.broadcast_to(f[s : s + 1], (BLK, TILE)) for f in fields], axis=0)
        for d in range(BLK):
            table[s * (BLK + 1) + d] = jnp.where(block == d, spread, 0.0).astype(jnp.bfloat16)
        table[s * (BLK + 1) + BLK] = jnp.zeros((rows, TILE), jnp.bfloat16)
    slots = weights.shape[1]

    def one_offset(i, carry):
        pltpu.make_async_copy(tiles.at[0, 0, i], weights.at[i], sems.at[i]).wait()
        total = jnp.zeros((rows, TILE), jnp.float32)
        for first in range(0, slots, GROUP):
            left = []
            for j in range(first, first + GROUP):
                target = dst[i, j]
                left.append(table[src[i, j] * (BLK + 1) + jnp.where(target < 0, BLK, target)])
            right = [weights[i, j] for j in range(first, first + GROUP)]
            total = total + lax.dot_general(
                jnp.concatenate(left, axis=1),
                jnp.concatenate(right, axis=1),
                (((1,), (1,)), ((), ())),
                preferred_element_type=jnp.float32,
            )
        sums[i] = total
        return carry

    lax.fori_loop(0, weights.shape[0], one_offset, 0)


def write_messages(sums, outs, messages, rows, halo, depth):
    row = lax.broadcasted_iota(jnp.int32, (BLK, TILE), 0)
    for out, (_, own, after, before) in zip(outs, messages):
        base = 0
        if own is not None:
            out[0:rows] = sums[own]
            base = rows
        for h, f in enumerate(halo):
            part = jnp.zeros((BLK, TILE), jnp.float32)
            if after is not None:
                part = jnp.where(row < depth, sums[after, f * BLK : (f + 1) * BLK], part)
            if before is not None:
                part = jnp.where(row >= BLK - depth, sums[before, f * BLK : (f + 1) * BLK], part)
            out[base + h * BLK : base + (h + 1) * BLK] = part


def total_of(recv, messages, rows):
    own = None
    edge = None
    for ref, (_, slot, _, _) in zip(recv, messages):
        if slot is not None:
            own = ref[0:rows] if own is None else own + ref[0:rows]
            beside = ref[rows:]
        else:
            beside = ref[...]
        edge = beside if edge is None else edge + beside
    return own, edge


def fetch(pairs, sems):
    copies = [pltpu.make_async_copy(a, b, sems.at[n]) for n, (a, b) in enumerate(pairs)]
    for c in copies:
        c.start()
    return copies


def lay_out(ref, count, out, base, change=None):
    for c in range(count):
        for r in range(BLK):
            piece = ref[c : c + 1, r * TILE : (r + 1) * TILE]
            if change is not None:
                piece = change(piece, r)
            out[(base + c) * BLK + r : (base + c) * BLK + r + 1] = piece.astype(out.dtype)


def send_kernel(messages, state, links, coef, land, tile_src, dst_lists, tiles, *refs):
    n = len(messages)
    outs, (own, high, low) = refs[:n], refs[n : n + 3]
    (weights, table, sums, src, dst, v_state, v_links, v_coef, v_land, work, wsems, sems) = refs[n + 3 :]
    section = lax.axis_index("sec")
    me = lax.axis_index("blk")

    @pl.when(section == 0)
    def _():
        copies = fetch(
            [(state.at[0], v_state), (land, v_land), (tile_src.at[0, 0], src), (dst_lists.at[0, me], dst)], sems
        )
        start_tiles(tiles, weights, wsems)
        copies[0].wait()
        copies[1].wait()
        lay_out(v_state, BLK, work, 0)
        lay_out(v_land, 1, work, LAND)
        channels = [work[c * BLK : (c + 1) * BLK] for c in range(LAND + 1)]
        fields = compute_fluxes(channels[:LAND], channels[LAND])
        copies[2].wait()
        copies[3].wait()
        run_tiles(fields, tiles, weights, wsems, src, dst, table, sums)
        write_messages(sums, outs, messages, FLUX * BLK, FLUX_HALO, 2)

    @pl.when(section == 1)
    def _():
        copies = fetch(
            [
                (state.at[0], v_state),
                (land, v_land),
                (links.at[0], v_links),
                (coef.at[0, 0], v_coef.at[0]),
                (coef.at[0, 1], v_coef.at[1]),
            ],
            sems,
        )
        for c in copies:
            c.wait()
        lay_out(v_state, BLK, own, 0)
        lay_out(v_land, 1, own, LAND)
        lay_out(v_coef.at[0], 6, own, COEF)
        lay_out(v_coef.at[1], 6, own, COEF + 6)
        lay_out(v_links, 6, own, LINK, link_code)
        for c in range(TABLE):
            low[2 * c : 2 * c + 2] = own[c * BLK : c * BLK + 2]
            high[2 * c : 2 * c + 2] = own[c * BLK + 6 : c * BLK + 8]


def sea_kernel(messages, *refs):
    n = len(messages)
    recv, refs = refs[:n], refs[n:]
    own_h, high_h, low_h, links, coef, land, tile_src, dst_lists, tiles = refs[:9]
    outs, keep, refs = refs[9 : 9 + n], refs[9 + n], refs[10 + n :]
    (weights, table, sums, src, dst, v_links, v_coef, v_land, own, high, low, edge) = refs[:12]
    v_recv, (wsems, sems) = refs[12 : 12 + n], refs[12 + n :]
    section = lax.axis_index("sec")
    me = lax.axis_index("blk")

    @pl.when(section == 0)
    def _():
        copies = fetch(
            [(land, v_land), (links.at[0], v_links), (coef.at[0, 0], v_coef.at[0]), (coef.at[0, 1], v_coef.at[1])], sems
        )
        for c in copies:
            c.wait()
        lay_out(v_coef.at[0], 6, keep, 0)
        lay_out(v_coef.at[1], 6, keep, 6)
        lay_out(v_links, 6, keep, 12, link_code)
        lay_out(v_land, 1, keep, 18)

    @pl.when(section == 1)
    def _():
        copies = fetch(
            list(zip(recv, v_recv))
            + [(own_h, own), (high_h, high), (low_h, low), (tile_src.at[0, 0], src), (dst_lists.at[1, me], dst)],
            sems,
        )
        start_tiles(tiles, weights, wsems)
        edge[...] = jnp.zeros_like(edge)
        for c in copies:
            c.wait()
        for c in range(TABLE):
            edge[c * BLK : c * BLK + 2] = low[2 * c : 2 * c + 2]
            edge[c * BLK + 6 : c * BLK + 8] = high[2 * c : 2 * c + 2]
        forcing, beside = total_of(v_recv, messages, FLUX * BLK)

        def near(c):
            return own[c * BLK : (c + 1) * BLK]

        def wide(c):
            return jnp.concatenate([near(c), edge[c * BLK : (c + 1) * BLK]], axis=0)

        def force(f):
            return forcing[f * BLK : (f + 1) * BLK]

        def force_wide(f):
            h = FLUX_HALO.index(f)
            return jnp.concatenate([force(f), beside[h * BLK : (h + 1) * BLK]], axis=0)

        spread = gatherer([wide(LINK + k).astype(jnp.int32) for k in range(6)])
        grad_wx = [wide(COEF + k) for k in range(6)]
        grad_wy = [wide(COEF + 6 + k) for k in range(6)]
        wet = wide(LAND)
        height, flow_u, flow_v = wide(0), wide(1), wide(2)
        depth = 1.0 + sigmoid(wide(3))
        ice = sigmoid(wide(5))
        coriol = 0.3 * jnp.tanh(wide(6))
        mixed = 1.0 + softplus(near(7))
        drag = 0.3 * (1.0 - ice)
        push_u, push_v, push_h = drag * force_wide(0), drag * force_wide(1), 0.1 * force_wide(8)
        for _ in range(SUBSTEPS):
            slopes = spread(height)
            grad_x = sum(w * s for w, s in zip(grad_wx, slopes))
            grad_y = sum(w * s for w, s in zip(grad_wy, slopes))
            next_u = wet * (flow_u - 0.5 * grad_x + coriol * flow_v + push_u)
            next_v = wet * (flow_v - 0.5 * grad_y - coriol * flow_u + push_v)
            moved_u = spread(depth * next_u)
            moved_v = spread(depth * next_v)
            moved = sum(wx * a + wy * b for wx, wy, a, b in zip(grad_wx, grad_wy, moved_u, moved_v))
            height = height - 0.5 * moved + push_h
            flow_u, flow_v = next_u, next_v
        new_temp = near(4) + 0.2 * near(LAND) * force(9) / mixed
        u, v = flow_u[:BLK], flow_v[:BLK]
        for r, field in enumerate([height[:BLK], u, v, new_temp]):
            keep[r * BLK : (r + 1) * BLK] = field
        run_tiles([new_temp, ice[:BLK], u, v], tiles, weights, wsems, src, dst, table, sums)
        write_messages(sums, outs, messages, SURF * BLK, SURF_HALO, 1)


def last_kernel(messages, *refs):
    n = len(messages)
    recv, keep_h, out = refs[:n], refs[n], refs[n + 1]
    keep, v_recv, sems = refs[n + 2], refs[n + 3 : n + 3 + n], refs[n + 3 + n]
    section = lax.axis_index("sec")

    def put(r, field):
        for b in range(BLK):
            out[0, r : r + 1, b * TILE : (b + 1) * TILE] = field[b : b + 1]

    @pl.when(section == 0)
    def _():
        copies = fetch([(keep_h, keep)] + list(zip(recv, v_recv)), sems)
        for c in copies:
            c.wait()
        returned, beside = total_of(v_recv, messages, SURF * BLK)
        blank = jnp.zeros((BLK, TILE), jnp.float32)

        def part(c):
            return keep[c * BLK : (c + 1) * BLK]

        code = [jnp.concatenate([part(12 + k), blank], axis=0).astype(jnp.int32) for k in range(6)]
        spread = gatherer(code)
        for r in range(SURF):
            field = returned[r * BLK : (r + 1) * BLK]
            slopes = spread(jnp.concatenate([field, beside[r * BLK : (r + 1) * BLK]], axis=0))
            first = 0 if r < 2 else 6
            smooth = field + sum(part(first + k) * s[:BLK] for k, s in enumerate(slopes))
            put(r, part(18) * smooth)

    @pl.when(section == 1)
    def _():
        copy = pltpu.make_async_copy(keep_h, keep, sems.at[0])
        copy.start()
        copy.wait()
        for r in range(SURF):
            put(r, keep[r * BLK : (r + 1) * BLK])


def body(surface_state, neighbours, coupling_coef, land, tile_src, dst_lists, tiles):
    count = lax.axis_size("blk")
    messages = messages_of(count)
    n = len(messages)
    recv_count, slots = tiles.shape[2:4]
    f32, i32 = jnp.float32, jnp.int32
    anywhere = pl.BlockSpec(memory_space=pl.ANY)
    inside = pl.BlockSpec(memory_space=pltpu.VMEM)
    params = pltpu.CompilerParams(vmem_limit_bytes=40 * 1024 * 1024)

    def shapes_for(rows, halo):
        return [
            jax.ShapeDtypeStruct(((0 if own is None else rows) + len(halo) * BLK, TILE), f32)
            for _, own, _, _ in messages
        ]

    def remap_scratch(rows):
        return [
            pltpu.VMEM((recv_count, slots, TILE, TILE), jnp.bfloat16),
            pltpu.VMEM((BLK * (BLK + 1), rows, TILE), jnp.bfloat16),
            pltpu.VMEM((recv_count, rows, TILE), f32),
            pltpu.SMEM((recv_count, slots), i32),
            pltpu.SMEM((recv_count, slots), i32),
        ]

    cost = pl.CostEstimate(flops=int(2 * tiles.size * 16), bytes_accessed=int(tiles.size * 2), transcendentals=0)
    width = BLK * TILE
    flux_shapes = shapes_for(FLUX * BLK, FLUX_HALO)
    surf_shapes = shapes_for(SURF * BLK, SURF_HALO)
    own_shape = jax.ShapeDtypeStruct((TABLE * BLK, TILE), f32)
    side_shape = jax.ShapeDtypeStruct((56, TILE), f32)
    keep_shape = jax.ShapeDtypeStruct((19 * BLK, TILE), f32)

    sent = pl.pallas_call(
        lambda *r: send_kernel(messages, *r),
        name="flux_remap",
        out_shape=flux_shapes + [own_shape, side_shape, side_shape],
        in_specs=[anywhere] * 7,
        out_specs=[inside] * (n + 3),
        scratch_shapes=remap_scratch(FLUX * BLK)
        + [
            pltpu.VMEM((8, width), f32),
            pltpu.VMEM((6, width), i32),
            pltpu.VMEM((2, 6, width), f32),
            pltpu.VMEM((1, width), i32),
            pltpu.VMEM(((LAND + 1) * BLK, TILE), f32),
            pltpu.SemaphoreType.DMA((recv_count,)),
            pltpu.SemaphoreType.DMA((5,)),
        ],
        compiler_params=params,
        cost_estimate=cost,
    )(surface_state, neighbours, coupling_coef, land, tile_src, dst_lists, tiles)
    own, high, low = sent[n:]

    def beside(x, step):
        return lax.ppermute(x, AXES, [(count + i, count + (i + step) % count) for i in range(count)])

    def across(x, step, section):
        pairs = [(section * count + i, (1 - section) * count + (i + step) % count) for i in range(count)]
        return lax.ppermute(x, AXES, pairs)

    high, low = beside(high, 1), beside(low, -1)
    recv = [across(x, m[0], 0) for x, m in zip(sent[:n], messages)]

    sent = pl.pallas_call(
        lambda *r: sea_kernel(messages, *r),
        name="sea_remap",
        out_shape=surf_shapes + [keep_shape],
        in_specs=[anywhere] * (n + 9),
        out_specs=[inside] * (n + 1),
        scratch_shapes=remap_scratch(SURF * BLK)
        + [
            pltpu.VMEM((6, width), i32),
            pltpu.VMEM((2, 6, width), f32),
            pltpu.VMEM((1, width), i32),
            pltpu.VMEM((TABLE * BLK, TILE), f32),
            pltpu.VMEM((56, TILE), f32),
            pltpu.VMEM((56, TILE), f32),
            pltpu.VMEM((TABLE * BLK, TILE), f32),
        ]
        + [pltpu.VMEM(s.shape, f32) for s in flux_shapes]
        + [pltpu.SemaphoreType.DMA((recv_count,)), pltpu.SemaphoreType.DMA((n + 5,))],
        compiler_params=params,
        cost_estimate=cost,
    )(*recv, own, high, low, neighbours, coupling_coef, land, tile_src, dst_lists, tiles)
    keep = sent[n]
    recv = [across(x, m[0], 1) for x, m in zip(sent[:n], messages)]

    return pl.pallas_call(
        lambda *r: last_kernel(messages, *r),
        name="smooth",
        out_shape=jax.ShapeDtypeStruct((1, SURF, width), f32),
        in_specs=[anywhere] * (n + 1),
        out_specs=inside,
        scratch_shapes=[pltpu.VMEM(keep_shape.shape, f32)]
        + [pltpu.VMEM(s.shape, f32) for s in surf_shapes]
        + [pltpu.SemaphoreType.DMA((n + 1,))],
        compiler_params=params,
    )(*recv, keep)


def solution(mesh):
    in_specs = (
        P("sec", None, "blk"),
        P("sec", None, "blk"),
        P("sec", None, None, "blk"),
        P("sec", "blk"),
        P("sec", "blk", None, None),
        P(),
        P("sec", "blk", None, None, None, None),
    )
    out_specs = P("sec", None, "blk")
    return jax.shard_map(body, mesh=mesh, in_specs=in_specs, out_specs=out_specs, check_vma=False)
```

time: 627 us -> 97.8 us (0.16)
  the two profiles are of different devices: /device:TPU:1 before, /device:TPU:0 now
where the time goes in v1:
time: 97.8 us; the launch traced here: 96.9 us
  starting transfers between devices  47.6 us (49%)
  waiting for transfers between devices  26.4 us (27%)
  local copies, waits for them, and re-layouts  14.1 us (14%)
  Pallas kernels  8.47 us (9%)
    ppermute x24, starting transfers between devices, across(): return lax.ppermute(x, AXES, pairs)  46.3 us
    ppermute x24, waiting for transfers between devices, across(): return lax.ppermute(x, AXES, pairs)  26.4 us
    unnamed x17, local copies, waits for them, and re-layouts  14.1 us
    pallas_call x1, Pallas kernels, body(): pl.pallas_call(lambda *r: send_kernel(messages, *r), name='flux_remap', o...  6.61 us
  transfers between devices with their start and end apart: 26, of which 10 were waited for; matrix products, arithmetic and copies ran while one was open for 0% of the time, Pallas kernels for 0%

profile of v1, /device:TPU:0, one launch (start us, length us, event | category | flops | bytes accessed | tf_op | source)
XLA Modules:
  0.0 96.9 jit_solution(3908434108642909444)
XLA Ops:
  0.0 0.8 copy.8.r_1_.r_15_
  0.8 0.8 copy.9.r_2_.r_16_
  1.6 1.2 %copy.10.r_5_.r_19_ = s32[2,64,8,48]{3,2,1,0:T(8,128)S(1)} copy(s32[2,64,8,48]{1,3,2,0:T(8,128)} %param.12) | data formatting | bytes 393216 | tf_op args[5]
  2.8 0.0 copy-start
  2.8 4.6 %copy-done = bf16[1,1,8,48,128,128]{5,4,3,2,1,0:T(8,128)(2,1)S(1)} copy-done((bf16[1,1,8,48,128,128]{5,4,3,2,1,0:T(8,128)(2,1)S(1)}, bf16[1,1,8,48,128,128]{5,4,3,2,1,0:T(8,128)(2,1)}, u32[]{:S(2)}) %copy-start) | copy-done | bytes 12582936
  7.4 0.8 copy-done.2
  8.2 0.7 copy-done.3
  8.9 0.7 copy-done.5
  9.5 6.6 %flux_remap.1 = (f32[104,128]{1,0:T(8,128)S(1)}, f32[104,128]{1,0:T(8,128)S(1)}, f32[104,128]{1,0:T(8,128)S(1)}, f32[104,128]{1,0:T(8,128)S(1)}, f32[104,128]{1,...) custom-call(f32[1,8,1024]{2,1,0:T(8,128)S(1)} %copy-done.2, ...), custom_call_target="tpu_custom_call" | custom-call | flops 201326592 | bytes 12582912 | tf_op jit(solution)/shard_map/flux_remap/pallas_call | solution.py:367
  16.2 1.3 %collective-permute-start.8 = (f32[24,128]{1,0:T(8,128)S(1)}, f32[24,128]{1,0:T(8,128)S(1)}, u32[]{:S(2)}, u32[]{:S(2)}) collective-permute-start(f32[24,128]{1,0:T(8,128)S(1)} %get-tuple-element.41), channel_id=1, source_target_pairs={{0,124},{1,125},{2,126},{3,127},{4,64},{5,65},{6,66},{7,67},{8,68}... | collective-permute-start | bytes 36872 | tf_op jit(solution)/shard_map/ppermute | solution.py:393
  17.5 1.3 %collective-permute-start.9 = (f32[24,128]{1,0:T(8,128)S(1)}, f32[24,128]{1,0:T(8,128)S(1)}, u32[]{:S(2)}, u32[]{:S(2)}) collective-permute-start(f32[24,128]{1,0:T(8,128)S(1)} %get-tuple-element.42), channel_id=1, source_target_pairs={{0,68},{1,69},{2,70},{3,71},{4,72},{5,73},{6,74},{7,75},{8,76},{9,... | collective-permute-start | bytes 36872 | tf_op jit(solution)/shard_map/ppermute | solution.py:393
  18.8 1.8 %collective-permute-start = (f32[104,128]{1,0:T(8,128)S(1)}, f32[104,128]{1,0:T(8,128)S(1)}, u32[]{:S(2)}, u32[]{:S(2)}) collective-permute-start(f32[104,128]{1,0:T(8,128)S(1)} %get-tuple-element.33), channel_id=1, source_target_pairs={{0,125},{1,126},{2,127},{3,64},{4,65},{5,66},{6,67},{7,68},{8,69},... | collective-permute-start | bytes 159752 | tf_op jit(solution)/shard_map/ppermute | solution.py:393
  20.6 3.3 %collective-permute-start.1 = (f32[104,128]{1,0:T(8,128)S(1)}, f32[104,128]{1,0:T(8,128)S(1)}, u32[]{:S(2)}, u32[]{:S(2)}) collective-permute-start(f32[104,128]{1,0:T(8,128)S(1)} %get-tuple-element.34), channel_id=1, source_target_pairs={{0,126},{1,127},{2,64},{3,65},{4,66},{5,67},{6,68},{7,69},{8,70},{... | collective-permute-start | bytes 159752 | tf_op jit(solution)/shard_map/ppermute | solution.py:393
  23.8 1.5 %collective-permute-start.2 = (f32[104,128]{1,0:T(8,128)S(1)}, f32[104,128]{1,0:T(8,128)S(1)}, u32[]{:S(2)}, u32[]{:S(2)}) collective-permute-start(f32[104,128]{1,0:T(8,128)S(1)} %get-tuple-element.35), channel_id=1, source_target_pairs={{0,127},{1,64},{2,65},{3,66},{4,67},{5,68},{6,69},{7,70},{8,71},{9... | collective-permute-start | bytes 159752 | tf_op jit(solution)/shard_map/ppermute | solution.py:393
  25.3 0.0 collective-permute-done.8.r_8_
  25.3 3.8 %collective-permute-start.10 = (f32[24,128]{1,0:T(8,128)S(1)}, f32[24,128]{1,0:T(8,128)S(1)}, u32[]{:S(2)}, u32[]{:S(2)}) collective-permute-start(f32[24,128]{1,0:T(8,128)S(1)} %get-tuple-element.43), channel_id=1, source_target_pairs={{0,95},{1,96},{2,97},{3,98},{4,99},{5,100},{6,101},{7,102},{8,103}... | collective-permute-start | bytes 36872 | tf_op jit(solution)/shard_map/ppermute | solution.py:393
  29.1 0.0 collective-permute-done.9.r_9_
  29.1 1.3 %collective-permute-start.11 = (f32[24,128]{1,0:T(8,128)S(1)}, f32[24,128]{1,0:T(8,128)S(1)}, u32[]{:S(2)}, u32[]{:S(2)}) collective-permute-start(f32[24,128]{1,0:T(8,128)S(1)} %get-tuple-element.44), channel_id=1, source_target_pairs={{0,97},{1,98},{2,99},{3,100},{4,101},{5,102},{6,103},{7,104},{8,10... | collective-permute-start | bytes 36872 | tf_op jit(solution)/shard_map/ppermute | solution.py:393
  30.4 0.1 collective-permute-done.10.r_10_
  30.5 0.7 collective-permute-start.12
  31.1 0.6 collective-permute-done.11.r_11_
  31.8 0.7 collective-permute-start.13
  32.4 0.0 collective-permute-done.12.r_13_
  32.4 10.1 %collective-permute-start.3 = (f32[104,128]{1,0:T(8,128)S(1)}, f32[104,128]{1,0:T(8,128)S(1)}, u32[]{:S(2)}, u32[]{:S(2)}) collective-permute-start(f32[104,128]{1,0:T(8,128)S(1)} %get-tuple-element.36), channel_id=1, source_target_pairs={{0,64},{1,65},{2,66},{3,67},{4,68},{5,69},{6,70},{7,71},{8,72},{9,... | collective-permute-start | bytes 159752 | tf_op jit(solution)/shard_map/ppermute | solution.py:393
  42.6 0.0 collective-permute-done.13.r_14_
  42.6 1.3 %collective-permute-start.4 = (f32[104,128]{1,0:T(8,128)S(1)}, f32[104,128]{1,0:T(8,128)S(1)}, u32[]{:S(2)}, u32[]{:S(2)}) collective-permute-start(f32[104,128]{1,0:T(8,128)S(1)} %get-tuple-element.37), channel_id=1, source_target_pairs={{0,65},{1,66},{2,67},{3,68},{4,69},{5,70},{6,71},{7,72},{8,73},{9,... | collective-permute-start | bytes 159752 | tf_op jit(solution)/shard_map/ppermute | solution.py:393
  43.9 0.0 collective-permute-done.r_0_
  43.9 1.3 %collective-permute-start.5 = (f32[104,128]{1,0:T(8,128)S(1)}, f32[104,128]{1,0:T(8,128)S(1)}, u32[]{:S(2)}, u32[]{:S(2)}) collective-permute-start(f32[104,128]{1,0:T(8,128)S(1)} %get-tuple-element.38), channel_id=1, source_target_pairs={{0,66},{1,67},{2,68},{3,69},{4,70},{5,71},{6,72},{7,73},{8,74},{9,... | collective-permute-start | bytes 159752 | tf_op jit(solution)/shard_map/ppermute | solution.py:393
  45.2 0.0 collective-permute-done.1.r_1_
  45.2 2.6 %collective-permute-start.6 = (f32[104,128]{1,0:T(8,128)S(1)}, f32[104,128]{1,0:T(8,128)S(1)}, u32[]{:S(2)}, u32[]{:S(2)}) collective-permute-start(f32[104,128]{1,0:T(8,128)S(1)} %get-tuple-element.39), channel_id=1, source_target_pairs={{0,67},{1,68},{2,69},{3,70},{4,71},{5,72},{6,73},{7,74},{8,75},{9,... | collective-permute-start | bytes 159752 | tf_op jit(solution)/shard_map/ppermute | solution.py:393
  47.8 0.0 collective-permute-done.2.r_2_
  47.8 1.4 %collective-permute-start.7 = (f32[104,128]{1,0:T(8,128)S(1)}, f32[104,128]{1,0:T(8,128)S(1)}, u32[]{:S(2)}, u32[]{:S(2)}) collective-permute-start(f32[104,128]{1,0:T(8,128)S(1)} %get-tuple-element.40), channel_id=1, source_target_pairs={{0,96},{1,97},{2,98},{3,99},{4,100},{5,101},{6,102},{7,103},{8,104... | collective-permute-start | bytes 159752 | tf_op jit(solution)/shard_map/ppermute | solution.py:393
  49.2 0.0 collective-permute-done.3.r_3_
  49.2 0.0 collective-permute-done.4.r_4_
  49.2 0.0 collective-permute-done.5.r_5_
  49.2 0.3 collective-permute-done.6.r_6_
  49.6 1.4 %collective-permute-done.7.r_7_ = f32[104,128]{1,0:T(8,128)S(1)} collective-permute-done((f32[104,128]{1,0:T(8,128)S(1)}, f32[104,128]{1,0:T(8,128)S(1)}, u32[]{:S(2)}, u32[]{:S(2)}) %collective-permute-start.7) | collective-permute-done | bytes 53280 | tf_op jit(solution)/shard_map/ppermute | solution.py:393
  51.0 4.6 %copy-done.1 = bf16[1,1,8,48,128,128]{5,4,3,2,1,0:T(8,128)(2,1)S(1)} copy-done((bf16[1,1,8,48,128,128]{5,4,3,2,1,0:T(8,128)(2,1)S(1)}, bf16[1,1,8,48,128,128]{5,4,3,2,1,0:T(8,128)(2,1)}, u32[]{:S(2)}) %copy-start.1) | copy-done | bytes 12582936
  55.5 0.4 sea_remap.1
  56.0 1.3 %collective-permute-start.22 = (f32[32,128]{1,0:T(8,128)S(1)}, f32[32,128]{1,0:T(8,128)S(1)}, u32[]{:S(2)}, u32[]{:S(2)}) collective-permute-start(f32[32,128]{1,0:T(8,128)S(1)} %get-tuple-element.56), channel_id=1, source_target_pairs={{64,60},{65,61},{66,62},{67,63},{68,0},{69,1},{70,2},{71,3},{72,4}... | collective-permute-start | bytes 49160 | tf_op jit(solution)/shard_map/ppermute | solution.py:393
  57.3 1.3 %collective-permute-start.23 = (f32[32,128]{1,0:T(8,128)S(1)}, f32[32,128]{1,0:T(8,128)S(1)}, u32[]{:S(2)}, u32[]{:S(2)}) collective-permute-start(f32[32,128]{1,0:T(8,128)S(1)} %get-tuple-element.57), channel_id=1, source_target_pairs={{64,4},{65,5},{66,6},{67,7},{68,8},{69,9},{70,10},{71,11},{72,12},... | collective-permute-start | bytes 49160 | tf_op jit(solution)/shard_map/ppermute | solution.py:393
  58.6 1.3 %collective-permute-start.14 = (f32[64,128]{1,0:T(8,128)S(1)}, f32[64,128]{1,0:T(8,128)S(1)}, u32[]{:S(2)}, u32[]{:S(2)}) collective-permute-start(f32[64,128]{1,0:T(8,128)S(1)} %get-tuple-element.48), channel_id=1, source_target_pairs={{64,61},{65,62},{66,63},{67,0},{68,1},{69,2},{70,3},{71,4},{72,5},... | collective-permute-start | bytes 98312 | tf_op jit(solution)/shard_map/ppermute | solution.py:393
  59.9 1.3 %collective-permute-start.15 = (f32[64,128]{1,0:T(8,128)S(1)}, f32[64,128]{1,0:T(8,128)S(1)}, u32[]{:S(2)}, u32[]{:S(2)}) collective-permute-start(f32[64,128]{1,0:T(8,128)S(1)} %get-tuple-element.49), channel_id=1, source_target_pairs={{64,62},{65,63},{66,0},{67,1},{68,2},{69,3},{70,4},{71,5},{72,6},{... | collective-permute-start | bytes 98312 | tf_op jit(solution)/shard_map/ppermute | solution.py:393
  61.2 1.3 %collective-permute-start.16 = (f32[64,128]{1,0:T(8,128)S(1)}, f32[64,128]{1,0:T(8,128)S(1)}, u32[]{:S(2)}, u32[]{:S(2)}) collective-permute-start(f32[64,128]{1,0:T(8,128)S(1)} %get-tuple-element.50), channel_id=1, source_target_pairs={{64,63},{65,0},{66,1},{67,2},{68,3},{69,4},{70,5},{71,6},{72,7},{7... | collective-permute-start | bytes 98312 | tf_op jit(solution)/shard_map/ppermute | solution.py:393
  62.5 6.8 %collective-permute-done.22.r_8_ = f32[32,128]{1,0:T(8,128)S(1)} collective-permute-done((f32[32,128]{1,0:T(8,128)S(1)}, f32[32,128]{1,0:T(8,128)S(1)}, u32[]{:S(2)}, u32[]{:S(2)}) %collective-permute-start.22) | collective-permute-done | bytes 16416 | tf_op jit(solution)/shard_map/ppermute | solution.py:393
  69.2 1.3 %collective-permute-start.24 = (f32[32,128]{1,0:T(8,128)S(1)}, f32[32,128]{1,0:T(8,128)S(1)}, u32[]{:S(2)}, u32[]{:S(2)}) collective-permute-start(f32[32,128]{1,0:T(8,128)S(1)} %get-tuple-element.58), channel_id=1, source_target_pairs={{64,31},{65,32},{66,33},{67,34},{68,35},{69,36},{70,37},{71,38},{7... | collective-permute-start | bytes 49160 | tf_op jit(solution)/shard_map/ppermute | solution.py:393
  70.5 3.4 %collective-permute-done.23.r_9_ = f32[32,128]{1,0:T(8,128)S(1)} collective-permute-done((f32[32,128]{1,0:T(8,128)S(1)}, f32[32,128]{1,0:T(8,128)S(1)}, u32[]{:S(2)}, u32[]{:S(2)}) %collective-permute-start.23) | collective-permute-done | bytes 16416 | tf_op jit(solution)/shard_map/ppermute | solution.py:393
  73.9 1.3 %collective-permute-start.25 = (f32[32,128]{1,0:T(8,128)S(1)}, f32[32,128]{1,0:T(8,128)S(1)}, u32[]{:S(2)}, u32[]{:S(2)}) collective-permute-start(f32[32,128]{1,0:T(8,128)S(1)} %get-tuple-element.59), channel_id=1, source_target_pairs={{64,33},{65,34},{66,35},{67,36},{68,37},{69,38},{70,39},{71,40},{7... | collective-permute-start | bytes 49160 | tf_op jit(solution)/shard_map/ppermute | solution.py:393
  75.2 2.3 %collective-permute-done.24.r_10_ = f32[32,128]{1,0:T(8,128)S(1)} collective-permute-done((f32[32,128]{1,0:T(8,128)S(1)}, f32[32,128]{1,0:T(8,128)S(1)}, u32[]{:S(2)}, u32[]{:S(2)}) %collective-permute-start.24) | collective-permute-done | bytes 16416 | tf_op jit(solution)/shard_map/ppermute | solution.py:393
  77.5 1.3 %collective-permute-start.17 = (f32[64,128]{1,0:T(8,128)S(1)}, f32[64,128]{1,0:T(8,128)S(1)}, u32[]{:S(2)}, u32[]{:S(2)}) collective-permute-start(f32[64,128]{1,0:T(8,128)S(1)} %get-tuple-element.51), channel_id=1, source_target_pairs={{64,0},{65,1},{66,2},{67,3},{68,4},{69,5},{70,6},{71,7},{72,8},{73... | collective-permute-start | bytes 98312 | tf_op jit(solution)/shard_map/ppermute | solution.py:393
  78.8 4.4 %collective-permute-done.25.r_11_ = f32[32,128]{1,0:T(8,128)S(1)} collective-permute-done((f32[32,128]{1,0:T(8,128)S(1)}, f32[32,128]{1,0:T(8,128)S(1)}, u32[]{:S(2)}, u32[]{:S(2)}) %collective-permute-start.25) | collective-permute-done | bytes 16416 | tf_op jit(solution)/shard_map/ppermute | solution.py:393
  83.2 1.3 %collective-permute-start.18 = (f32[64,128]{1,0:T(8,128)S(1)}, f32[64,128]{1,0:T(8,128)S(1)}, u32[]{:S(2)}, u32[]{:S(2)}) collective-permute-start(f32[64,128]{1,0:T(8,128)S(1)} %get-tuple-element.52), channel_id=1, source_target_pairs={{64,1},{65,2},{66,3},{67,4},{68,5},{69,6},{70,7},{71,8},{72,9},{73... | collective-permute-start | bytes 98312 | tf_op jit(solution)/shard_map/ppermute | solution.py:393
  84.5 0.0 collective-permute-done.14.r_0_
  84.5 1.3 %collective-permute-start.19 = (f32[64,128]{1,0:T(8,128)S(1)}, f32[64,128]{1,0:T(8,128)S(1)}, u32[]{:S(2)}, u32[]{:S(2)}) collective-permute-start(f32[64,128]{1,0:T(8,128)S(1)} %get-tuple-element.53), channel_id=1, source_target_pairs={{64,2},{65,3},{66,4},{67,5},{68,6},{69,7},{70,8},{71,9},{72,10},{7... | collective-permute-start | bytes 98312 | tf_op jit(solution)/shard_map/ppermute | solution.py:393
  85.8 0.0 collective-permute-done.15.r_1_
  85.8 1.3 %collective-permute-start.20 = (f32[64,128]{1,0:T(8,128)S(1)}, f32[64,128]{1,0:T(8,128)S(1)}, u32[]{:S(2)}, u32[]{:S(2)}) collective-permute-start(f32[64,128]{1,0:T(8,128)S(1)} %get-tuple-element.54), channel_id=1, source_target_pairs={{64,3},{65,4},{66,5},{67,6},{68,7},{69,8},{70,9},{71,10},{72,11},{... | collective-permute-start | bytes 98312 | tf_op jit(solution)/shard_map/ppermute | solution.py:393
  87.1 0.0 collective-permute-done.16.r_2_
  87.1 1.3 %collective-permute-start.21 = (f32[64,128]{1,0:T(8,128)S(1)}, f32[64,128]{1,0:T(8,128)S(1)}, u32[]{:S(2)}, u32[]{:S(2)}) collective-permute-start(f32[64,128]{1,0:T(8,128)S(1)} %get-tuple-element.55), channel_id=1, source_target_pairs={{64,32},{65,33},{66,34},{67,35},{68,36},{69,37},{70,38},{71,39},{7... | collective-permute-start | bytes 98312 | tf_op jit(solution)/shard_map/ppermute | solution.py:393
  88.4 0.0 collective-permute-done.17.r_3_
  88.4 5.4 %collective-permute-done.18.r_4_ = f32[64,128]{1,0:T(8,128)S(1)} collective-permute-done((f32[64,128]{1,0:T(8,128)S(1)}, f32[64,128]{1,0:T(8,128)S(1)}, u32[]{:S(2)}, u32[]{:S(2)}) %collective-permute-start.18) | collective-permute-done | bytes 32800 | tf_op jit(solution)/shard_map/ppermute | solution.py:393
  93.8 1.6 %collective-permute-done.19.r_5_ = f32[64,128]{1,0:T(8,128)S(1)} collective-permute-done((f32[64,128]{1,0:T(8,128)S(1)}, f32[64,128]{1,0:T(8,128)S(1)}, u32[]{:S(2)}, u32[]{:S(2)}) %collective-permute-start.19) | collective-permute-done | bytes 32800 | tf_op jit(solution)/shard_map/ppermute | solution.py:393
  95.4 0.0 collective-permute-done.20.r_6_
  95.4 0.0 collective-permute-done.21.r_7_
  95.4 1.4 %smooth.1 = f32[1,4,1024]{2,1,0:T(4,128)} custom-call(f32[64,128]{1,0:T(8,128)S(1)} %collective-permute-done.14.r_0_, f32[64,128]{1,0:T(8,128)S(1)} %collective-permute-done.15.r_1_, f32[64,128]{1,0:T(8,128)S(1)} %collective-permute-done.16.r_2_, f32[64,128]{1,0:T(8,128)S(1)} %collective-permute-done.17.r_3_, f32[64,128]{1,0:T(8,128)S(1)} %collective-permute-done.18.r_4_, ...), custom_call_target="tpu_custom_call" | custom-call | tf_op jit(solution)/shard_map/smooth/pallas_call | solution.py:422
  (8 shorter events, 0.0 us)
Async XLA Ops:
  0.0 51.0 %copy-start.6 = (s32[1,1,8,48]{3,2,1,0:T(8,128)S(1)}, s32[1,1,8,48]{3,2,1,0:T(8,128)}, u32[]{:S(2)}) copy-start(s32[1,1,8,48]{3,2,1,0:T(8,128)} %r_18_.1) | copy-start | bytes 4612
  0.0 51.0 %copy-start.4 = (s32[1,1024]{1,0:T(1,128)S(1)}, s32[1,1024]{1,0:T(1,128)}, u32[]{:S(2)}) copy-start(s32[1,1024]{1,0:T(1,128)} %r_17_.1) | copy-start | bytes 12292
  2.8 4.6 %copy-start = (bf16[1,1,8,48,128,128]{5,4,3,2,1,0:T(8,128)(2,1)S(1)}, bf16[1,1,8,48,128,128]{5,4,3,2,1,0:T(8,128)(2,1)}, u32[]{:S(2)}) copy-start(bf16[1,1,8,48,128,128]{5,4,3,2,1,0:T(8,128)(2,1)} %r_20_.1) | copy-start | bytes 37748740
  7.4 0.8 copy-start.2
  8.2 0.7 copy-start.3
  8.9 0.7 copy-start.5
  16.2 9.1 %collective-permute-start.8 = (f32[24,128]{1,0:T(8,128)S(1)}, f32[24,128]{1,0:T(8,128)S(1)}, u32[]{:S(2)}, u32[]{:S(2)}) collective-permute-start(f32[24,128]{1,0:T(8,128)S(1)} %get-tuple-element.41), channel_id=1, source_target_pairs={{0,124},{1,125},{2,126},{3,127},{4,64},{5,65},{6,66},{7,67},{8,68}... | collective-permute-start | bytes 36872 | tf_op jit(solution)/shard_map/ppermute | solution.py:393
  17.5 11.6 %collective-permute-start.9 = (f32[24,128]{1,0:T(8,128)S(1)}, f32[24,128]{1,0:T(8,128)S(1)}, u32[]{:S(2)}, u32[]{:S(2)}) collective-permute-start(f32[24,128]{1,0:T(8,128)S(1)} %get-tuple-element.42), channel_id=1, source_target_pairs={{0,68},{1,69},{2,70},{3,71},{4,72},{5,73},{6,74},{7,75},{8,76},{9,... | collective-permute-start | bytes 36872 | tf_op jit(solution)/shard_map/ppermute | solution.py:393
  18.8 25.1 %collective-permute-start = (f32[104,128]{1,0:T(8,128)S(1)}, f32[104,128]{1,0:T(8,128)S(1)}, u32[]{:S(2)}, u32[]{:S(2)}) collective-permute-start(f32[104,128]{1,0:T(8,128)S(1)} %get-tuple-element.33), channel_id=1, source_target_pairs={{0,125},{1,126},{2,127},{3,64},{4,65},{5,66},{6,67},{7,68},{8,69},... | collective-permute-start | bytes 159752 | tf_op jit(solution)/shard_map/ppermute | solution.py:393
  20.6 24.6 %collective-permute-start.1 = (f32[104,128]{1,0:T(8,128)S(1)}, f32[104,128]{1,0:T(8,128)S(1)}, u32[]{:S(2)}, u32[]{:S(2)}) collective-permute-start(f32[104,128]{1,0:T(8,128)S(1)} %get-tuple-element.34), channel_id=1, source_target_pairs={{0,126},{1,127},{2,64},{3,65},{4,66},{5,67},{6,68},{7,69},{8,70},{... | collective-permute-start | bytes 159752 | tf_op jit(solution)/shard_map/ppermute | solution.py:393
  23.8 24.0 %collective-permute-start.2 = (f32[104,128]{1,0:T(8,128)S(1)}, f32[104,128]{1,0:T(8,128)S(1)}, u32[]{:S(2)}, u32[]{:S(2)}) collective-permute-start(f32[104,128]{1,0:T(8,128)S(1)} %get-tuple-element.35), channel_id=1, source_target_pairs={{0,127},{1,64},{2,65},{3,66},{4,67},{5,68},{6,69},{7,70},{8,71},{9... | collective-permute-start | bytes 159752 | tf_op jit(solution)/shard_map/ppermute | solution.py:393
  25.3 5.2 %collective-permute-start.10 = (f32[24,128]{1,0:T(8,128)S(1)}, f32[24,128]{1,0:T(8,128)S(1)}, u32[]{:S(2)}, u32[]{:S(2)}) collective-permute-start(f32[24,128]{1,0:T(8,128)S(1)} %get-tuple-element.43), channel_id=1, source_target_pairs={{0,95},{1,96},{2,97},{3,98},{4,99},{5,100},{6,101},{7,102},{8,103}... | collective-permute-start | bytes 36872 | tf_op jit(solution)/shard_map/ppermute | solution.py:393
  29.1 2.7 %collective-permute-start.11 = (f32[24,128]{1,0:T(8,128)S(1)}, f32[24,128]{1,0:T(8,128)S(1)}, u32[]{:S(2)}, u32[]{:S(2)}) collective-permute-start(f32[24,128]{1,0:T(8,128)S(1)} %get-tuple-element.44), channel_id=1, source_target_pairs={{0,97},{1,98},{2,99},{3,100},{4,101},{5,102},{6,103},{7,104},{8,10... | collective-permute-start | bytes 36872 | tf_op jit(solution)/shard_map/ppermute | solution.py:393
  30.5 2.0 %collective-permute-start.12 = (f32[56,128]{1,0:T(8,128)S(1)}, f32[56,128]{1,0:T(8,128)S(1)}, u32[]{:S(2)}, u32[]{:S(2)}) collective-permute-start(f32[56,128]{1,0:T(8,128)S(1)} %get-tuple-element.46), channel_id=1, source_target_pairs={{64,65},{65,66},{66,67},{67,68},{68,69},{69,70},{70,71},{71,72},{7... | collective-permute-start | bytes 86024 | tf_op jit(solution)/shard_map/ppermute | solution.py:389
  31.8 10.8 %collective-permute-start.13 = (f32[56,128]{1,0:T(8,128)S(1)}, f32[56,128]{1,0:T(8,128)S(1)}, u32[]{:S(2)}, u32[]{:S(2)}) collective-permute-start(f32[56,128]{1,0:T(8,128)S(1)} %get-tuple-element.47), channel_id=1, source_target_pairs={{64,127},{65,64},{66,65},{67,66},{68,67},{69,68},{70,69},{71,70},{... | collective-permute-start | bytes 86024 | tf_op jit(solution)/shard_map/ppermute | solution.py:389
  32.4 16.8 %collective-permute-start.3 = (f32[104,128]{1,0:T(8,128)S(1)}, f32[104,128]{1,0:T(8,128)S(1)}, u32[]{:S(2)}, u32[]{:S(2)}) collective-permute-start(f32[104,128]{1,0:T(8,128)S(1)} %get-tuple-element.36), channel_id=1, source_target_pairs={{0,64},{1,65},{2,66},{3,67},{4,68},{5,69},{6,70},{7,71},{8,72},{9,... | collective-permute-start | bytes 159752 | tf_op jit(solution)/shard_map/ppermute | solution.py:393
  42.6 6.6 %collective-permute-start.4 = (f32[104,128]{1,0:T(8,128)S(1)}, f32[104,128]{1,0:T(8,128)S(1)}, u32[]{:S(2)}, u32[]{:S(2)}) collective-permute-start(f32[104,128]{1,0:T(8,128)S(1)} %get-tuple-element.37), channel_id=1, source_target_pairs={{0,65},{1,66},{2,67},{3,68},{4,69},{5,70},{6,71},{7,72},{8,73},{9,... | collective-permute-start | bytes 159752 | tf_op jit(solution)/shard_map/ppermute | solution.py:393
  43.9 5.3 %collective-permute-start.5 = (f32[104,128]{1,0:T(8,128)S(1)}, f32[104,128]{1,0:T(8,128)S(1)}, u32[]{:S(2)}, u32[]{:S(2)}) collective-permute-start(f32[104,128]{1,0:T(8,128)S(1)} %get-tuple-element.38), channel_id=1, source_target_pairs={{0,66},{1,67},{2,68},{3,69},{4,70},{5,71},{6,72},{7,73},{8,74},{9,... | collective-permute-start | bytes 159752 | tf_op jit(solution)/shard_map/ppermute | solution.py:393
  45.2 4.4 %collective-permute-start.6 = (f32[104,128]{1,0:T(8,128)S(1)}, f32[104,128]{1,0:T(8,128)S(1)}, u32[]{:S(2)}, u32[]{:S(2)}) collective-permute-start(f32[104,128]{1,0:T(8,128)S(1)} %get-tuple-element.39), channel_id=1, source_target_pairs={{0,67},{1,68},{2,69},{3,70},{4,71},{5,72},{6,73},{7,74},{8,75},{9,... | collective-permute-start | bytes 159752 | tf_op jit(solution)/shard_map/ppermute | solution.py:393
  47.8 3.1 %collective-permute-start.7 = (f32[104,128]{1,0:T(8,128)S(1)}, f32[104,128]{1,0:T(8,128)S(1)}, u32[]{:S(2)}, u32[]{:S(2)}) collective-permute-start(f32[104,128]{1,0:T(8,128)S(1)} %get-tuple-element.40), channel_id=1, source_target_pairs={{0,96},{1,97},{2,98},{3,99},{4,100},{5,101},{6,102},{7,103},{8,104... | collective-permute-start | bytes 159752 | tf_op jit(solution)/shard_map/ppermute | solution.py:393
  51.0 4.6 %copy-start.1 = (bf16[1,1,8,48,128,128]{5,4,3,2,1,0:T(8,128)(2,1)S(1)}, bf16[1,1,8,48,128,128]{5,4,3,2,1,0:T(8,128)(2,1)}, u32[]{:S(2)}) copy-start(bf16[1,1,8,48,128,128]{5,4,3,2,1,0:T(8,128)(2,1)} %r_20_.1) | copy-start | bytes 37748740
  56.0 13.3 %collective-permute-start.22 = (f32[32,128]{1,0:T(8,128)S(1)}, f32[32,128]{1,0:T(8,128)S(1)}, u32[]{:S(2)}, u32[]{:S(2)}) collective-permute-start(f32[32,128]{1,0:T(8,128)S(1)} %get-tuple-element.56), channel_id=1, source_target_pairs={{64,60},{65,61},{66,62},{67,63},{68,0},{69,1},{70,2},{71,3},{72,4}... | collective-permute-start | bytes 49160 | tf_op jit(solution)/shard_map/ppermute | solution.py:393
  57.3 16.6 %collective-permute-start.23 = (f32[32,128]{1,0:T(8,128)S(1)}, f32[32,128]{1,0:T(8,128)S(1)}, u32[]{:S(2)}, u32[]{:S(2)}) collective-permute-start(f32[32,128]{1,0:T(8,128)S(1)} %get-tuple-element.57), channel_id=1, source_target_pairs={{64,4},{65,5},{66,6},{67,7},{68,8},{69,9},{70,10},{71,11},{72,12},... | collective-permute-start | bytes 49160 | tf_op jit(solution)/shard_map/ppermute | solution.py:393
  58.6 25.9 %collective-permute-start.14 = (f32[64,128]{1,0:T(8,128)S(1)}, f32[64,128]{1,0:T(8,128)S(1)}, u32[]{:S(2)}, u32[]{:S(2)}) collective-permute-start(f32[64,128]{1,0:T(8,128)S(1)} %get-tuple-element.48), channel_id=1, source_target_pairs={{64,61},{65,62},{66,63},{67,0},{68,1},{69,2},{70,3},{71,4},{72,5},... | collective-permute-start | bytes 98312 | tf_op jit(solution)/shard_map/ppermute | solution.py:393
  59.9 25.9 %collective-permute-start.15 = (f32[64,128]{1,0:T(8,128)S(1)}, f32[64,128]{1,0:T(8,128)S(1)}, u32[]{:S(2)}, u32[]{:S(2)}) collective-permute-start(f32[64,128]{1,0:T(8,128)S(1)} %get-tuple-element.49), channel_id=1, source_target_pairs={{64,62},{65,63},{66,0},{67,1},{68,2},{69,3},{70,4},{71,5},{72,6},{... | collective-permute-start | bytes 98312 | tf_op jit(solution)/shard_map/ppermute | solution.py:393
  61.2 25.9 %collective-permute-start.16 = (f32[64,128]{1,0:T(8,128)S(1)}, f32[64,128]{1,0:T(8,128)S(1)}, u32[]{:S(2)}, u32[]{:S(2)}) collective-permute-start(f32[64,128]{1,0:T(8,128)S(1)} %get-tuple-element.50), channel_id=1, source_target_pairs={{64,63},{65,0},{66,1},{67,2},{68,3},{69,4},{70,5},{71,6},{72,7},{7... | collective-permute-start | bytes 98312 | tf_op jit(solution)/shard_map/ppermute | solution.py:393
  69.2 8.3 %collective-permute-start.24 = (f32[32,128]{1,0:T(8,128)S(1)}, f32[32,128]{1,0:T(8,128)S(1)}, u32[]{:S(2)}, u32[]{:S(2)}) collective-permute-start(f32[32,128]{1,0:T(8,128)S(1)} %get-tuple-element.58), channel_id=1, source_target_pairs={{64,31},{65,32},{66,33},{67,34},{68,35},{69,36},{70,37},{71,38},{7... | collective-permute-start | bytes 49160 | tf_op jit(solution)/shard_map/ppermute | solution.py:393
  73.9 9.3 %collective-permute-start.25 = (f32[32,128]{1,0:T(8,128)S(1)}, f32[32,128]{1,0:T(8,128)S(1)}, u32[]{:S(2)}, u32[]{:S(2)}) collective-permute-start(f32[32,128]{1,0:T(8,128)S(1)} %get-tuple-element.59), channel_id=1, source_target_pairs={{64,33},{65,34},{66,35},{67,36},{68,37},{69,38},{70,39},{71,40},{7... | collective-permute-start | bytes 49160 | tf_op jit(solution)/shard_map/ppermute | solution.py:393
  77.5 10.9 %collective-permute-start.17 = (f32[64,128]{1,0:T(8,128)S(1)}, f32[64,128]{1,0:T(8,128)S(1)}, u32[]{:S(2)}, u32[]{:S(2)}) collective-permute-start(f32[64,128]{1,0:T(8,128)S(1)} %get-tuple-element.51), channel_id=1, source_target_pairs={{64,0},{65,1},{66,2},{67,3},{68,4},{69,5},{70,6},{71,7},{72,8},{73... | collective-permute-start | bytes 98312 | tf_op jit(solution)/shard_map/ppermute | solution.py:393
  83.2 10.7 %collective-permute-start.18 = (f32[64,128]{1,0:T(8,128)S(1)}, f32[64,128]{1,0:T(8,128)S(1)}, u32[]{:S(2)}, u32[]{:S(2)}) collective-permute-start(f32[64,128]{1,0:T(8,128)S(1)} %get-tuple-element.52), channel_id=1, source_target_pairs={{64,1},{65,2},{66,3},{67,4},{68,5},{69,6},{70,7},{71,8},{72,9},{73... | collective-permute-start | bytes 98312 | tf_op jit(solution)/shard_map/ppermute | solution.py:393
  84.5 11.0 %collective-permute-start.19 = (f32[64,128]{1,0:T(8,128)S(1)}, f32[64,128]{1,0:T(8,128)S(1)}, u32[]{:S(2)}, u32[]{:S(2)}) collective-permute-start(f32[64,128]{1,0:T(8,128)S(1)} %get-tuple-element.53), channel_id=1, source_target_pairs={{64,2},{65,3},{66,4},{67,5},{68,6},{69,7},{70,8},{71,9},{72,10},{7... | collective-permute-start | bytes 98312 | tf_op jit(solution)/shard_map/ppermute | solution.py:393
  85.8 9.6 %collective-permute-start.20 = (f32[64,128]{1,0:T(8,128)S(1)}, f32[64,128]{1,0:T(8,128)S(1)}, u32[]{:S(2)}, u32[]{:S(2)}) collective-permute-start(f32[64,128]{1,0:T(8,128)S(1)} %get-tuple-element.54), channel_id=1, source_target_pairs={{64,3},{65,4},{66,5},{67,6},{68,7},{69,8},{70,9},{71,10},{72,11},{... | collective-permute-start | bytes 98312 | tf_op jit(solution)/shard_map/ppermute | solution.py:393
  87.1 8.3 %collective-permute-start.21 = (f32[64,128]{1,0:T(8,128)S(1)}, f32[64,128]{1,0:T(8,128)S(1)}, u32[]{:S(2)}, u32[]{:S(2)}) collective-permute-start(f32[64,128]{1,0:T(8,128)S(1)} %get-tuple-element.55), channel_id=1, source_target_pairs={{64,32},{65,33},{66,34},{67,35},{68,36},{69,37},{70,38},{71,39},{7... | collective-permute-start | bytes 98312 | tf_op jit(solution)/shard_map/ppermute | solution.py:393

commit v2 on v1

v2 whole, which is shorter than its diff:
```python
import jax
import jax.numpy as jnp
from jax import lax
from jax.experimental import pallas as pl
from jax.experimental.pallas import tpu as pltpu
from jax.sharding import PartitionSpec as P

TILE = 128
BLK = 8
FLUX = 10
SURF = 4
HW = 64
SUBSTEPS = 2
AXES = ("sec", "blk")
NEAR = (-3, -2, -1, 0, 1, 2, 3)
FLUX_HALO = (0, 1, 8)
SURF_HALO = (0, 1, 2, 3)
LAND, COEF, LINK, TABLE = 8, 9, 21, 27
GROUP = 8
VMEM_BYTES = 56 * 1024 * 1024


def offsets_of(count):
    return list(NEAR) + [count // 2]


def slots_of(count):
    return {o: i for i, o in enumerate(offsets_of(count))}


def routes_of(count):
    half = count // 2
    return [(3, -3), (2, -2), (1, -1), (half, -4), (half - 1, half + 1), (4, None)]


WHOLE = 4
BESIDE = 2
SIDE = 56


def softplus(x):
    return jnp.maximum(x, 0.0) + jnp.log1p(jnp.exp(-jnp.abs(x)))


def sigmoid(x):
    return 1.0 / (1.0 + jnp.exp(-x))


def link_code(links, rows):
    place = links + (TILE - HW)
    return (place & (TILE - 1)) + jnp.where((place >> 7) == rows + 1, 0, TILE)


def gatherer(code):
    count = code[0].shape[0]
    lane = lax.broadcasted_iota(jnp.int32, (count, TILE), 1)
    low = lane < HW
    where = [(c & (TILE - 1), c >= TILE) for c in code]

    def take(x, index):
        return jnp.take_along_axis(x, index, axis=1, mode="promise_in_bounds")

    def spread(x):
        beside = jnp.where(low, pltpu.roll(x, count - 1, 0), pltpu.roll(x, 1, 0))
        return [jnp.where(far, take(beside, index), take(x, index)) - x for index, far in where]

    return spread


def compute_fluxes(a, ocean_frac):
    speed = jnp.sqrt(a[0] * a[0] + a[1] * a[1] + 1.0)
    sensible = 0.3 * speed * (a[7] - a[2])
    latent = 0.3 * speed * (jnp.tanh(a[7]) - a[3])
    net_short = 0.8 * softplus(a[4])
    net_long = softplus(a[5]) - softplus(a[7])
    rain = softplus(a[6])
    rows = [
        0.5 * speed * a[0],
        0.5 * speed * a[1],
        sensible,
        latent,
        net_short,
        net_long,
        rain,
        0.5 * latent,
        rain - 0.5 * latent,
        net_short + net_long - sensible - latent,
    ]
    return [r * ocean_frac for r in rows]


def start_tiles(tiles, weights, sems):
    for i in range(weights.shape[0]):
        pltpu.make_async_copy(tiles.at[0, 0, i], weights.at[i], sems.at[i]).start()


def run_tiles(fields, tiles, weights, sems, src, dst, table, sums):
    rows = len(fields) * BLK
    block = lax.broadcasted_iota(jnp.int32, (rows, TILE), 0) & (BLK - 1)
    for s in range(BLK):
        spread = jnp.concatenate([jnp.broadcast_to(f[s : s + 1], (BLK, TILE)) for f in fields], axis=0)
        for d in range(BLK):
            table[s * (BLK + 1) + d] = jnp.where(block == d, spread, 0.0).astype(jnp.bfloat16)
        table[s * (BLK + 1) + BLK] = jnp.zeros((rows, TILE), jnp.bfloat16)
    slots = weights.shape[1]

    def one_offset(i, carry):
        pltpu.make_async_copy(tiles.at[0, 0, i], weights.at[i], sems.at[i]).wait()
        total = jnp.zeros((rows, TILE), jnp.float32)
        for first in range(0, slots, GROUP):
            left = []
            for j in range(first, first + GROUP):
                target = dst[i, j]
                left.append(table[src[i, j] * (BLK + 1) + jnp.where(target < 0, BLK, target)])
            right = [weights[i, j] for j in range(first, first + GROUP)]
            total = total + lax.dot_general(
                jnp.concatenate(left, axis=1),
                jnp.concatenate(right, axis=1),
                (((1,), (1,)), ((), ())),
                preferred_element_type=jnp.float32,
            )
        sums[i] = total
        return carry

    lax.fori_loop(0, weights.shape[0], one_offset, 0)


def write_message(sums, out, base, offset, slots, rows, halo, depth):
    if offset in slots:
        out[base : base + rows] = sums[slots[offset]]
        base += rows
    row = lax.broadcasted_iota(jnp.int32, (BLK, TILE), 0)
    after, before = slots.get(offset + 1), slots.get(offset - 1)
    for f in halo:
        part = jnp.zeros((BLK, TILE), jnp.float32)
        if after is not None:
            part = jnp.where(row < depth, sums[after, f * BLK : (f + 1) * BLK], part)
        if before is not None:
            part = jnp.where(row >= BLK - depth, sums[before, f * BLK : (f + 1) * BLK], part)
        out[base : base + BLK] = part
        base += BLK
    return base


def write_messages(sums, outs, handed, count, rows, halo, depth):
    slots = slots_of(count)
    base = 0
    for out, (near, far) in zip(outs[1:], routes_of(count)):
        write_message(sums, out, 0, near, slots, rows, halo, depth)
        if far is not None:
            base = write_message(sums, handed, base, far, slots, rows, halo, depth)
    write_message(sums, outs[0], 0, 0, slots, rows, halo, depth)


def fetch(pairs, sems):
    copies = [pltpu.make_async_copy(a, b, sems.at[n]) for n, (a, b) in enumerate(pairs)]
    for c in copies:
        c.start()
    return copies


def lay_out(row_of, count, out, base, change=None):
    for c in range(count):
        for r in range(BLK):
            piece = row_of(c, pl.ds(r * TILE, TILE))
            if change is not None:
                piece = change(piece, r)
            out[(base + c) * BLK + r : (base + c) * BLK + r + 1] = piece.astype(out.dtype)


def lay_out_links(v_links, v_coef, v_land, out, coef, links, land):
    lay_out(lambda c, at: v_coef[0, c, 0:1, at], 6, out, coef)
    lay_out(lambda c, at: v_coef[0, c, 1:2, at], 6, out, coef + 6)
    lay_out(lambda c, at: v_links[c, :, at], 6, out, links, link_code)
    lay_out(lambda c, at: v_land[:, at], 1, out, land)


def send_kernel(count, state, links, coef, land, tile_src, targets, tiles, *refs):
    outs, (handed, low, own) = refs[:7], refs[7:10]
    (weights, table, sums, src, dst, v_state, v_links, v_coef, v_land, work, wsems, sems) = refs[10:]
    section = lax.axis_index("sec")

    @pl.when(section == 0)
    def _():
        copies = fetch([(state.at[0], v_state), (land, v_land), (tile_src.at[0, 0], src), (targets.at[0], dst)], sems)
        start_tiles(tiles, weights, wsems)
        copies[0].wait()
        copies[1].wait()
        lay_out(lambda c, at: v_state[c : c + 1, at], BLK, work, 0)
        lay_out(lambda c, at: v_land[:, at], 1, work, LAND)
        channels = [work[c * BLK : (c + 1) * BLK] for c in range(LAND + 1)]
        fields = compute_fluxes(channels[:LAND], channels[LAND])
        copies[2].wait()
        copies[3].wait()
        run_tiles(fields, tiles, weights, wsems, src, dst, table, sums)
        write_messages(sums, outs, handed, count, FLUX * BLK, FLUX_HALO, 2)

    @pl.when(section == 1)
    def _():
        copies = fetch([(state.at[0], v_state), (land, v_land), (links, v_links), (coef, v_coef)], sems)
        outs[0][...] = jnp.zeros_like(outs[0])
        for c in copies:
            c.wait()
        lay_out(lambda c, at: v_state[c : c + 1, at], BLK, own, 0)
        lay_out_links(v_links, v_coef, v_land, own, COEF, LINK, LAND)
        for c in range(TABLE):
            low[2 * c : 2 * c + 2] = own[c * BLK : c * BLK + 2]
            handed[2 * c : 2 * c + 2] = own[c * BLK + 6 : c * BLK + 8]


def sea_kernel(count, here, there, own_h, links, coef, land, tile_src, targets, tiles, *refs):
    outs, (handed, keep) = refs[:7], refs[7:9]
    (weights, table, sums, src, dst, v_links, v_coef, v_land, own, v_here, v_there, edge, wsems, sems) = refs[9:]
    section = lax.axis_index("sec")

    @pl.when(section == 0)
    def _():
        copies = fetch([(land, v_land), (links, v_links), (coef, v_coef)], sems)
        outs[0][...] = jnp.zeros_like(outs[0])
        for c in copies:
            c.wait()
        lay_out_links(v_links, v_coef, v_land, keep, 0, 12, 18)

    @pl.when(section == 1)
    def _():
        copies = fetch(
            [(here, v_here), (there, v_there), (own_h, own), (tile_src.at[0, 0], src), (targets.at[1], dst)], sems
        )
        start_tiles(tiles, weights, wsems)
        edge[...] = jnp.zeros_like(edge)
        for c in copies:
            c.wait()
        rows = FLUX * BLK
        side = rows + len(FLUX_HALO) * BLK
        for c in range(TABLE):
            edge[c * BLK : c * BLK + 2] = v_here[side + 2 * c : side + 2 * c + 2]
            edge[c * BLK + 6 : c * BLK + 8] = v_there[side + 2 * c : side + 2 * c + 2]
        forcing = v_here[0:side] + v_there[0:side]

        def near(c):
            return own[c * BLK : (c + 1) * BLK]

        def wide(c):
            return jnp.concatenate([near(c), edge[c * BLK : (c + 1) * BLK]], axis=0)

        def force(f):
            return forcing[f * BLK : (f + 1) * BLK]

        def force_wide(f):
            return jnp.concatenate([force(f), force(FLUX + FLUX_HALO.index(f))], axis=0)

        spread = gatherer([wide(LINK + k).astype(jnp.int32) for k in range(6)])
        grad_wx = [wide(COEF + k) for k in range(6)]
        grad_wy = [wide(COEF + 6 + k) for k in range(6)]
        wet = wide(LAND)
        height, flow_u, flow_v = wide(0), wide(1), wide(2)
        depth = 1.0 + sigmoid(wide(3))
        ice = sigmoid(wide(5))
        coriol = 0.3 * jnp.tanh(wide(6))
        mixed = 1.0 + softplus(near(7))
        drag = 0.3 * (1.0 - ice)
        push_u, push_v, push_h = drag * force_wide(0), drag * force_wide(1), 0.1 * force_wide(8)
        for _ in range(SUBSTEPS):
            slopes = spread(height)
            grad_x = sum(w * s for w, s in zip(grad_wx, slopes))
            grad_y = sum(w * s for w, s in zip(grad_wy, slopes))
            next_u = wet * (flow_u - 0.5 * grad_x + coriol * flow_v + push_u)
            next_v = wet * (flow_v - 0.5 * grad_y - coriol * flow_u + push_v)
            moved_u = spread(depth * next_u)
            moved_v = spread(depth * next_v)
            moved = sum(wx * a + wy * b for wx, wy, a, b in zip(grad_wx, grad_wy, moved_u, moved_v))
            height = height - 0.5 * moved + push_h
            flow_u, flow_v = next_u, next_v
        new_temp = near(4) + 0.2 * near(LAND) * force(9) / mixed
        u, v = flow_u[:BLK], flow_v[:BLK]
        for r, field in enumerate([height[:BLK], u, v, new_temp]):
            keep[r * BLK : (r + 1) * BLK] = field
        run_tiles([new_temp, ice[:BLK], u, v], tiles, weights, wsems, src, dst, table, sums)
        write_messages(sums, outs, handed, count, SURF * BLK, SURF_HALO, 1)


def last_kernel(here, there, keep, out):
    section = lax.axis_index("sec")

    def part(c):
        return keep[c * BLK : (c + 1) * BLK]

    def put(r, field):
        for b in range(BLK):
            out[0, r : r + 1, b * TILE : (b + 1) * TILE] = field[b : b + 1]

    @pl.when(section == 0)
    def _():
        returned = here[...] + there[...]
        blank = jnp.zeros((BLK, TILE), jnp.float32)
        code = [jnp.concatenate([part(12 + k), blank], axis=0).astype(jnp.int32) for k in range(6)]
        spread = gatherer(code)
        for r in range(SURF):
            field = returned[r * BLK : (r + 1) * BLK]
            outer = returned[(SURF + r) * BLK : (SURF + r + 1) * BLK]
            slopes = spread(jnp.concatenate([field, outer], axis=0))
            first = 0 if r < 2 else 6
            smooth = field + sum(part(first + k) * s[:BLK] for k, s in enumerate(slopes))
            put(r, part(18) * smooth)

    @pl.when(section == 1)
    def _():
        for r in range(SURF):
            put(r, part(r))


def exchange(outs, handed, source, section, count, rows, halo, side=None):
    swap = [(0, 1), (1, 0)]
    crossed = lax.ppermute(handed, "sec", swap)
    mine = section == source
    full = rows + halo
    base = 0
    got = []
    for n, (near, far) in enumerate(routes_of(count)):
        own = outs[n + 1]
        if far is None:
            other = jnp.zeros_like(own)
        elif far in slots_of(count) or n >= WHOLE:
            other = crossed[base : base + own.shape[0]]
            base += own.shape[0]
        else:
            other = jnp.concatenate([jnp.zeros((rows, TILE), jnp.float32), crossed[base : base + halo]])
            base += halo
        if side is not None and n == BESIDE:
            own = jnp.concatenate([own, crossed[:SIDE]])
            other = jnp.concatenate([other, side])
        far = near if far is None else far
        pairs = [(source * count + i, source * count + (i + near) % count) for i in range(count)]
        pairs += [((1 - source) * count + i, (1 - source) * count + (i + far) % count) for i in range(count)]
        got.append(lax.ppermute(jnp.where(mine, own, other), AXES, pairs))
    total = outs[0] + sum(g[:full] for g in got[:WHOLE])
    parts = [total[:rows], total[rows:] + sum(got[WHOLE:])]
    if side is not None:
        parts.append(got[BESIDE][full:])
    here = jnp.concatenate(parts)
    return here, lax.ppermute(here, "sec", swap)


def body(surface_state, neighbours, coupling_coef, land, tile_src, dst_lists, tiles):
    count = lax.axis_size("blk")
    section = lax.axis_index("sec")
    recv_count, slots = tiles.shape[2:4]
    f32, i32 = jnp.float32, jnp.int32
    anywhere = pl.BlockSpec(memory_space=pl.ANY)
    inside = pl.BlockSpec(memory_space=pltpu.VMEM)
    params = pltpu.CompilerParams(vmem_limit_bytes=VMEM_BYTES)
    targets = lax.dynamic_index_in_dim(dst_lists, lax.axis_index("blk"), axis=1, keepdims=False)
    links = neighbours.transpose(1, 0, 2)
    coef = coupling_coef.transpose(0, 2, 1, 3)

    def shaped(rows):
        return jax.ShapeDtypeStruct((rows, TILE), f32)

    def shapes_for(rows, halo):
        routes = routes_of(count)
        slot = slots_of(count)
        outs = [shaped(rows + halo if near in slot else halo) for near, _ in [(0, 0)] + routes]
        handed = sum(rows + halo if far in slot else halo for _, far in routes if far is not None)
        return outs + [shaped(handed)]

    def remap_scratch(rows):
        return [
            pltpu.VMEM((recv_count, slots, TILE, TILE), jnp.bfloat16),
            pltpu.VMEM((BLK * (BLK + 1), rows, TILE), jnp.bfloat16),
            pltpu.VMEM((recv_count, rows, TILE), f32),
            pltpu.SMEM((recv_count, slots), i32),
            pltpu.SMEM((recv_count, slots), i32),
        ]

    cost = pl.CostEstimate(flops=int(2 * tiles.size * 16), bytes_accessed=int(tiles.size * 2), transcendentals=0)
    width = BLK * TILE
    rows, halo = FLUX * BLK, len(FLUX_HALO) * BLK
    shapes = shapes_for(rows, halo)
    sent = pl.pallas_call(
        lambda *r: send_kernel(count, *r),
        name="flux_remap",
        out_shape=shapes + [shaped(SIDE), shaped(TABLE * BLK)],
        in_specs=[anywhere] * 7,
        out_specs=[inside] * (len(shapes) + 2),
        scratch_shapes=remap_scratch(rows)
        + [
            pltpu.VMEM((8, width), f32),
            pltpu.VMEM((6, 1, width), i32),
            pltpu.VMEM((1, 6, 2, width), f32),
            pltpu.VMEM((1, width), i32),
            pltpu.VMEM(((LAND + 1) * BLK, TILE), f32),
            pltpu.SemaphoreType.DMA((recv_count,)),
            pltpu.SemaphoreType.DMA((4,)),
        ],
        compiler_params=params,
        cost_estimate=cost,
    )(surface_state, links, coef, land, tile_src, targets, tiles)
    outs, (handed, low, own) = sent[:7], sent[7:]
    here, there = exchange(outs, handed, 0, section, count, rows, halo, low)

    rows, halo = SURF * BLK, len(SURF_HALO) * BLK
    shapes = shapes_for(rows, halo)
    sent = pl.pallas_call(
        lambda *r: sea_kernel(count, *r),
        name="sea_remap",
        out_shape=shapes + [shaped(19 * BLK)],
        in_specs=[anywhere] * 9,
        out_specs=[inside] * (len(shapes) + 1),
        scratch_shapes=remap_scratch(rows)
        + [
            pltpu.VMEM((6, 1, width), i32),
            pltpu.VMEM((1, 6, 2, width), f32),
            pltpu.VMEM((1, width), i32),
            pltpu.VMEM((TABLE * BLK, TILE), f32),
            pltpu.VMEM(here.shape, f32),
            pltpu.VMEM(here.shape, f32),
            pltpu.VMEM((TABLE * BLK, TILE), f32),
            pltpu.SemaphoreType.DMA((recv_count,)),
            pltpu.SemaphoreType.DMA((5,)),
        ],
        compiler_params=params,
        cost_estimate=cost,
    )(here, there, own, links, coef, land, tile_src, targets, tiles)
    outs, (handed, keep) = sent[:7], sent[7:]
    here, there = exchange(outs, handed, 1, section, count, rows, halo)

    return pl.pallas_call(
        last_kernel,
        name="smooth",
        out_shape=jax.ShapeDtypeStruct((1, SURF, width), f32),
        in_specs=[inside] * 3,
        out_specs=inside,
    )(here, there, keep)


def solution(mesh):
    in_specs = (
        P("sec", None, "blk"),
        P("sec", None, "blk"),
        P("sec", None, None, "blk"),
        P("sec", "blk"),
        P("sec", "blk", None, None),
        P(),
        P("sec", "blk", None, None, None, None),
    )
    out_specs = P("sec", None, "blk")
    return jax.shard_map(body, mesh=mesh, in_specs=in_specs, out_specs=out_specs, check_vma=False)
```

time: 97.8 us -> 71.3 us (0.73)
  the two profiles are of different devices: /device:TPU:0 before, /device:TPU:1 now
where the time goes in v2:
time: 71.3 us; the launch traced here: 70.7 us
  starting transfers between devices  38.5 us (54%)
  Pallas kernels  13.2 us (19%)
  waiting for transfers between devices  10.3 us (14%)
  other arithmetic  5.51 us (8%)
  local copies, waits for them, and re-layouts  3.17 us (4%)
    ppermute x12, starting transfers between devices, exchange(): got.append(lax.ppermute(jnp.where(mine, own, other), AXES, pairs))  23.7 us
    pallas_call x1, Pallas kernels, body(): pl.pallas_call(lambda *r: sea_kernel(count, *r), name='sea_remap', out_sh...  9.73 us
    ppermute x2, starting transfers between devices, exchange(): crossed = lax.ppermute(handed, 'sec', swap)  9.35 us
    ppermute x12, waiting for transfers between devices, exchange(): got.append(lax.ppermute(jnp.where(mine, own, other), AXES, pairs))  5.69 us
    ppermute x2, starting transfers between devices, exchange(): return (here, lax.ppermute(here, 'sec', swap))  5.42 us
    select_n x9, other arithmetic, exchange(): got.append(lax.ppermute(jnp.where(mine, own, other), AXES, pairs))  3.88 us
    unnamed x11, local copies, waits for them, and re-layouts  3 us
    ppermute x2, waiting for transfers between devices, exchange(): crossed = lax.ppermute(handed, 'sec', swap)  2.81 us
  transfers between devices with their start and end apart: 16, of which 9 were waited for; matrix products, arithmetic and copies ran while one was open for 5% of the time, Pallas kernels for 0%

profile of v2, /device:TPU:1, one launch (start us, length us, event | category | flops | bytes accessed | tf_op | source)
XLA Modules:
  0.0 70.7 jit_solution(2855782092350799110)
XLA Ops:
  0.0 0.0 copy-start
  0.0 1.0 %copy-done = s32[2,64,8,48]{1,3,2,0:T(8,128)S(1)} copy-done((s32[2,64,8,48]{1,3,2,0:T(8,128)S(1)}, s32[2,64,8,48]{1,3,2,0:T(8,128)}, u32[]{:S(2)}) %copy-start) | copy-done | bytes 196632
  1.0 0.2 constant_dynamic-slice_fusion
  1.2 0.8 %copy.9 = s32[2,1,8,48]{3,2,0,1:T(8,128)} copy(s32[2,1,8,48]{1,3,2,0:T(8,128)S(1)} %constant_dynamic-slice_fusion) | data formatting | bytes 6144
  1.9 1.9 %flux_remap.1 = (f32[104,128]{1,0:T(8,128)}, f32[104,128]{1,0:T(8,128)}, f32[104,128]{1,0:T(8,128)}, f32[104,128]{1,0:T(8,128)}, f32[104,128]{1,0:T(8,128)}, /*i...) custom-call(f32[1,8,1024]{2,1,0:T(8,128)} %r_0_.1, ...), custom_call_target="tpu_custom_call" | custom-call | flops 201326592 | bytes 12582912 | tf_op jit(solution)/shard_map/flux_remap/pallas_call | solution.py:379
  3.8 9.3 %collective-permute-start = (f32[360,128]{1,0:T(8,128)}, f32[360,128]{1,0:T(8,128)S(1)}, u32[]{:S(2)}, u32[]{:S(2)}) collective-permute-start(f32[360,128]{1,0:T(8,128)} %get-tuple-element.26), channel_id=1, source_target_pairs={{0,64},{64,0},{1,65},{65,1},{2,66},{66,2},{3,67},{67,3},{4,68},{68... | collective-permute-start | bytes 552968 | tf_op jit(solution)/shard_map/ppermute | solution.py:314
  13.1 1.3 %collective-permute-done = f32[360,128]{1,0:T(8,128)S(1)} collective-permute-done((f32[360,128]{1,0:T(8,128)}, f32[360,128]{1,0:T(8,128)S(1)}, u32[]{:S(2)}, u32[]{:S(2)}) %collective-permute-start) | collective-permute-done | bytes 184352 | tf_op jit(solution)/shard_map/ppermute | solution.py:314
  14.4 0.8 %maximum_select_fusion = f32[160,128]{1,0:T(8,128)S(1)} fusion(f32[56,128]{1,0:T(8,128)S(1)} %slice.70, f32[104,128]{1,0:T(8,128)} %get-tuple-element.28, f32[56,128]{1,0:T(8,128)} %get-tuple-element.29, f32[104,128]{1,0:T(8,128)S(1)} %get-tuple-element.46, pred[]{:T(512)S(6)} %eq.6), kind=kLoop, calls=%fused_computation | loop fusion | flops 61440 | bytes 245761 | tf_op jit(solution)/shard_map/jit(_where)/select_n | solution.py:335
  15.2 8.6 %collective-permute-start.3 = (f32[160,128]{1,0:T(8,128)S(1)}, f32[160,128]{1,0:T(8,128)S(1)}, u32[]{:S(2)}, u32[]{:S(2)}) collective-permute-start(f32[160,128]{1,0:T(8,128)S(1)} %maximum_select_fusion), channel_id=1, source_target_pairs={{0,1},{1,2},{2,3},{3,4},{4,5},{5,6},{6,7},{7,8},{8,9},{9,10},{10,1... | collective-permute-start | bytes 245768 | tf_op jit(solution)/shard_map/ppermute | solution.py:335
  23.8 0.5 collective-permute-start.4
  24.3 0.0 collective-permute-start.1
  24.3 1.2 %collective-permute-start.2 = (f32[104,128]{1,0:T(8,128)S(1)}, f32[104,128]{1,0:T(8,128)S(1)}, u32[]{:S(2)}, u32[]{:S(2)}) collective-permute-start(f32[104,128]{1,0:T(8,128)S(1)} %get-tuple-element.45), channel_id=1, source_target_pairs={{0,2},{1,3},{2,4},{3,5},{4,6},{5,7},{6,8},{7,9},{8,10},{9,11},{10,... | collective-permute-start | bytes 159752 | tf_op jit(solution)/shard_map/ppermute | solution.py:335
  25.5 1.3 %collective-permute-start.6 = (f32[24,128]{1,0:T(8,128)S(1)}, f32[24,128]{1,0:T(8,128)S(1)}, u32[]{:S(2)}, u32[]{:S(2)}) collective-permute-start(f32[24,128]{1,0:T(8,128)S(1)} %broadcast_select_fusion.1), channel_id=1, source_target_pairs={{0,4},{1,5},{2,6},{3,7},{4,8},{5,9},{6,10},{7,11},{8,12},{9,13},{1... | collective-permute-start | bytes 36872 | tf_op jit(solution)/shard_map/ppermute | solution.py:335
  26.8 0.3 collective-permute-done.4
  27.1 1.9 %collective-permute-start.5 = (f32[24,128]{1,0:T(8,128)S(1)}, f32[24,128]{1,0:T(8,128)S(1)}, u32[]{:S(2)}, u32[]{:S(2)}) collective-permute-start(f32[24,128]{1,0:T(8,128)S(1)} %get-tuple-element.43), channel_id=1, source_target_pairs={{0,31},{1,32},{2,33},{3,34},{4,35},{5,36},{6,37},{7,38},{8,39},{9,... | collective-permute-start | bytes 36872 | tf_op jit(solution)/shard_map/ppermute | solution.py:335
  29.0 0.1 collective-permute-done.1
  29.1 0.0 collective-permute-done.2
  29.1 0.0 collective-permute-done.3
  29.1 0.8 %fusion.1 = f32[104,128]{1,0:T(8,128)S(1)} fusion(f32[104,128]{1,0:T(8,128)} %get-tuple-element.24, f32[104,128]{1,0:T(8,128)S(1)} %collective-permute-done.4, f32[160,128]{1,0:T(8,128)S(1)} %collective-permute-done.3, f32[104,128]{1,0:T(8,128)S(1)} %collective-permute-done.1, f32[104,128]{1,0:T(8,128)S(1)} %collective-permute-done.2), kind=kLoop, calls=%fused_computation.4 | loop fusion | flops 53248 | bytes 319488 | tf_op jit(solution)/shard_map/add | solution.py:336
  30.0 1.4 %collective-permute-done.6 = f32[24,128]{1,0:T(8,128)S(1)} collective-permute-done((f32[24,128]{1,0:T(8,128)S(1)}, f32[24,128]{1,0:T(8,128)S(1)}, u32[]{:S(2)}, u32[]{:S(2)}) %collective-permute-start.6) | collective-permute-done | bytes 12320 | tf_op jit(solution)/shard_map/ppermute | solution.py:335
  31.4 2.8 %collective-permute-done.5 = f32[24,128]{1,0:T(8,128)S(1)} collective-permute-done((f32[24,128]{1,0:T(8,128)S(1)}, f32[24,128]{1,0:T(8,128)S(1)}, u32[]{:S(2)}, u32[]{:S(2)}) %collective-permute-start.5) | collective-permute-done | bytes 12320 | tf_op jit(solution)/shard_map/ppermute | solution.py:335
  34.2 0.0 copy-start.1
  34.2 2.3 %collective-permute-start.7 = (f32[160,128]{1,0:T(8,128)S(1)}, f32[160,128]{1,0:T(8,128)S(1)}, u32[]{:S(2)}, u32[]{:S(2)}) collective-permute-start(f32[160,128]{1,0:T(8,128)S(1)} %pad_maximum_fusion.r_0_), channel_id=1, source_target_pairs={{0,64},{64,0},{1,65},{65,1},{2,66},{66,2},{3,67},{67,3},{4,68},{68... | collective-permute-start | bytes 245768 | tf_op jit(solution)/shard_map/ppermute | solution.py:341
  36.5 0.9 %collective-permute-done.7.r_1_ = f32[160,128]{1,0:T(8,128)S(1)} collective-permute-done((f32[160,128]{1,0:T(8,128)S(1)}, f32[160,128]{1,0:T(8,128)S(1)}, u32[]{:S(2)}, u32[]{:S(2)}) %collective-permute-start.7) | collective-permute-done | bytes 81952 | tf_op jit(solution)/shard_map/ppermute | solution.py:341
  37.5 0.0 copy-start.3
  37.5 0.0 copy-done.1
  37.5 0.6 copy-done.3
  38.1 9.7 %sea_remap.1 = (f32[64,128]{1,0:T(8,128)}, f32[64,128]{1,0:T(8,128)}, f32[64,128]{1,0:T(8,128)}, f32[64,128]{1,0:T(8,128)}, f32[64,128]{1,0:T(8,128)}, /*index=5...) custom-call(f32[160,128]{1,0:T(8,128)} %copy-done.1, f32[160,128]{1,0:T(8,128)} %copy-done.3, ...), custom_call_target="tpu_custom_call" | custom-call | flops 201326592 | bytes 12582912 | tf_op jit(solution)/shard_map/sea_remap/pallas_call | solution.py:403
  47.8 0.1 collective-permute-start.8
  47.9 1.5 %collective-permute-done.8 = f32[256,128]{1,0:T(8,128)S(1)} collective-permute-done((f32[256,128]{1,0:T(8,128)}, f32[256,128]{1,0:T(8,128)S(1)}, u32[]{:S(2)}, u32[]{:S(2)}) %collective-permute-start.8) | collective-permute-done | bytes 131104 | tf_op jit(solution)/shard_map/ppermute | solution.py:314
  49.5 0.8 %slice_select_fusion.3 = (f32[64,128]{1,0:T(8,128)S(1)}, f32[64,128]{1,0:T(8,128)S(1)}, f32[64,128]{1,0:T(8,128)S(1)}) fusion(f32[64,128]{1,0:T(8,128)} %get-tuple-element.37, f32[256,128]{1,0:T(8,128)S(1)} %collective-permute-done.8, pred[]{:T(512)S(6)} %eq.7, f32[64,128]{1,0:T(8,128)} %get-tuple-element.38, f32[64,128]{1,0:T(8,128)} %get-tuple-element.35), kind=kLoop, calls=%fused_computation.9 | loop fusion | flops 24576 | bytes 294913 | tf_op jit(solution)/shard_map/jit(_where)/select_n | solution.py:335
  50.3 1.5 %collective-permute-start.10 = (f32[64,128]{1,0:T(8,128)S(1)}, f32[64,128]{1,0:T(8,128)S(1)}, u32[]{:S(2)}, u32[]{:S(2)}) collective-permute-start(f32[64,128]{1,0:T(8,128)S(1)} %get-tuple-element.50), channel_id=1, source_target_pairs={{64,66},{65,67},{66,68},{67,69},{68,70},{69,71},{70,72},{71,73},{7... | collective-permute-start | bytes 98312 | tf_op jit(solution)/shard_map/ppermute | solution.py:335
  51.8 2.4 %collective-permute-start.11 = (f32[64,128]{1,0:T(8,128)S(1)}, f32[64,128]{1,0:T(8,128)S(1)}, u32[]{:S(2)}, u32[]{:S(2)}) collective-permute-start(f32[64,128]{1,0:T(8,128)S(1)} %get-tuple-element.51), channel_id=1, source_target_pairs={{64,65},{65,66},{66,67},{67,68},{68,69},{69,70},{70,71},{71,72},{7... | collective-permute-start | bytes 98312 | tf_op jit(solution)/shard_map/ppermute | solution.py:335
  54.2 1.0 %collective-permute-start.9 = (f32[64,128]{1,0:T(8,128)S(1)}, f32[64,128]{1,0:T(8,128)S(1)}, u32[]{:S(2)}, u32[]{:S(2)}) collective-permute-start(f32[64,128]{1,0:T(8,128)S(1)} %get-tuple-element.52), channel_id=1, source_target_pairs={{64,67},{65,68},{66,69},{67,70},{68,71},{69,72},{70,73},{71,74},{7... | collective-permute-start | bytes 98312 | tf_op jit(solution)/shard_map/ppermute | solution.py:335
  55.2 0.7 %slice_select_fusion.5 = (f32[32,128]{1,0:T(8,128)S(1)}, f32[32,128]{1,0:T(8,128)S(1)}) fusion(f32[32,128]{1,0:T(8,128)} %get-tuple-element.40, f32[256,128]{1,0:T(8,128)S(1)} %collective-permute-done.8, pred[]{:T(512)S(6)} %eq.7), kind=kLoop, calls=%fused_computation.14 | loop fusion | flops 4096 | bytes 81921 | tf_op jit(solution)/shard_map/jit(_where)/select_n | solution.py:335
  55.9 0.8 %pad_select_fusion.1 = f32[64,128]{1,0:T(8,128)S(1)} fusion(f32[64,128]{1,0:T(8,128)} %get-tuple-element.39, f32[32,128]{1,0:T(8,128)S(1)} %get-tuple-element.49, pred[]{:T(512)S(6)} %eq.7), kind=kLoop, calls=%fused_computation.13 | loop fusion | flops 8192 | bytes 81921 | tf_op jit(solution)/shard_map/jit(_where)/select_n | solution.py:335
  56.6 0.3 collective-permute-start.12
  56.9 0.7 %broadcast_select_fusion = f32[32,128]{1,0:T(8,128)S(1)} fusion(f32[32,128]{1,0:T(8,128)} %get-tuple-element.41, pred[]{:T(512)S(6)} %eq.7), kind=kLoop, calls=%fused_computation.18 | loop fusion | flops 4096 | bytes 32769 | tf_op jit(solution)/shard_map/jit(_where)/select_n | solution.py:335
  57.6 1.7 %collective-permute-start.14 = (f32[32,128]{1,0:T(8,128)S(1)}, f32[32,128]{1,0:T(8,128)S(1)}, u32[]{:S(2)}, u32[]{:S(2)}) collective-permute-start(f32[32,128]{1,0:T(8,128)S(1)} %broadcast_select_fusion), channel_id=1, source_target_pairs={{64,68},{65,69},{66,70},{67,71},{68,72},{69,73},{70,74},{71,75},{7... | collective-permute-start | bytes 49160 | tf_op jit(solution)/shard_map/ppermute | solution.py:335
  59.3 0.0 collective-permute-done.10
  59.3 3.5 %collective-permute-start.13 = (f32[32,128]{1,0:T(8,128)S(1)}, f32[32,128]{1,0:T(8,128)S(1)}, u32[]{:S(2)}, u32[]{:S(2)}) collective-permute-start(f32[32,128]{1,0:T(8,128)S(1)} %get-tuple-element.48), channel_id=1, source_target_pairs={{64,95},{65,96},{66,97},{67,98},{68,99},{69,100},{70,101},{71,102}... | collective-permute-start | bytes 49160 | tf_op jit(solution)/shard_map/ppermute | solution.py:335
  62.7 0.0 collective-permute-done.11
  62.7 0.0 collective-permute-done.9
  62.7 0.0 collective-permute-done.12
  62.8 0.8 %add_add_fusion = f32[64,128]{1,0:T(8,128)S(1)} fusion(f32[64,128]{1,0:T(8,128)} %get-tuple-element.34, f32[64,128]{1,0:T(8,128)S(1)} %collective-permute-done.12, f32[64,128]{1,0:T(8,128)S(1)} %collective-permute-done.11, f32[64,128]{1,0:T(8,128)S(1)} %collective-permute-done.9, f32[64,128]{1,0:T(8,128)S(1)} %collective-permute-done.10), kind=kLoop, calls=%fused_computation.12 | loop fusion | flops 32768 | bytes 196608 | tf_op jit(solution)/shard_map/add | solution.py:336
  63.5 0.0 collective-permute-done.14
  63.5 1.0 %collective-permute-done.13 = f32[32,128]{1,0:T(8,128)S(1)} collective-permute-done((f32[32,128]{1,0:T(8,128)S(1)}, f32[32,128]{1,0:T(8,128)S(1)}, u32[]{:S(2)}, u32[]{:S(2)}) %collective-permute-start.13) | collective-permute-done | bytes 16416 | tf_op jit(solution)/shard_map/ppermute | solution.py:335
  64.6 0.0 copy-start.2
  64.6 3.1 %collective-permute-start.15 = (f32[64,128]{1,0:T(8,128)S(1)}, f32[64,128]{1,0:T(8,128)S(1)}, u32[]{:S(2)}, u32[]{:S(2)}) collective-permute-start(f32[64,128]{1,0:T(8,128)S(1)} %pad_maximum_fusion.1.here), channel_id=1, source_target_pairs={{0,64},{64,0},{1,65},{65,1},{2,66},{66,2},{3,67},{67,3},{4,68},{68... | collective-permute-start | bytes 98312 | tf_op jit(solution)/shard_map/ppermute | solution.py:341
  67.7 0.9 %collective-permute-done.15.there = f32[64,128]{1,0:T(8,128)S(1)} collective-permute-done((f32[64,128]{1,0:T(8,128)S(1)}, f32[64,128]{1,0:T(8,128)S(1)}, u32[]{:S(2)}, u32[]{:S(2)}) %collective-permute-start.15) | collective-permute-done | bytes 32800 | tf_op jit(solution)/shard_map/ppermute | solution.py:341
  68.6 0.0 copy-start.4
  68.6 0.0 copy-done.2
  68.6 0.6 copy-done.4
  69.2 1.5 %smooth.1 = f32[1,4,1024]{2,1,0:T(4,128)} custom-call(f32[64,128]{1,0:T(8,128)} %copy-done.2, f32[64,128]{1,0:T(8,128)} %copy-done.4, f32[152,128]{1,0:T(8,128)} %get-tuple-element.42.keep), custom_call_target="tpu_custom_call" | custom-call | tf_op jit(solution)/shard_map/smooth/pallas_call | solution.py:427
  (11 shorter events, 0.1 us)
Async XLA Ops:
  0.0 1.0 %copy-start = (s32[2,64,8,48]{1,3,2,0:T(8,128)S(1)}, s32[2,64,8,48]{1,3,2,0:T(8,128)}, u32[]{:S(2)}) copy-start(s32[2,64,8,48]{1,3,2,0:T(8,128)} %param.12) | copy-start | bytes 589828
  3.8 10.5 %collective-permute-start = (f32[360,128]{1,0:T(8,128)}, f32[360,128]{1,0:T(8,128)S(1)}, u32[]{:S(2)}, u32[]{:S(2)}) collective-permute-start(f32[360,128]{1,0:T(8,128)} %get-tuple-element.26), channel_id=1, source_target_pairs={{0,64},{64,0},{1,65},{65,1},{2,66},{66,2},{3,67},{67,3},{4,68},{68... | collective-permute-start | bytes 552968 | tf_op jit(solution)/shard_map/ppermute | solution.py:314
  15.2 13.9 %collective-permute-start.3 = (f32[160,128]{1,0:T(8,128)S(1)}, f32[160,128]{1,0:T(8,128)S(1)}, u32[]{:S(2)}, u32[]{:S(2)}) collective-permute-start(f32[160,128]{1,0:T(8,128)S(1)} %maximum_select_fusion), channel_id=1, source_target_pairs={{0,1},{1,2},{2,3},{3,4},{4,5},{5,6},{6,7},{7,8},{8,9},{9,10},{10,1... | collective-permute-start | bytes 245768 | tf_op jit(solution)/shard_map/ppermute | solution.py:335
  23.8 3.3 %collective-permute-start.4 = (f32[104,128]{1,0:T(8,128)S(1)}, f32[104,128]{1,0:T(8,128)S(1)}, u32[]{:S(2)}, u32[]{:S(2)}) collective-permute-start(f32[104,128]{1,0:T(8,128)S(1)} %pad_select_fusion), channel_id=1, source_target_pairs={{0,32},{1,33},{2,34},{3,35},{4,36},{5,37},{6,38},{7,39},{8,40},{9,... | collective-permute-start | bytes 159752 | tf_op jit(solution)/shard_map/ppermute | solution.py:335
  24.3 4.8 %collective-permute-start.1 = (f32[104,128]{1,0:T(8,128)S(1)}, f32[104,128]{1,0:T(8,128)S(1)}, u32[]{:S(2)}, u32[]{:S(2)}) collective-permute-start(f32[104,128]{1,0:T(8,128)S(1)} %get-tuple-element.47), channel_id=1, source_target_pairs={{0,3},{1,4},{2,5},{3,6},{4,7},{5,8},{6,9},{7,10},{8,11},{9,12},{10... | collective-permute-start | bytes 159752 | tf_op jit(solution)/shard_map/ppermute | solution.py:335
  24.3 4.8 %collective-permute-start.2 = (f32[104,128]{1,0:T(8,128)S(1)}, f32[104,128]{1,0:T(8,128)S(1)}, u32[]{:S(2)}, u32[]{:S(2)}) collective-permute-start(f32[104,128]{1,0:T(8,128)S(1)} %get-tuple-element.45), channel_id=1, source_target_pairs={{0,2},{1,3},{2,4},{3,5},{4,6},{5,7},{6,8},{7,9},{8,10},{9,11},{10,... | collective-permute-start | bytes 159752 | tf_op jit(solution)/shard_map/ppermute | solution.py:335
  25.5 5.9 %collective-permute-start.6 = (f32[24,128]{1,0:T(8,128)S(1)}, f32[24,128]{1,0:T(8,128)S(1)}, u32[]{:S(2)}, u32[]{:S(2)}) collective-permute-start(f32[24,128]{1,0:T(8,128)S(1)} %broadcast_select_fusion.1), channel_id=1, source_target_pairs={{0,4},{1,5},{2,6},{3,7},{4,8},{5,9},{6,10},{7,11},{8,12},{9,13},{1... | collective-permute-start | bytes 36872 | tf_op jit(solution)/shard_map/ppermute | solution.py:335
  27.1 7.1 %collective-permute-start.5 = (f32[24,128]{1,0:T(8,128)S(1)}, f32[24,128]{1,0:T(8,128)S(1)}, u32[]{:S(2)}, u32[]{:S(2)}) collective-permute-start(f32[24,128]{1,0:T(8,128)S(1)} %get-tuple-element.43), channel_id=1, source_target_pairs={{0,31},{1,32},{2,33},{3,34},{4,35},{5,36},{6,37},{7,38},{8,39},{9,... | collective-permute-start | bytes 36872 | tf_op jit(solution)/shard_map/ppermute | solution.py:335
  34.2 3.3 %copy-start.1 = (f32[160,128]{1,0:T(8,128)}, f32[160,128]{1,0:T(8,128)S(1)}, u32[]{:S(2)}) copy-start(f32[160,128]{1,0:T(8,128)S(1)} %pad_maximum_fusion.r_0_) | copy-start | bytes 245764
  34.2 3.2 %collective-permute-start.7 = (f32[160,128]{1,0:T(8,128)S(1)}, f32[160,128]{1,0:T(8,128)S(1)}, u32[]{:S(2)}, u32[]{:S(2)}) collective-permute-start(f32[160,128]{1,0:T(8,128)S(1)} %pad_maximum_fusion.r_0_), channel_id=1, source_target_pairs={{0,64},{64,0},{1,65},{65,1},{2,66},{66,2},{3,67},{67,3},{4,68},{68... | collective-permute-start | bytes 245768 | tf_op jit(solution)/shard_map/ppermute | solution.py:341
  37.5 0.6 copy-start.3
  47.8 1.6 %collective-permute-start.8 = (f32[256,128]{1,0:T(8,128)}, f32[256,128]{1,0:T(8,128)S(1)}, u32[]{:S(2)}, u32[]{:S(2)}) collective-permute-start(f32[256,128]{1,0:T(8,128)} %get-tuple-element.36), channel_id=1, source_target_pairs={{0,64},{64,0},{1,65},{65,1},{2,66},{66,2},{3,67},{67,3},{4,68},{68... | collective-permute-start | bytes 393224 | tf_op jit(solution)/shard_map/ppermute | solution.py:314
  50.3 9.0 %collective-permute-start.10 = (f32[64,128]{1,0:T(8,128)S(1)}, f32[64,128]{1,0:T(8,128)S(1)}, u32[]{:S(2)}, u32[]{:S(2)}) collective-permute-start(f32[64,128]{1,0:T(8,128)S(1)} %get-tuple-element.50), channel_id=1, source_target_pairs={{64,66},{65,67},{66,68},{67,69},{68,70},{69,71},{70,72},{71,73},{7... | collective-permute-start | bytes 98312 | tf_op jit(solution)/shard_map/ppermute | solution.py:335
  51.8 11.0 %collective-permute-start.11 = (f32[64,128]{1,0:T(8,128)S(1)}, f32[64,128]{1,0:T(8,128)S(1)}, u32[]{:S(2)}, u32[]{:S(2)}) collective-permute-start(f32[64,128]{1,0:T(8,128)S(1)} %get-tuple-element.51), channel_id=1, source_target_pairs={{64,65},{65,66},{66,67},{67,68},{68,69},{69,70},{70,71},{71,72},{7... | collective-permute-start | bytes 98312 | tf_op jit(solution)/shard_map/ppermute | solution.py:335
  54.2 8.6 %collective-permute-start.9 = (f32[64,128]{1,0:T(8,128)S(1)}, f32[64,128]{1,0:T(8,128)S(1)}, u32[]{:S(2)}, u32[]{:S(2)}) collective-permute-start(f32[64,128]{1,0:T(8,128)S(1)} %get-tuple-element.52), channel_id=1, source_target_pairs={{64,67},{65,68},{66,69},{67,70},{68,71},{69,72},{70,73},{71,74},{7... | collective-permute-start | bytes 98312 | tf_op jit(solution)/shard_map/ppermute | solution.py:335
  56.6 6.1 %collective-permute-start.12 = (f32[64,128]{1,0:T(8,128)S(1)}, f32[64,128]{1,0:T(8,128)S(1)}, u32[]{:S(2)}, u32[]{:S(2)}) collective-permute-start(f32[64,128]{1,0:T(8,128)S(1)} %pad_select_fusion.1), channel_id=1, source_target_pairs={{64,96},{65,97},{66,98},{67,99},{68,100},{69,101},{70,102},{71,103... | collective-permute-start | bytes 98312 | tf_op jit(solution)/shard_map/ppermute | solution.py:335
  57.6 5.9 %collective-permute-start.14 = (f32[32,128]{1,0:T(8,128)S(1)}, f32[32,128]{1,0:T(8,128)S(1)}, u32[]{:S(2)}, u32[]{:S(2)}) collective-permute-start(f32[32,128]{1,0:T(8,128)S(1)} %broadcast_select_fusion), channel_id=1, source_target_pairs={{64,68},{65,69},{66,70},{67,71},{68,72},{69,73},{70,74},{71,75},{7... | collective-permute-start | bytes 49160 | tf_op jit(solution)/shard_map/ppermute | solution.py:335
  59.3 5.3 %collective-permute-start.13 = (f32[32,128]{1,0:T(8,128)S(1)}, f32[32,128]{1,0:T(8,128)S(1)}, u32[]{:S(2)}, u32[]{:S(2)}) collective-permute-start(f32[32,128]{1,0:T(8,128)S(1)} %get-tuple-element.48), channel_id=1, source_target_pairs={{64,95},{65,96},{66,97},{67,98},{68,99},{69,100},{70,101},{71,102}... | collective-permute-start | bytes 49160 | tf_op jit(solution)/shard_map/ppermute | solution.py:335
  64.6 4.0 %copy-start.2 = (f32[64,128]{1,0:T(8,128)}, f32[64,128]{1,0:T(8,128)S(1)}, u32[]{:S(2)}) copy-start(f32[64,128]{1,0:T(8,128)S(1)} %pad_maximum_fusion.1.here) | copy-start | bytes 98308
  64.6 4.0 %collective-permute-start.15 = (f32[64,128]{1,0:T(8,128)S(1)}, f32[64,128]{1,0:T(8,128)S(1)}, u32[]{:S(2)}, u32[]{:S(2)}) collective-permute-start(f32[64,128]{1,0:T(8,128)S(1)} %pad_maximum_fusion.1.here), channel_id=1, source_target_pairs={{0,64},{64,0},{1,65},{65,1},{2,66},{66,2},{3,67},{67,3},{4,68},{68... | collective-permute-start | bytes 98312 | tf_op jit(solution)/shard_map/ppermute | solution.py:341
  68.6 0.6 copy-start.4

commit v3 on v2

--- a/solution.py
+++ b/solution.py
@@ -17,7 +17,9 @@
 SURF_HALO = (0, 1, 2, 3)
 LAND, COEF, LINK, TABLE = 8, 9, 21, 27
 GROUP = 8
-VMEM_BYTES = 56 * 1024 * 1024
+SEND_VMEM = 40 * 1024 * 1024
+SEA_VMEM = 16 * 1024 * 1024
+AHEAD = 3
 
 
 def offsets_of(count):
@@ -89,12 +91,23 @@
     return [r * ocean_frac for r in rows]
 
 
-def start_tiles(tiles, weights, sems):
-    for i in range(weights.shape[0]):
-        pltpu.make_async_copy(tiles.at[0, 0, i], weights.at[i], sems.at[i]).start()
-
-
-def run_tiles(fields, tiles, weights, sems, src, dst, table, sums):
+def tile_copy(tiles, weights, sems, i):
+    return pltpu.make_async_copy(tiles.at[0, 0, i], weights.at[i], sems.at[i])
+
+
+def own_targets(plane, chosen, dst, sem):
+    offsets, slots, count = plane.shape
+    me = lax.axis_index("blk")
+    pick = (lax.broadcasted_iota(jnp.int32, (BLK, count), 1) == me).astype(jnp.float32)
+    every = plane[...].astype(jnp.float32).reshape(offsets * slots, count)
+    row = lax.dot_general(pick, every, (((1,), (1,)), ((), ())), preferred_element_type=jnp.float32)
+    chosen[...] = row.astype(jnp.int32)
+    copy = pltpu.make_async_copy(chosen, dst, sem)
+    copy.start()
+    return copy
+
+
+def run_tiles(fields, weights, src, dst, table, sums, arrive=None):
     rows = len(fields) * BLK
     block = lax.broadcasted_iota(jnp.int32, (rows, TILE), 0) & (BLK - 1)
     for s in range(BLK):
@@ -105,12 +118,13 @@
     slots = weights.shape[1]
 
     def one_offset(i, carry):
-        pltpu.make_async_copy(tiles.at[0, 0, i], weights.at[i], sems.at[i]).wait()
+        if arrive is not None:
+            arrive(i)
         total = jnp.zeros((rows, TILE), jnp.float32)
         for first in range(0, slots, GROUP):
             left = []
             for j in range(first, first + GROUP):
-                target = dst[i, j]
+                target = dst[0, i * slots + j]
                 left.append(table[src[i, j] * (BLK + 1) + jnp.where(target < 0, BLK, target)])
             right = [weights[i, j] for j in range(first, first + GROUP)]
             total = total + lax.dot_general(
@@ -176,14 +190,17 @@
 
 
 def send_kernel(count, state, links, coef, land, tile_src, targets, tiles, *refs):
-    outs, (handed, low, own) = refs[:7], refs[7:10]
-    (weights, table, sums, src, dst, v_state, v_links, v_coef, v_land, work, wsems, sems) = refs[10:]
+    outs, (handed, low, own, weights) = refs[:7], refs[7:11]
+    (table, sums, src, plane, chosen, dst, v_state, v_links, v_coef, v_land, work, wsems, sems) = refs[11:]
     section = lax.axis_index("sec")
 
     @pl.when(section == 0)
     def _():
-        copies = fetch([(state.at[0], v_state), (land, v_land), (tile_src.at[0, 0], src), (targets.at[0], dst)], sems)
-        start_tiles(tiles, weights, wsems)
+        copies = fetch([(state.at[0], v_state), (land, v_land), (tile_src.at[0, 0], src), (targets.at[0], plane)], sems)
+        for i in range(AHEAD):
+            tile_copy(tiles, weights, wsems, i).start()
+        copies[3].wait()
+        chosen_in = own_targets(plane, chosen, dst, sems.at[3])
         copies[0].wait()
         copies[1].wait()
         lay_out(lambda c, at: v_state[c : c + 1, at], BLK, work, 0)
@@ -191,13 +208,24 @@
         channels = [work[c * BLK : (c + 1) * BLK] for c in range(LAND + 1)]
         fields = compute_fluxes(channels[:LAND], channels[LAND])
         copies[2].wait()
-        copies[3].wait()
-        run_tiles(fields, tiles, weights, wsems, src, dst, table, sums)
+        chosen_in.wait()
+
+        def arrive(i):
+            @pl.when(i + AHEAD < weights.shape[0])
+            def _():
+                tile_copy(tiles, weights, wsems, i + AHEAD).start()
+
+            tile_copy(tiles, weights, wsems, i).wait()
+
+        run_tiles(fields, weights, src, dst, table, sums, arrive)
         write_messages(sums, outs, handed, count, FLUX * BLK, FLUX_HALO, 2)
 
     @pl.when(section == 1)
     def _():
         copies = fetch([(state.at[0], v_state), (land, v_land), (links, v_links), (coef, v_coef)], sems)
+        filled = [tile_copy(tiles, weights, wsems, i) for i in range(weights.shape[0])]
+        for c in filled:
+            c.start()
         outs[0][...] = jnp.zeros_like(outs[0])
         for c in copies:
             c.wait()
@@ -206,11 +234,13 @@
         for c in range(TABLE):
             low[2 * c : 2 * c + 2] = own[c * BLK : c * BLK + 2]
             handed[2 * c : 2 * c + 2] = own[c * BLK + 6 : c * BLK + 8]
-
-
-def sea_kernel(count, here, there, own_h, links, coef, land, tile_src, targets, tiles, *refs):
+        for c in filled:
+            c.wait()
+
+
+def sea_kernel(count, here, there, own, weights, links, coef, land, tile_src, targets, *refs):
     outs, (handed, keep) = refs[:7], refs[7:9]
-    (weights, table, sums, src, dst, v_links, v_coef, v_land, own, v_here, v_there, edge, wsems, sems) = refs[9:]
+    (table, sums, src, plane, chosen, dst, v_links, v_coef, v_land, edge, sems) = refs[9:]
     section = lax.axis_index("sec")
 
     @pl.when(section == 0)
@@ -223,19 +253,17 @@
 
     @pl.when(section == 1)
     def _():
-        copies = fetch(
-            [(here, v_here), (there, v_there), (own_h, own), (tile_src.at[0, 0], src), (targets.at[1], dst)], sems
-        )
-        start_tiles(tiles, weights, wsems)
+        copies = fetch([(tile_src.at[0, 0], src), (targets.at[1], plane)], sems)
         edge[...] = jnp.zeros_like(edge)
         for c in copies:
             c.wait()
+        chosen_in = own_targets(plane, chosen, dst, sems.at[2])
         rows = FLUX * BLK
         side = rows + len(FLUX_HALO) * BLK
         for c in range(TABLE):
-            edge[c * BLK : c * BLK + 2] = v_here[side + 2 * c : side + 2 * c + 2]
-            edge[c * BLK + 6 : c * BLK + 8] = v_there[side + 2 * c : side + 2 * c + 2]
-        forcing = v_here[0:side] + v_there[0:side]
+            edge[c * BLK : c * BLK + 2] = here[side + 2 * c : side + 2 * c + 2]
+            edge[c * BLK + 6 : c * BLK + 8] = there[side + 2 * c : side + 2 * c + 2]
+        forcing = here[0:side] + there[0:side]
 
         def near(c):
             return own[c * BLK : (c + 1) * BLK]
@@ -275,7 +303,8 @@
         u, v = flow_u[:BLK], flow_v[:BLK]
         for r, field in enumerate([height[:BLK], u, v, new_temp]):
             keep[r * BLK : (r + 1) * BLK] = field
-        run_tiles([new_temp, ice[:BLK], u, v], tiles, weights, wsems, src, dst, table, sums)
+        chosen_in.wait()
+        run_tiles([new_temp, ice[:BLK], u, v], weights, src, dst, table, sums)
         write_messages(sums, outs, handed, count, SURF * BLK, SURF_HALO, 1)
 
 
@@ -348,13 +377,16 @@
     f32, i32 = jnp.float32, jnp.int32
     anywhere = pl.BlockSpec(memory_space=pl.ANY)
     inside = pl.BlockSpec(memory_space=pltpu.VMEM)
-    params = pltpu.CompilerParams(vmem_limit_bytes=VMEM_BYTES)
-    targets = lax.dynamic_index_in_dim(dst_lists, lax.axis_index("blk"), axis=1, keepdims=False)
+    targets = dst_lists.transpose(0, 2, 3, 1)
     links = neighbours.transpose(1, 0, 2)
     coef = coupling_coef.transpose(0, 2, 1, 3)
+    surface_state, links, coef, land, tile_src, targets, tiles = [
+        pltpu.with_memory_space_constraint(x, pltpu.HBM)
+        for x in (surface_state, links, coef, land, tile_src, targets, tiles)
+    ]
 
     def shaped(rows):
-        return jax.ShapeDtypeStruct((rows, TILE), f32)
+        return pltpu.VMEM((rows, TILE), f32)
 
     def shapes_for(rows, halo):
         routes = routes_of(count)
@@ -365,23 +397,25 @@
 
     def remap_scratch(rows):
         return [
-            pltpu.VMEM((recv_count, slots, TILE, TILE), jnp.bfloat16),
             pltpu.VMEM((BLK * (BLK + 1), rows, TILE), jnp.bfloat16),
             pltpu.VMEM((recv_count, rows, TILE), f32),
             pltpu.SMEM((recv_count, slots), i32),
-            pltpu.SMEM((recv_count, slots), i32),
+            pltpu.VMEM((recv_count, slots, count), i32),
+            pltpu.VMEM((BLK, recv_count * slots), i32),
+            pltpu.SMEM((BLK, recv_count * slots), i32),
         ]
 
     cost = pl.CostEstimate(flops=int(2 * tiles.size * 16), bytes_accessed=int(tiles.size * 2), transcendentals=0)
     width = BLK * TILE
     rows, halo = FLUX * BLK, len(FLUX_HALO) * BLK
     shapes = shapes_for(rows, halo)
+    held = pltpu.VMEM((recv_count, slots, TILE, TILE), jnp.bfloat16)
     sent = pl.pallas_call(
         lambda *r: send_kernel(count, *r),
         name="flux_remap",
-        out_shape=shapes + [shaped(SIDE), shaped(TABLE * BLK)],
+        out_shape=shapes + [shaped(SIDE), shaped(TABLE * BLK), held],
         in_specs=[anywhere] * 7,
-        out_specs=[inside] * (len(shapes) + 2),
+        out_specs=[inside] * (len(shapes) + 3),
         scratch_shapes=remap_scratch(rows)
         + [
             pltpu.VMEM((8, width), f32),
@@ -392,10 +426,10 @@
             pltpu.SemaphoreType.DMA((recv_count,)),
             pltpu.SemaphoreType.DMA((4,)),
         ],
-        compiler_params=params,
+        compiler_params=pltpu.CompilerParams(vmem_limit_bytes=SEND_VMEM),
         cost_estimate=cost,
     )(surface_state, links, coef, land, tile_src, targets, tiles)
-    outs, (handed, low, own) = sent[:7], sent[7:]
+    outs, (handed, low, own, weights) = sent[:7], sent[7:]
     here, there = exchange(outs, handed, 0, section, count, rows, halo, low)
 
     rows, halo = SURF * BLK, len(SURF_HALO) * BLK
@@ -404,7 +438,7 @@
         lambda *r: sea_kernel(count, *r),
         name="sea_remap",
         out_shape=shapes + [shaped(19 * BLK)],
-        in_specs=[anywhere] * 9,
+        in_specs=[inside] * 4 + [anywhere] * 5,
         out_specs=[inside] * (len(shapes) + 1),
         scratch_shapes=remap_scratch(rows)
         + [
@@ -412,15 +446,11 @@
             pltpu.VMEM((1, 6, 2, width), f32),
             pltpu.VMEM((1, width), i32),
             pltpu.VMEM((TABLE * BLK, TILE), f32),
-            pltpu.VMEM(here.shape, f32),
-            pltpu.VMEM(here.shape, f32),
-            pltpu.VMEM((TABLE * BLK, TILE), f32),
-            pltpu.SemaphoreType.DMA((recv_count,)),
-            pltpu.SemaphoreType.DMA((5,)),
+            pltpu.SemaphoreType.DMA((3,)),
         ],
-        compiler_params=params,
+        compiler_params=pltpu.CompilerParams(vmem_limit_bytes=SEA_VMEM),
         cost_estimate=cost,
-    )(here, there, own, links, coef, land, tile_src, targets, tiles)
+    )(here, there, own, weights, links, coef, land, tile_src, targets)
     outs, (handed, keep) = sent[:7], sent[7:]
     here, there = exchange(outs, handed, 1, section, count, rows, halo)
 

time: 71.3 us -> 70 us (0.982)
  starting transfers between devices: 38.5 us -> 29.7 us
  local copies, waits for them, and re-layouts: 3.17 us -> 10.3 us
  waiting for transfers between devices: 10.3 us -> 15.9 us
  other arithmetic: 5.51 us -> 0.14 us
    unnamed x11 -> x10, local copies, waits for them, and re-layouts: 3 us -> 10.3 us
    ppermute x12, waiting for transfers between devices: 5.69 us -> 11.4 us  [exchange(): got.append(lax.ppermute(jnp.where(mine, own, other), AXES, pairs))]
    ppermute x2, starting transfers between devices: 9.35 us -> 5.1 us  [exchange(): crossed = lax.ppermute(handed, 'sec', swap)]
    select_n x9, other arithmetic: 3.88 us -> 0.07 us  [exchange(): got.append(lax.ppermute(jnp.where(mine, own, other), AXES, pairs))]
    ppermute x12, starting transfers between devices: 23.7 us -> 20.8 us  [exchange(): got.append(lax.ppermute(jnp.where(mine, own, other), AXES, pairs))]
    pallas_call x1, Pallas kernels: 1.89 us -> 4.78 us  [body(): pl.pallas_call(lambda *r: send_kernel(count, *r), name='flux_remap', out_...]
    pallas_call x1, Pallas kernels: 9.73 us -> 7.27 us  [body(): pl.pallas_call(lambda *r: sea_kernel(count, *r), name='sea_remap', out_sh...]
    ppermute x2, starting transfers between devices: 5.42 us -> 3.84 us  [exchange(): return (here, lax.ppermute(here, 'sec', swap))]
  transfers between devices with their start and end apart: 16 -> 16, of which waited for: 9 -> 12; matrix products, arithmetic and copies ran while one was open for 5% -> 0% of each run, Pallas kernels for 0% -> 0%
where the time goes in v3:
time: 70 us; the launch traced here: 69.8 us
  starting transfers between devices  29.7 us (42%)
  waiting for transfers between devices  15.9 us (23%)
  Pallas kernels  13.6 us (19%)
  local copies, waits for them, and re-layouts  10.3 us (15%)
    ppermute x12, starting transfers between devices, exchange(): got.append(lax.ppermute(jnp.where(mine, own, other), AXES, pairs))  20.8 us
    ppermute x12, waiting for transfers between devices, exchange(): got.append(lax.ppermute(jnp.where(mine, own, other), AXES, pairs))  11.4 us
    unnamed x10, local copies, waits for them, and re-layouts  10.3 us
    pallas_call x1, Pallas kernels, body(): pl.pallas_call(lambda *r: sea_kernel(count, *r), name='sea_remap', out_sh...  7.27 us
    ppermute x2, starting transfers between devices, exchange(): crossed = lax.ppermute(handed, 'sec', swap)  5.1 us
    pallas_call x1, Pallas kernels, body(): pl.pallas_call(lambda *r: send_kernel(count, *r), name='flux_remap', out_...  4.78 us
    ppermute x2, starting transfers between devices, exchange(): return (here, lax.ppermute(here, 'sec', swap))  3.84 us
    ppermute x2, waiting for transfers between devices, exchange(): crossed = lax.ppermute(handed, 'sec', swap)  2.4 us
  transfers between devices with their start and end apart: 16, of which 12 were waited for; matrix products, arithmetic and copies ran while one was open for 0% of the time, Pallas kernels for 0%

profile of v3, /device:TPU:1, one launch (start us, length us, event | category | flops | bytes accessed | tf_op | source)
XLA Modules:
  0.0 69.8 jit_solution(15007118296314689561)
XLA Ops:
  0.0 4.8 %flux_remap.1 = (f32[104,128]{1,0:T(8,128)S(1)}, f32[104,128]{1,0:T(8,128)S(1)}, f32[104,128]{1,0:T(8,128)S(1)}, f32[104,128]{1,0:T(8,128)S(1)}, f32[104,128]{1,...) custom-call(f32[1,8,1024]{2,1,0:T(8,128)} %r_0_.1, ...), custom_call_target="tpu_custom_call" | custom-call | flops 201326592 | bytes 12582912 | tf_op jit(solution)/shard_map/flux_remap/pallas_call | solution.py:413
  4.8 0.0 copy-start
  4.8 4.5 %copy-done = bf16[8,48,128,128]{3,2,1,0:T(8,128)(2,1)} copy-done((bf16[8,48,128,128]{3,2,1,0:T(8,128)(2,1)}, bf16[8,48,128,128]{3,2,1,0:T(8,128)(2,1)S(1)}, u32[]{:S(2)}) %copy-start) | copy-done | bytes 12582936
  9.3 5.1 %collective-permute-start = (f32[360,128]{1,0:T(8,128)S(1)}, f32[360,128]{1,0:T(8,128)S(1)}, u32[]{:S(2)}, u32[]{:S(2)}) collective-permute-start(f32[360,128]{1,0:T(8,128)S(1)} %get-tuple-element.27), channel_id=1, source_target_pairs={{0,64},{64,0},{1,65},{65,1},{2,66},{66,2},{3,67},{67,3},{4,68},{68... | collective-permute-start | bytes 552968 | tf_op jit(solution)/shard_map/ppermute | solution.py:343
  14.4 1.1 %collective-permute-done = f32[360,128]{1,0:T(8,128)S(1)} collective-permute-done((f32[360,128]{1,0:T(8,128)S(1)}, f32[360,128]{1,0:T(8,128)S(1)}, u32[]{:S(2)}, u32[]{:S(2)}) %collective-permute-start) | collective-permute-done | bytes 184352 | tf_op jit(solution)/shard_map/ppermute | solution.py:343
  15.5 8.6 %collective-permute-start.3 = (f32[160,128]{1,0:T(8,128)S(1)}, f32[160,128]{1,0:T(8,128)S(1)}, u32[]{:S(2)}, u32[]{:S(2)}) collective-permute-start(f32[160,128]{1,0:T(8,128)S(1)} %maximum_select_fusion), channel_id=1, source_target_pairs={{0,1},{1,2},{2,3},{3,4},{4,5},{5,6},{6,7},{7,8},{8,9},{9,10},{10,1... | collective-permute-start | bytes 245768 | tf_op jit(solution)/shard_map/ppermute | solution.py:364
  24.1 0.5 collective-permute-start.4
  24.6 0.0 collective-permute-start.1
  24.6 1.2 %collective-permute-start.2 = (f32[104,128]{1,0:T(8,128)S(1)}, f32[104,128]{1,0:T(8,128)S(1)}, u32[]{:S(2)}, u32[]{:S(2)}) collective-permute-start(f32[104,128]{1,0:T(8,128)S(1)} %get-tuple-element.47), channel_id=1, source_target_pairs={{0,2},{1,3},{2,4},{3,5},{4,6},{5,7},{6,8},{7,9},{8,10},{9,11},{10,... | collective-permute-start | bytes 159752 | tf_op jit(solution)/shard_map/ppermute | solution.py:364
  25.8 1.3 %collective-permute-start.6 = (f32[24,128]{1,0:T(8,128)S(1)}, f32[24,128]{1,0:T(8,128)S(1)}, u32[]{:S(2)}, u32[]{:S(2)}) collective-permute-start(f32[24,128]{1,0:T(8,128)S(1)} %broadcast_select_fusion.1), channel_id=1, source_target_pairs={{0,4},{1,5},{2,6},{3,7},{4,8},{5,9},{6,10},{7,11},{8,12},{9,13},{1... | collective-permute-start | bytes 36872 | tf_op jit(solution)/shard_map/ppermute | solution.py:364
  27.1 0.3 collective-permute-done.4
  27.4 1.9 %collective-permute-start.5 = (f32[24,128]{1,0:T(8,128)S(1)}, f32[24,128]{1,0:T(8,128)S(1)}, u32[]{:S(2)}, u32[]{:S(2)}) collective-permute-start(f32[24,128]{1,0:T(8,128)S(1)} %get-tuple-element.45), channel_id=1, source_target_pairs={{0,31},{1,32},{2,33},{3,34},{4,35},{5,36},{6,37},{7,38},{8,39},{9,... | collective-permute-start | bytes 36872 | tf_op jit(solution)/shard_map/ppermute | solution.py:364
  29.3 0.1 collective-permute-done.1
  29.4 0.0 collective-permute-done.2
  29.4 0.0 collective-permute-done.3
  29.4 2.5 %collective-permute-done.6 = f32[24,128]{1,0:T(8,128)S(1)} collective-permute-done((f32[24,128]{1,0:T(8,128)S(1)}, f32[24,128]{1,0:T(8,128)S(1)}, u32[]{:S(2)}, u32[]{:S(2)}) %collective-permute-start.6) | collective-permute-done | bytes 12320 | tf_op jit(solution)/shard_map/ppermute | solution.py:364
  32.0 2.2 %collective-permute-done.5 = f32[24,128]{1,0:T(8,128)S(1)} collective-permute-done((f32[24,128]{1,0:T(8,128)S(1)}, f32[24,128]{1,0:T(8,128)S(1)}, u32[]{:S(2)}, u32[]{:S(2)}) %collective-permute-start.5) | collective-permute-done | bytes 12320 | tf_op jit(solution)/shard_map/ppermute | solution.py:364
  34.2 0.1 collective-permute-start.7
  34.3 1.3 %collective-permute-done.7.r_1_ = f32[160,128]{1,0:T(8,128)S(1)} collective-permute-done((f32[160,128]{1,0:T(8,128)S(1)}, f32[160,128]{1,0:T(8,128)S(1)}, u32[]{:S(2)}, u32[]{:S(2)}) %collective-permute-start.7) | collective-permute-done | bytes 81952 | tf_op jit(solution)/shard_map/ppermute | solution.py:370
  35.6 0.0 copy-start.1
  35.6 4.6 %copy-done.1 = bf16[8,48,128,128]{3,2,1,0:T(8,128)(2,1)S(1)} copy-done((bf16[8,48,128,128]{3,2,1,0:T(8,128)(2,1)S(1)}, bf16[8,48,128,128]{3,2,1,0:T(8,128)(2,1)}, u32[]{:S(2)}) %copy-start.1) | copy-done | bytes 12582936
  40.1 7.3 %sea_remap.1 = (f32[64,128]{1,0:T(8,128)S(1)}, f32[64,128]{1,0:T(8,128)S(1)}, f32[64,128]{1,0:T(8,128)S(1)}, f32[64,128]{1,0:T(8,128)S(1)}, f32[64,128]{1,0:T(8,...) custom-call(f32[160,128]{1,0:T(8,128)S(1)} %pad_maximum_fusion.r_0_, ...), custom_call_target="tpu_custom_call" | custom-call | flops 201326592 | bytes 12582912 | tf_op jit(solution)/shard_map/sea_remap/pallas_call | solution.py:437
  47.4 0.0 copy-start.2
  47.4 0.6 copy-done.2
  48.0 0.0 collective-permute-start.8
  48.0 1.3 %collective-permute-done.8 = f32[256,128]{1,0:T(8,128)S(1)} collective-permute-done((f32[256,128]{1,0:T(8,128)S(1)}, f32[256,128]{1,0:T(8,128)S(1)}, u32[]{:S(2)}, u32[]{:S(2)}) %collective-permute-start.8) | collective-permute-done | bytes 131104 | tf_op jit(solution)/shard_map/ppermute | solution.py:343
  49.4 0.7 collective-permute-start.10
  50.1 2.4 %collective-permute-start.11 = (f32[64,128]{1,0:T(8,128)S(1)}, f32[64,128]{1,0:T(8,128)S(1)}, u32[]{:S(2)}, u32[]{:S(2)}) collective-permute-start(f32[64,128]{1,0:T(8,128)S(1)} %get-tuple-element.53), channel_id=1, source_target_pairs={{64,65},{65,66},{66,67},{67,68},{68,69},{69,70},{70,71},{71,72},{7... | collective-permute-start | bytes 98312 | tf_op jit(solution)/shard_map/ppermute | solution.py:364
  52.5 1.0 %collective-permute-start.9 = (f32[64,128]{1,0:T(8,128)S(1)}, f32[64,128]{1,0:T(8,128)S(1)}, u32[]{:S(2)}, u32[]{:S(2)}) collective-permute-start(f32[64,128]{1,0:T(8,128)S(1)} %get-tuple-element.54), channel_id=1, source_target_pairs={{64,67},{65,68},{66,69},{67,70},{68,71},{69,72},{70,73},{71,74},{7... | collective-permute-start | bytes 98312 | tf_op jit(solution)/shard_map/ppermute | solution.py:364
  53.5 1.0 %collective-permute-start.12 = (f32[64,128]{1,0:T(8,128)S(1)}, f32[64,128]{1,0:T(8,128)S(1)}, u32[]{:S(2)}, u32[]{:S(2)}) collective-permute-start(f32[64,128]{1,0:T(8,128)S(1)} %pad_select_fusion.1), channel_id=1, source_target_pairs={{64,96},{65,97},{66,98},{67,99},{68,100},{69,101},{70,102},{71,103... | collective-permute-start | bytes 98312 | tf_op jit(solution)/shard_map/ppermute | solution.py:364
  54.5 1.3 %collective-permute-start.14 = (f32[32,128]{1,0:T(8,128)S(1)}, f32[32,128]{1,0:T(8,128)S(1)}, u32[]{:S(2)}, u32[]{:S(2)}) collective-permute-start(f32[32,128]{1,0:T(8,128)S(1)} %broadcast_select_fusion), channel_id=1, source_target_pairs={{64,68},{65,69},{66,70},{67,71},{68,72},{69,73},{70,74},{71,75},{7... | collective-permute-start | bytes 49160 | tf_op jit(solution)/shard_map/ppermute | solution.py:364
  55.8 2.2 %collective-permute-done.10 = f32[64,128]{1,0:T(8,128)S(1)} collective-permute-done((f32[64,128]{1,0:T(8,128)S(1)}, f32[64,128]{1,0:T(8,128)S(1)}, u32[]{:S(2)}, u32[]{:S(2)}) %collective-permute-start.10) | collective-permute-done | bytes 32800 | tf_op jit(solution)/shard_map/ppermute | solution.py:364
  58.0 0.9 %collective-permute-start.13 = (f32[32,128]{1,0:T(8,128)S(1)}, f32[32,128]{1,0:T(8,128)S(1)}, u32[]{:S(2)}, u32[]{:S(2)}) collective-permute-start(f32[32,128]{1,0:T(8,128)S(1)} %get-tuple-element.50), channel_id=1, source_target_pairs={{64,95},{65,96},{66,97},{67,98},{68,99},{69,100},{70,101},{71,102}... | collective-permute-start | bytes 49160 | tf_op jit(solution)/shard_map/ppermute | solution.py:364
  59.0 0.0 collective-permute-done.11
  59.0 0.5 collective-permute-done.9
  59.5 0.0 collective-permute-done.12
  59.5 0.9 %collective-permute-done.14 = f32[32,128]{1,0:T(8,128)S(1)} collective-permute-done((f32[32,128]{1,0:T(8,128)S(1)}, f32[32,128]{1,0:T(8,128)S(1)}, u32[]{:S(2)}, u32[]{:S(2)}) %collective-permute-start.14) | collective-permute-done | bytes 16416 | tf_op jit(solution)/shard_map/ppermute | solution.py:364
  60.4 2.6 %collective-permute-done.13 = f32[32,128]{1,0:T(8,128)S(1)} collective-permute-done((f32[32,128]{1,0:T(8,128)S(1)}, f32[32,128]{1,0:T(8,128)S(1)}, u32[]{:S(2)}, u32[]{:S(2)}) %collective-permute-start.13) | collective-permute-done | bytes 16416 | tf_op jit(solution)/shard_map/ppermute | solution.py:364
  63.0 0.0 copy-start.3
  63.0 3.8 %collective-permute-start.15 = (f32[64,128]{1,0:T(8,128)S(1)}, f32[64,128]{1,0:T(8,128)S(1)}, u32[]{:S(2)}, u32[]{:S(2)}) collective-permute-start(f32[64,128]{1,0:T(8,128)S(1)} %pad_maximum_fusion.1.here), channel_id=1, source_target_pairs={{0,64},{64,0},{1,65},{65,1},{2,66},{66,2},{3,67},{67,3},{4,68},{68... | collective-permute-start | bytes 98312 | tf_op jit(solution)/shard_map/ppermute | solution.py:370
  66.8 0.9 %collective-permute-done.15.there = f32[64,128]{1,0:T(8,128)S(1)} collective-permute-done((f32[64,128]{1,0:T(8,128)S(1)}, f32[64,128]{1,0:T(8,128)S(1)}, u32[]{:S(2)}, u32[]{:S(2)}) %collective-permute-start.15) | collective-permute-done | bytes 32800 | tf_op jit(solution)/shard_map/ppermute | solution.py:370
  67.6 0.0 copy-start.4
  67.6 0.0 copy-done.3
  67.6 0.6 copy-done.4
  68.3 1.5 %smooth.1 = f32[1,4,1024]{2,1,0:T(4,128)} custom-call(f32[64,128]{1,0:T(8,128)} %copy-done.3, f32[64,128]{1,0:T(8,128)} %copy-done.4, f32[152,128]{1,0:T(8,128)} %copy-done.2), custom_call_target="tpu_custom_call" | custom-call | tf_op jit(solution)/shard_map/smooth/pallas_call | solution.py:457
  (18 shorter events, 0.2 us)
Async XLA Ops:
  4.8 4.5 %copy-start = (bf16[8,48,128,128]{3,2,1,0:T(8,128)(2,1)}, bf16[8,48,128,128]{3,2,1,0:T(8,128)(2,1)S(1)}, u32[]{:S(2)}) copy-start(bf16[8,48,128,128]{3,2,1,0:T(8,128)(2,1)S(1)} %get-tuple-element.35.r_3_) | copy-start | bytes 37748740
  9.3 6.2 %collective-permute-start = (f32[360,128]{1,0:T(8,128)S(1)}, f32[360,128]{1,0:T(8,128)S(1)}, u32[]{:S(2)}, u32[]{:S(2)}) collective-permute-start(f32[360,128]{1,0:T(8,128)S(1)} %get-tuple-element.27), channel_id=1, source_target_pairs={{0,64},{64,0},{1,65},{65,1},{2,66},{66,2},{3,67},{67,3},{4,68},{68... | collective-permute-start | bytes 552968 | tf_op jit(solution)/shard_map/ppermute | solution.py:343
  15.5 13.9 %collective-permute-start.3 = (f32[160,128]{1,0:T(8,128)S(1)}, f32[160,128]{1,0:T(8,128)S(1)}, u32[]{:S(2)}, u32[]{:S(2)}) collective-permute-start(f32[160,128]{1,0:T(8,128)S(1)} %maximum_select_fusion), channel_id=1, source_target_pairs={{0,1},{1,2},{2,3},{3,4},{4,5},{5,6},{6,7},{7,8},{8,9},{9,10},{10,1... | collective-permute-start | bytes 245768 | tf_op jit(solution)/shard_map/ppermute | solution.py:364
  24.1 3.3 %collective-permute-start.4 = (f32[104,128]{1,0:T(8,128)S(1)}, f32[104,128]{1,0:T(8,128)S(1)}, u32[]{:S(2)}, u32[]{:S(2)}) collective-permute-start(f32[104,128]{1,0:T(8,128)S(1)} %pad_select_fusion), channel_id=1, source_target_pairs={{0,32},{1,33},{2,34},{3,35},{4,36},{5,37},{6,38},{7,39},{8,40},{9,... | collective-permute-start | bytes 159752 | tf_op jit(solution)/shard_map/ppermute | solution.py:364
  24.6 4.8 %collective-permute-start.1 = (f32[104,128]{1,0:T(8,128)S(1)}, f32[104,128]{1,0:T(8,128)S(1)}, u32[]{:S(2)}, u32[]{:S(2)}) collective-permute-start(f32[104,128]{1,0:T(8,128)S(1)} %get-tuple-element.49), channel_id=1, source_target_pairs={{0,3},{1,4},{2,5},{3,6},{4,7},{5,8},{6,9},{7,10},{8,11},{9,12},{10... | collective-permute-start | bytes 159752 | tf_op jit(solution)/shard_map/ppermute | solution.py:364
  24.6 4.8 %collective-permute-start.2 = (f32[104,128]{1,0:T(8,128)S(1)}, f32[104,128]{1,0:T(8,128)S(1)}, u32[]{:S(2)}, u32[]{:S(2)}) collective-permute-start(f32[104,128]{1,0:T(8,128)S(1)} %get-tuple-element.47), channel_id=1, source_target_pairs={{0,2},{1,3},{2,4},{3,5},{4,6},{5,7},{6,8},{7,9},{8,10},{9,11},{10,... | collective-permute-start | bytes 159752 | tf_op jit(solution)/shard_map/ppermute | solution.py:364
  25.8 6.2 %collective-permute-start.6 = (f32[24,128]{1,0:T(8,128)S(1)}, f32[24,128]{1,0:T(8,128)S(1)}, u32[]{:S(2)}, u32[]{:S(2)}) collective-permute-start(f32[24,128]{1,0:T(8,128)S(1)} %broadcast_select_fusion.1), channel_id=1, source_target_pairs={{0,4},{1,5},{2,6},{3,7},{4,8},{5,9},{6,10},{7,11},{8,12},{9,13},{1... | collective-permute-start | bytes 36872 | tf_op jit(solution)/shard_map/ppermute | solution.py:364
  27.4 6.8 %collective-permute-start.5 = (f32[24,128]{1,0:T(8,128)S(1)}, f32[24,128]{1,0:T(8,128)S(1)}, u32[]{:S(2)}, u32[]{:S(2)}) collective-permute-start(f32[24,128]{1,0:T(8,128)S(1)} %get-tuple-element.45), channel_id=1, source_target_pairs={{0,31},{1,32},{2,33},{3,34},{4,35},{5,36},{6,37},{7,38},{8,39},{9,... | collective-permute-start | bytes 36872 | tf_op jit(solution)/shard_map/ppermute | solution.py:364
  34.2 1.4 %collective-permute-start.7 = (f32[160,128]{1,0:T(8,128)S(1)}, f32[160,128]{1,0:T(8,128)S(1)}, u32[]{:S(2)}, u32[]{:S(2)}) collective-permute-start(f32[160,128]{1,0:T(8,128)S(1)} %pad_maximum_fusion.r_0_), channel_id=1, source_target_pairs={{0,64},{64,0},{1,65},{65,1},{2,66},{66,2},{3,67},{67,3},{4,68},{68... | collective-permute-start | bytes 245768 | tf_op jit(solution)/shard_map/ppermute | solution.py:370
  35.6 4.6 %copy-start.1 = (bf16[8,48,128,128]{3,2,1,0:T(8,128)(2,1)S(1)}, bf16[8,48,128,128]{3,2,1,0:T(8,128)(2,1)}, u32[]{:S(2)}) copy-start(bf16[8,48,128,128]{3,2,1,0:T(8,128)(2,1)} %copy-done) | copy-start | bytes 37748740
  47.4 0.6 copy-start.2
  48.0 1.3 %collective-permute-start.8 = (f32[256,128]{1,0:T(8,128)S(1)}, f32[256,128]{1,0:T(8,128)S(1)}, u32[]{:S(2)}, u32[]{:S(2)}) collective-permute-start(f32[256,128]{1,0:T(8,128)S(1)} %get-tuple-element.38), channel_id=1, source_target_pairs={{0,64},{64,0},{1,65},{65,1},{2,66},{66,2},{3,67},{67,3},{4,68},{68... | collective-permute-start | bytes 393224 | tf_op jit(solution)/shard_map/ppermute | solution.py:343
  49.4 8.6 %collective-permute-start.10 = (f32[64,128]{1,0:T(8,128)S(1)}, f32[64,128]{1,0:T(8,128)S(1)}, u32[]{:S(2)}, u32[]{:S(2)}) collective-permute-start(f32[64,128]{1,0:T(8,128)S(1)} %get-tuple-element.52), channel_id=1, source_target_pairs={{64,66},{65,67},{66,68},{67,69},{68,70},{69,71},{70,72},{71,73},{7... | collective-permute-start | bytes 98312 | tf_op jit(solution)/shard_map/ppermute | solution.py:364
  50.1 8.9 %collective-permute-start.11 = (f32[64,128]{1,0:T(8,128)S(1)}, f32[64,128]{1,0:T(8,128)S(1)}, u32[]{:S(2)}, u32[]{:S(2)}) collective-permute-start(f32[64,128]{1,0:T(8,128)S(1)} %get-tuple-element.53), channel_id=1, source_target_pairs={{64,65},{65,66},{66,67},{67,68},{68,69},{69,70},{70,71},{71,72},{7... | collective-permute-start | bytes 98312 | tf_op jit(solution)/shard_map/ppermute | solution.py:364
  52.5 7.0 %collective-permute-start.9 = (f32[64,128]{1,0:T(8,128)S(1)}, f32[64,128]{1,0:T(8,128)S(1)}, u32[]{:S(2)}, u32[]{:S(2)}) collective-permute-start(f32[64,128]{1,0:T(8,128)S(1)} %get-tuple-element.54), channel_id=1, source_target_pairs={{64,67},{65,68},{66,69},{67,70},{68,71},{69,72},{70,73},{71,74},{7... | collective-permute-start | bytes 98312 | tf_op jit(solution)/shard_map/ppermute | solution.py:364
  53.5 6.0 %collective-permute-start.12 = (f32[64,128]{1,0:T(8,128)S(1)}, f32[64,128]{1,0:T(8,128)S(1)}, u32[]{:S(2)}, u32[]{:S(2)}) collective-permute-start(f32[64,128]{1,0:T(8,128)S(1)} %pad_select_fusion.1), channel_id=1, source_target_pairs={{64,96},{65,97},{66,98},{67,99},{68,100},{69,101},{70,102},{71,103... | collective-permute-start | bytes 98312 | tf_op jit(solution)/shard_map/ppermute | solution.py:364
  54.5 5.9 %collective-permute-start.14 = (f32[32,128]{1,0:T(8,128)S(1)}, f32[32,128]{1,0:T(8,128)S(1)}, u32[]{:S(2)}, u32[]{:S(2)}) collective-permute-start(f32[32,128]{1,0:T(8,128)S(1)} %broadcast_select_fusion), channel_id=1, source_target_pairs={{64,68},{65,69},{66,70},{67,71},{68,72},{69,73},{70,74},{71,75},{7... | collective-permute-start | bytes 49160 | tf_op jit(solution)/shard_map/ppermute | solution.py:364
  58.0 5.0 %collective-permute-start.13 = (f32[32,128]{1,0:T(8,128)S(1)}, f32[32,128]{1,0:T(8,128)S(1)}, u32[]{:S(2)}, u32[]{:S(2)}) collective-permute-start(f32[32,128]{1,0:T(8,128)S(1)} %get-tuple-element.50), channel_id=1, source_target_pairs={{64,95},{65,96},{66,97},{67,98},{68,99},{69,100},{70,101},{71,102}... | collective-permute-start | bytes 49160 | tf_op jit(solution)/shard_map/ppermute | solution.py:364
  63.0 4.6 %copy-start.3 = (f32[64,128]{1,0:T(8,128)}, f32[64,128]{1,0:T(8,128)S(1)}, u32[]{:S(2)}) copy-start(f32[64,128]{1,0:T(8,128)S(1)} %pad_maximum_fusion.1.here) | copy-start | bytes 98308
  63.0 4.6 %collective-permute-start.15 = (f32[64,128]{1,0:T(8,128)S(1)}, f32[64,128]{1,0:T(8,128)S(1)}, u32[]{:S(2)}, u32[]{:S(2)}) collective-permute-start(f32[64,128]{1,0:T(8,128)S(1)} %pad_maximum_fusion.1.here), channel_id=1, source_target_pairs={{0,64},{64,0},{1,65},{65,1},{2,66},{66,2},{3,67},{67,3},{4,68},{68... | collective-permute-start | bytes 98312 | tf_op jit(solution)/shard_map/ppermute | solution.py:370
  67.6 0.6 copy-start.4

commit v4 on v3

--- a/solution.py
+++ b/solution.py
@@ -17,9 +17,11 @@
 SURF_HALO = (0, 1, 2, 3)
 LAND, COEF, LINK, TABLE = 8, 9, 21, 27
 GROUP = 8
-SEND_VMEM = 40 * 1024 * 1024
-SEA_VMEM = 16 * 1024 * 1024
-AHEAD = 3
+SEND_VMEM = 24 * 1024 * 1024
+SEA_VMEM = 24 * 1024 * 1024
+LAST_VMEM = 4 * 1024 * 1024
+SEND_AHEAD = 3
+SEA_AHEAD = 3
 
 
 def offsets_of(count):
@@ -32,11 +34,12 @@
 
 def routes_of(count):
     half = count // 2
-    return [(3, -3), (2, -2), (1, -1), (half, -4), (half - 1, half + 1), (4, None)]
-
-
-WHOLE = 4
-BESIDE = 2
+    return [(3, -3), (2, -2), (half, half), (1, -1), (half - 1, half + 1), (4, -4)]
+
+
+SMALL = 4
+FAR = 2
+BESIDE = 3
 SIDE = 56
 
 
@@ -107,7 +110,7 @@
     return copy
 
 
-def run_tiles(fields, weights, src, dst, table, sums, arrive=None):
+def run_tiles(fields, tiles, weights, sems, ahead, src, dst, table, sums):
     rows = len(fields) * BLK
     block = lax.broadcasted_iota(jnp.int32, (rows, TILE), 0) & (BLK - 1)
     for s in range(BLK):
@@ -118,8 +121,13 @@
     slots = weights.shape[1]
 
     def one_offset(i, carry):
-        if arrive is not None:
-            arrive(i)
+        if ahead < weights.shape[0]:
+
+            @pl.when(i + ahead < weights.shape[0])
+            def _():
+                tile_copy(tiles, weights, sems, i + ahead).start()
+
+        tile_copy(tiles, weights, sems, i).wait()
         total = jnp.zeros((rows, TILE), jnp.float32)
         for first in range(0, slots, GROUP):
             left = []
@@ -159,9 +167,15 @@
 def write_messages(sums, outs, handed, count, rows, halo, depth):
     slots = slots_of(count)
     base = 0
-    for out, (near, far) in zip(outs[1:], routes_of(count)):
-        write_message(sums, out, 0, near, slots, rows, halo, depth)
-        if far is not None:
+    for n, (near, far) in enumerate(routes_of(count)):
+        if n == FAR:
+            whole = sums[slots[near]]
+            upper = (lax.broadcasted_iota(jnp.int32, (rows, TILE), 0) & (BLK - 1)) >= BLK // 2
+            outs[n + 1][...] = jnp.where(upper, whole, 0.0)
+            handed[base : base + rows] = jnp.where(upper, 0.0, whole)
+            base += rows
+        else:
+            write_message(sums, outs[n + 1], 0, near, slots, rows, halo, depth)
             base = write_message(sums, handed, base, far, slots, rows, halo, depth)
     write_message(sums, outs[0], 0, 0, slots, rows, halo, depth)
 
@@ -190,14 +204,14 @@
 
 
 def send_kernel(count, state, links, coef, land, tile_src, targets, tiles, *refs):
-    outs, (handed, low, own, weights) = refs[:7], refs[7:11]
-    (table, sums, src, plane, chosen, dst, v_state, v_links, v_coef, v_land, work, wsems, sems) = refs[11:]
+    outs, (handed, low, own) = refs[:7], refs[7:10]
+    (weights, table, sums, src, plane, chosen, dst, v_state, v_links, v_coef, v_land, work, wsems, sems) = refs[10:]
     section = lax.axis_index("sec")
 
     @pl.when(section == 0)
     def _():
         copies = fetch([(state.at[0], v_state), (land, v_land), (tile_src.at[0, 0], src), (targets.at[0], plane)], sems)
-        for i in range(AHEAD):
+        for i in range(SEND_AHEAD):
             tile_copy(tiles, weights, wsems, i).start()
         copies[3].wait()
         chosen_in = own_targets(plane, chosen, dst, sems.at[3])
@@ -209,23 +223,12 @@
         fields = compute_fluxes(channels[:LAND], channels[LAND])
         copies[2].wait()
         chosen_in.wait()
-
-        def arrive(i):
-            @pl.when(i + AHEAD < weights.shape[0])
-            def _():
-                tile_copy(tiles, weights, wsems, i + AHEAD).start()
-
-            tile_copy(tiles, weights, wsems, i).wait()
-
-        run_tiles(fields, weights, src, dst, table, sums, arrive)
+        run_tiles(fields, tiles, weights, wsems, SEND_AHEAD, src, dst, table, sums)
         write_messages(sums, outs, handed, count, FLUX * BLK, FLUX_HALO, 2)
 
     @pl.when(section == 1)
     def _():
         copies = fetch([(state.at[0], v_state), (land, v_land), (links, v_links), (coef, v_coef)], sems)
-        filled = [tile_copy(tiles, weights, wsems, i) for i in range(weights.shape[0])]
-        for c in filled:
-            c.start()
         outs[0][...] = jnp.zeros_like(outs[0])
         for c in copies:
             c.wait()
@@ -234,13 +237,11 @@
         for c in range(TABLE):
             low[2 * c : 2 * c + 2] = own[c * BLK : c * BLK + 2]
             handed[2 * c : 2 * c + 2] = own[c * BLK + 6 : c * BLK + 8]
-        for c in filled:
-            c.wait()
-
-
-def sea_kernel(count, here, there, own, weights, links, coef, land, tile_src, targets, *refs):
+
+
+def sea_kernel(count, here, there, own, links, coef, land, tile_src, targets, tiles, *refs):
     outs, (handed, keep) = refs[:7], refs[7:9]
-    (table, sums, src, plane, chosen, dst, v_links, v_coef, v_land, edge, sems) = refs[9:]
+    (weights, table, sums, src, plane, chosen, dst, v_links, v_coef, v_land, edge, wsems, sems) = refs[9:]
     section = lax.axis_index("sec")
 
     @pl.when(section == 0)
@@ -254,6 +255,8 @@
     @pl.when(section == 1)
     def _():
         copies = fetch([(tile_src.at[0, 0], src), (targets.at[1], plane)], sems)
+        for i in range(SEA_AHEAD):
+            tile_copy(tiles, weights, wsems, i).start()
         edge[...] = jnp.zeros_like(edge)
         for c in copies:
             c.wait()
@@ -304,7 +307,7 @@
         for r, field in enumerate([height[:BLK], u, v, new_temp]):
             keep[r * BLK : (r + 1) * BLK] = field
         chosen_in.wait()
-        run_tiles([new_temp, ice[:BLK], u, v], weights, src, dst, table, sums)
+        run_tiles([new_temp, ice[:BLK], u, v], tiles, weights, wsems, SEA_AHEAD, src, dst, table, sums)
         write_messages(sums, outs, handed, count, SURF * BLK, SURF_HALO, 1)
 
 
@@ -338,32 +341,28 @@
             put(r, part(r))
 
 
-def exchange(outs, handed, source, section, count, rows, halo, side=None):
+def exchange(outs, handed, source, section, count, rows, halo, depth, side=None):
     swap = [(0, 1), (1, 0)]
     crossed = lax.ppermute(handed, "sec", swap)
     mine = section == source
-    full = rows + halo
+    full = rows + len(halo) * BLK
     base = 0
     got = []
     for n, (near, far) in enumerate(routes_of(count)):
         own = outs[n + 1]
-        if far is None:
-            other = jnp.zeros_like(own)
-        elif far in slots_of(count) or n >= WHOLE:
-            other = crossed[base : base + own.shape[0]]
-            base += own.shape[0]
-        else:
-            other = jnp.concatenate([jnp.zeros((rows, TILE), jnp.float32), crossed[base : base + halo]])
-            base += halo
-        if side is not None and n == BESIDE:
-            own = jnp.concatenate([own, crossed[:SIDE]])
-            other = jnp.concatenate([other, side])
-        far = near if far is None else far
+        size = own.shape[0]
+        payload = jnp.where(mine, own, crossed[base : base + size])
+        base += size
+        if n == BESIDE:
+            parts = [payload]
+            if side is not None:
+                parts.append(jnp.where(mine, crossed[:SIDE], side))
+            payload = jnp.concatenate(parts)
         pairs = [(source * count + i, source * count + (i + near) % count) for i in range(count)]
         pairs += [((1 - source) * count + i, (1 - source) * count + (i + far) % count) for i in range(count)]
-        got.append(lax.ppermute(jnp.where(mine, own, other), AXES, pairs))
-    total = outs[0] + sum(g[:full] for g in got[:WHOLE])
-    parts = [total[:rows], total[rows:] + sum(got[WHOLE:])]
+        got.append(lax.ppermute(payload, AXES, pairs))
+    total = outs[0] + sum(g[:full] for n, g in enumerate(got[:SMALL]) if n != FAR)
+    parts = [total[:rows] + got[FAR], total[rows:] + sum(got[SMALL:])]
     if side is not None:
         parts.append(got[BESIDE][full:])
     here = jnp.concatenate(parts)
@@ -389,14 +388,12 @@
         return pltpu.VMEM((rows, TILE), f32)
 
     def shapes_for(rows, halo):
-        routes = routes_of(count)
-        slot = slots_of(count)
-        outs = [shaped(rows + halo if near in slot else halo) for near, _ in [(0, 0)] + routes]
-        handed = sum(rows + halo if far in slot else halo for _, far in routes if far is not None)
-        return outs + [shaped(handed)]
+        sizes = [rows if n == FAR else halo if n >= SMALL else rows + halo for n in range(len(routes_of(count)))]
+        return [shaped(size) for size in [rows + halo] + sizes + [sum(sizes)]]
 
     def remap_scratch(rows):
         return [
+            pltpu.VMEM((recv_count, slots, TILE, TILE), jnp.bfloat16),
             pltpu.VMEM((BLK * (BLK + 1), rows, TILE), jnp.bfloat16),
             pltpu.VMEM((recv_count, rows, TILE), f32),
             pltpu.SMEM((recv_count, slots), i32),
@@ -409,13 +406,12 @@
     width = BLK * TILE
     rows, halo = FLUX * BLK, len(FLUX_HALO) * BLK
     shapes = shapes_for(rows, halo)
-    held = pltpu.VMEM((recv_count, slots, TILE, TILE), jnp.bfloat16)
     sent = pl.pallas_call(
         lambda *r: send_kernel(count, *r),
         name="flux_remap",
-        out_shape=shapes + [shaped(SIDE), shaped(TABLE * BLK), held],
+        out_shape=shapes + [shaped(SIDE), shaped(TABLE * BLK)],
         in_specs=[anywhere] * 7,
-        out_specs=[inside] * (len(shapes) + 3),
+        out_specs=[inside] * (len(shapes) + 2),
         scratch_shapes=remap_scratch(rows)
         + [
             pltpu.VMEM((8, width), f32),
@@ -429,8 +425,8 @@
         compiler_params=pltpu.CompilerParams(vmem_limit_bytes=SEND_VMEM),
         cost_estimate=cost,
     )(surface_state, links, coef, land, tile_src, targets, tiles)
-    outs, (handed, low, own, weights) = sent[:7], sent[7:]
-    here, there = exchange(outs, handed, 0, section, count, rows, halo, low)
+    outs, (handed, low, own) = sent[:7], sent[7:]
+    here, there = exchange(outs, handed, 0, section, count, rows, FLUX_HALO, 2, low)
 
     rows, halo = SURF * BLK, len(SURF_HALO) * BLK
     shapes = shapes_for(rows, halo)
@@ -438,7 +434,7 @@
         lambda *r: sea_kernel(count, *r),
         name="sea_remap",
         out_shape=shapes + [shaped(19 * BLK)],
-        in_specs=[inside] * 4 + [anywhere] * 5,
+        in_specs=[inside] * 3 + [anywhere] * 6,
         out_specs=[inside] * (len(shapes) + 1),
         scratch_shapes=remap_scratch(rows)
         + [
@@ -446,13 +442,14 @@
             pltpu.VMEM((1, 6, 2, width), f32),
             pltpu.VMEM((1, width), i32),
             pltpu.VMEM((TABLE * BLK, TILE), f32),
+            pltpu.SemaphoreType.DMA((recv_count,)),
             pltpu.SemaphoreType.DMA((3,)),
         ],
         compiler_params=pltpu.CompilerParams(vmem_limit_bytes=SEA_VMEM),
         cost_estimate=cost,
-    )(here, there, own, weights, links, coef, land, tile_src, targets)
+    )(here, there, own, links, coef, land, tile_src, targets, tiles)
     outs, (handed, keep) = sent[:7], sent[7:]
-    here, there = exchange(outs, handed, 1, section, count, rows, halo)
+    here, there = exchange(outs, handed, 1, section, count, rows, SURF_HALO, 1)
 
     return pl.pallas_call(
         last_kernel,
@@ -460,6 +457,7 @@
         out_shape=jax.ShapeDtypeStruct((1, SURF, width), f32),
         in_specs=[inside] * 3,
         out_specs=inside,
+        compiler_params=pltpu.CompilerParams(vmem_limit_bytes=LAST_VMEM),
     )(here, there, keep)
 
 

time: 70 us -> 58.7 us (0.84)
  local copies, waits for them, and re-layouts: 10.3 us -> 0.01 us
  starting transfers between devices: 29.7 us -> 35.4 us
  Pallas kernels: 13.6 us -> 10 us
  waiting for transfers between devices: 15.9 us -> 13 us
    unnamed x10 -> x0, local copies, waits for them, and re-layouts: 10.3 us -> none
    ppermute x2, starting transfers between devices: 5.1 us -> 8.97 us  [exchange(): crossed = lax.ppermute(handed, 'sec', swap)]
    pallas_call x1, Pallas kernels: 4.78 us -> 1.08 us  [body(): pl.pallas_call(lambda *r: send_kernel(count, *r), name='flux_remap', out_...]
    ppermute x12, waiting for transfers between devices: 11.4 us -> 8.38 us  [exchange(): got.append(lax.ppermute(payload, AXES, pairs))]
    ppermute x12, starting transfers between devices: 20.8 us -> 23.3 us  [exchange(): got.append(lax.ppermute(payload, AXES, pairs))]
    pallas_call x1, Pallas kernels: 7.27 us -> 8.3 us  [body(): pl.pallas_call(lambda *r: sea_kernel(count, *r), name='sea_remap', out_sh...]
    pallas_call x1, Pallas kernels: 1.54 us -> 0.61 us  [body(): pl.pallas_call(last_kernel, name='smooth', out_shape=jax.ShapeDtypeStruct...]
    ppermute x2, starting transfers between devices: 3.84 us -> 3.08 us  [exchange(): return (here, lax.ppermute(here, 'sec', swap))]
  transfers between devices with their start and end apart: 16 -> 16, of which waited for: 12 -> 9; matrix products, arithmetic and copies ran while one was open for 0% -> 0% of each run, Pallas kernels for 0% -> 0%
where the time goes in v4:
time: 58.7 us; the launch traced here: 58.6 us
  starting transfers between devices  35.4 us (60%)
  waiting for transfers between devices  13 us (22%)
  Pallas kernels  10 us (17%)
    ppermute x12, starting transfers between devices, exchange(): got.append(lax.ppermute(payload, AXES, pairs))  23.3 us
    ppermute x2, starting transfers between devices, exchange(): crossed = lax.ppermute(handed, 'sec', swap)  8.97 us
    ppermute x12, waiting for transfers between devices, exchange(): got.append(lax.ppermute(payload, AXES, pairs))  8.38 us
    pallas_call x1, Pallas kernels, body(): pl.pallas_call(lambda *r: sea_kernel(count, *r), name='sea_remap', out_sh...  8.3 us
    ppermute x2, starting transfers between devices, exchange(): return (here, lax.ppermute(here, 'sec', swap))  3.08 us
    ppermute x2, waiting for transfers between devices, exchange(): crossed = lax.ppermute(handed, 'sec', swap)  2.47 us
    ppermute x2, waiting for transfers between devices, exchange(): return (here, lax.ppermute(here, 'sec', swap))  2.12 us
  transfers between devices with their start and end apart: 16, of which 9 were waited for; matrix products, arithmetic and copies ran while one was open for 0% of the time, Pallas kernels for 0%

profile of v4, /device:TPU:1, one launch (start us, length us, event | category | flops | bytes accessed | tf_op | source)
XLA Modules:
  0.0 58.6 jit_solution(4809070605523534234)
XLA Ops:
  0.0 1.1 %flux_remap.1 = (f32[104,128]{1,0:T(8,128)S(1)}, f32[104,128]{1,0:T(8,128)S(1)}, f32[104,128]{1,0:T(8,128)S(1)}, f32[80,128]{1,0:T(8,128)S(1)}, f32[104,128]{1,0...) custom-call(f32[1,8,1024]{2,1,0:T(8,128)} %r_0_.1, ...), custom_call_target="tpu_custom_call" | custom-call | flops 201326592 | bytes 12582912 | tf_op jit(solution)/shard_map/flux_remap/pallas_call | solution.py:409
  1.1 8.9 %collective-permute-start = (f32[440,128]{1,0:T(8,128)S(1)}, f32[440,128]{1,0:T(8,128)S(1)}, u32[]{:S(2)}, u32[]{:S(2)}) collective-permute-start(f32[440,128]{1,0:T(8,128)S(1)} %get-tuple-element.26), channel_id=1, source_target_pairs={{0,64},{64,0},{1,65},{65,1},{2,66},{66,2},{3,67},{67,3},{4,68},{68... | collective-permute-start | bytes 675848 | tf_op jit(solution)/shard_map/ppermute | solution.py:346
  10.0 1.1 %collective-permute-done = f32[440,128]{1,0:T(8,128)S(1)} collective-permute-done((f32[440,128]{1,0:T(8,128)S(1)}, f32[440,128]{1,0:T(8,128)S(1)}, u32[]{:S(2)}, u32[]{:S(2)}) %collective-permute-start) | collective-permute-done | bytes 225312 | tf_op jit(solution)/shard_map/ppermute | solution.py:346
  11.1 8.5 %collective-permute-start.3 = (f32[160,128]{1,0:T(8,128)S(1)}, f32[160,128]{1,0:T(8,128)S(1)}, u32[]{:S(2)}, u32[]{:S(2)}) collective-permute-start(f32[160,128]{1,0:T(8,128)S(1)} %pad_maximum_fusion), channel_id=1, source_target_pairs={{0,1},{1,2},{2,3},{3,4},{4,5},{5,6},{6,7},{7,8},{8,9},{9,10},{10,1... | collective-permute-start | bytes 245768 | tf_op jit(solution)/shard_map/ppermute | solution.py:363
  19.7 0.0 collective-permute-start.1
  19.7 1.5 %collective-permute-start.2 = (f32[104,128]{1,0:T(8,128)S(1)}, f32[104,128]{1,0:T(8,128)S(1)}, u32[]{:S(2)}, u32[]{:S(2)}) collective-permute-start(f32[104,128]{1,0:T(8,128)S(1)} %get-tuple-element.45), channel_id=1, source_target_pairs={{0,2},{1,3},{2,4},{3,5},{4,6},{5,7},{6,8},{7,9},{8,10},{9,11},{10,... | collective-permute-start | bytes 159752 | tf_op jit(solution)/shard_map/ppermute | solution.py:363
  21.2 0.5 collective-permute-start.4
  21.7 4.1 %collective-permute-start.5 = (f32[24,128]{1,0:T(8,128)S(1)}, f32[24,128]{1,0:T(8,128)S(1)}, u32[]{:S(2)}, u32[]{:S(2)}) collective-permute-start(f32[24,128]{1,0:T(8,128)S(1)} %get-tuple-element.44), channel_id=1, source_target_pairs={{0,31},{1,32},{2,33},{3,34},{4,35},{5,36},{6,37},{7,38},{8,39},{9,... | collective-permute-start | bytes 36872 | tf_op jit(solution)/shard_map/ppermute | solution.py:363
  25.8 0.0 collective-permute-done.1
  25.8 0.2 collective-permute-start.6
  26.0 0.0 collective-permute-done.2
  26.0 0.0 collective-permute-done.3
  26.0 0.0 collective-permute-done.4
  26.1 2.4 %collective-permute-done.5 = f32[24,128]{1,0:T(8,128)S(1)} collective-permute-done((f32[24,128]{1,0:T(8,128)S(1)}, f32[24,128]{1,0:T(8,128)S(1)}, u32[]{:S(2)}, u32[]{:S(2)}) %collective-permute-start.5) | collective-permute-done | bytes 12320 | tf_op jit(solution)/shard_map/ppermute | solution.py:363
  28.5 0.0 collective-permute-done.6
  28.5 3.0 %collective-permute-start.7 = (f32[160,128]{1,0:T(8,128)S(1)}, f32[160,128]{1,0:T(8,128)S(1)}, u32[]{:S(2)}, u32[]{:S(2)}) collective-permute-start(f32[160,128]{1,0:T(8,128)S(1)} %pad_maximum_fusion.1.r_0_), channel_id=1, source_target_pairs={{0,64},{64,0},{1,65},{65,1},{2,66},{66,2},{3,67},{67,3},{4,68},{68... | collective-permute-start | bytes 245768 | tf_op jit(solution)/shard_map/ppermute | solution.py:369
  31.5 0.9 %collective-permute-done.7.r_1_ = f32[160,128]{1,0:T(8,128)S(1)} collective-permute-done((f32[160,128]{1,0:T(8,128)S(1)}, f32[160,128]{1,0:T(8,128)S(1)}, u32[]{:S(2)}, u32[]{:S(2)}) %collective-permute-start.7) | collective-permute-done | bytes 81952 | tf_op jit(solution)/shard_map/ppermute | solution.py:369
  32.4 8.3 %sea_remap.1 = (f32[64,128]{1,0:T(8,128)S(1)}, f32[64,128]{1,0:T(8,128)S(1)}, f32[64,128]{1,0:T(8,128)S(1)}, f32[32,128]{1,0:T(8,128)S(1)}, f32[64,128]{1,0:T(8,...) custom-call(f32[160,128]{1,0:T(8,128)S(1)} %pad_maximum_fusion.1.r_0_, ...), custom_call_target="tpu_custom_call" | custom-call | flops 201326592 | bytes 12582912 | tf_op jit(solution)/shard_map/sea_remap/pallas_call | solution.py:433
  40.7 0.1 collective-permute-start.8
  40.8 1.4 %collective-permute-done.8 = f32[288,128]{1,0:T(8,128)S(1)} collective-permute-done((f32[288,128]{1,0:T(8,128)S(1)}, f32[288,128]{1,0:T(8,128)S(1)}, u32[]{:S(2)}, u32[]{:S(2)}) %collective-permute-start.8) | collective-permute-done | bytes 147488 | tf_op jit(solution)/shard_map/ppermute | solution.py:346
  42.2 0.9 %collective-permute-start.10 = (f32[64,128]{1,0:T(8,128)S(1)}, f32[64,128]{1,0:T(8,128)S(1)}, u32[]{:S(2)}, u32[]{:S(2)}) collective-permute-start(f32[64,128]{1,0:T(8,128)S(1)} %get-tuple-element.51), channel_id=1, source_target_pairs={{64,66},{65,67},{66,68},{67,69},{68,70},{69,71},{70,72},{71,73},{7... | collective-permute-start | bytes 98312 | tf_op jit(solution)/shard_map/ppermute | solution.py:363
  43.1 0.0 collective-permute-start.11
  43.1 0.8 %collective-permute-start.9 = (f32[64,128]{1,0:T(8,128)S(1)}, f32[64,128]{1,0:T(8,128)S(1)}, u32[]{:S(2)}, u32[]{:S(2)}) collective-permute-start(f32[64,128]{1,0:T(8,128)S(1)} %get-tuple-element.53), channel_id=1, source_target_pairs={{64,67},{65,68},{66,69},{67,70},{68,71},{69,72},{70,73},{71,74},{7... | collective-permute-start | bytes 98312 | tf_op jit(solution)/shard_map/ppermute | solution.py:363
  43.9 2.1 %collective-permute-start.12 = (f32[32,128]{1,0:T(8,128)S(1)}, f32[32,128]{1,0:T(8,128)S(1)}, u32[]{:S(2)}, u32[]{:S(2)}) collective-permute-start(f32[32,128]{1,0:T(8,128)S(1)} %get-tuple-element.48), channel_id=1, source_target_pairs={{64,96},{65,97},{66,98},{67,99},{68,100},{69,101},{70,102},{71,103... | collective-permute-start | bytes 49160 | tf_op jit(solution)/shard_map/ppermute | solution.py:363
  46.0 4.7 %collective-permute-start.13 = (f32[32,128]{1,0:T(8,128)S(1)}, f32[32,128]{1,0:T(8,128)S(1)}, u32[]{:S(2)}, u32[]{:S(2)}) collective-permute-start(f32[32,128]{1,0:T(8,128)S(1)} %get-tuple-element.50), channel_id=1, source_target_pairs={{64,95},{65,96},{66,97},{67,98},{68,99},{69,100},{70,101},{71,102}... | collective-permute-start | bytes 49160 | tf_op jit(solution)/shard_map/ppermute | solution.py:363
  50.7 0.1 collective-permute-done.10
  50.8 0.0 collective-permute-start.14
  50.8 0.6 collective-permute-done.11
  51.3 0.0 collective-permute-done.9
  51.3 0.0 collective-permute-done.12
  51.3 0.2 collective-permute-done.13
  51.6 5.1 %collective-permute-done.14 = f32[32,128]{1,0:T(8,128)S(1)} collective-permute-done((f32[32,128]{1,0:T(8,128)S(1)}, f32[32,128]{1,0:T(8,128)S(1)}, u32[]{:S(2)}, u32[]{:S(2)}) %collective-permute-start.14) | collective-permute-done | bytes 16416 | tf_op jit(solution)/shard_map/ppermute | solution.py:363
  56.7 0.1 collective-permute-start.15
  56.8 1.2 %collective-permute-done.15.there = f32[64,128]{1,0:T(8,128)S(1)} collective-permute-done((f32[64,128]{1,0:T(8,128)S(1)}, f32[64,128]{1,0:T(8,128)S(1)}, u32[]{:S(2)}, u32[]{:S(2)}) %collective-permute-start.15) | collective-permute-done | bytes 32800 | tf_op jit(solution)/shard_map/ppermute | solution.py:369
  58.0 0.6 %smooth.1 = f32[1,4,1024]{2,1,0:T(4,128)} custom-call(f32[64,128]{1,0:T(8,128)S(1)} %pad_maximum_fusion.2.here, f32[64,128]{1,0:T(8,128)S(1)} %collective-permute-done.15.there, f32[152,128]{1,0:T(8,128)S(1)} %get-tuple-element.42.keep), custom_call_target="tpu_custom_call" | custom-call | tf_op jit(solution)/shard_map/smooth/pallas_call | solution.py:454
  (15 shorter events, 0.1 us)
Async XLA Ops:
  1.1 10.0 %collective-permute-start = (f32[440,128]{1,0:T(8,128)S(1)}, f32[440,128]{1,0:T(8,128)S(1)}, u32[]{:S(2)}, u32[]{:S(2)}) collective-permute-start(f32[440,128]{1,0:T(8,128)S(1)} %get-tuple-element.26), channel_id=1, source_target_pairs={{0,64},{64,0},{1,65},{65,1},{2,66},{66,2},{3,67},{67,3},{4,68},{68... | collective-permute-start | bytes 675848 | tf_op jit(solution)/shard_map/ppermute | solution.py:346
  11.1 14.9 %collective-permute-start.3 = (f32[160,128]{1,0:T(8,128)S(1)}, f32[160,128]{1,0:T(8,128)S(1)}, u32[]{:S(2)}, u32[]{:S(2)}) collective-permute-start(f32[160,128]{1,0:T(8,128)S(1)} %pad_maximum_fusion), channel_id=1, source_target_pairs={{0,1},{1,2},{2,3},{3,4},{4,5},{5,6},{6,7},{7,8},{8,9},{9,10},{10,1... | collective-permute-start | bytes 245768 | tf_op jit(solution)/shard_map/ppermute | solution.py:363
  19.7 6.1 %collective-permute-start.1 = (f32[104,128]{1,0:T(8,128)S(1)}, f32[104,128]{1,0:T(8,128)S(1)}, u32[]{:S(2)}, u32[]{:S(2)}) collective-permute-start(f32[104,128]{1,0:T(8,128)S(1)} %get-tuple-element.47), channel_id=1, source_target_pairs={{0,3},{1,4},{2,5},{3,6},{4,7},{5,8},{6,9},{7,10},{8,11},{9,12},{10... | collective-permute-start | bytes 159752 | tf_op jit(solution)/shard_map/ppermute | solution.py:363
  19.7 6.3 %collective-permute-start.2 = (f32[104,128]{1,0:T(8,128)S(1)}, f32[104,128]{1,0:T(8,128)S(1)}, u32[]{:S(2)}, u32[]{:S(2)}) collective-permute-start(f32[104,128]{1,0:T(8,128)S(1)} %get-tuple-element.45), channel_id=1, source_target_pairs={{0,2},{1,3},{2,4},{3,5},{4,6},{5,7},{6,8},{7,9},{8,10},{9,11},{10,... | collective-permute-start | bytes 159752 | tf_op jit(solution)/shard_map/ppermute | solution.py:363
  21.2 4.9 %collective-permute-start.4 = (f32[80,128]{1,0:T(8,128)S(1)}, f32[80,128]{1,0:T(8,128)S(1)}, u32[]{:S(2)}, u32[]{:S(2)}) collective-permute-start(f32[80,128]{1,0:T(8,128)S(1)} %slice_select_fusion.3), channel_id=1, source_target_pairs={{0,32},{1,33},{2,34},{3,35},{4,36},{5,37},{6,38},{7,39},{8,40},{9,... | collective-permute-start | bytes 122888 | tf_op jit(solution)/shard_map/ppermute | solution.py:363
  21.7 6.8 %collective-permute-start.5 = (f32[24,128]{1,0:T(8,128)S(1)}, f32[24,128]{1,0:T(8,128)S(1)}, u32[]{:S(2)}, u32[]{:S(2)}) collective-permute-start(f32[24,128]{1,0:T(8,128)S(1)} %get-tuple-element.44), channel_id=1, source_target_pairs={{0,31},{1,32},{2,33},{3,34},{4,35},{5,36},{6,37},{7,38},{8,39},{9,... | collective-permute-start | bytes 36872 | tf_op jit(solution)/shard_map/ppermute | solution.py:363
  25.8 2.6 %collective-permute-start.6 = (f32[24,128]{1,0:T(8,128)S(1)}, f32[24,128]{1,0:T(8,128)S(1)}, u32[]{:S(2)}, u32[]{:S(2)}) collective-permute-start(f32[24,128]{1,0:T(8,128)S(1)} %get-tuple-element.43), channel_id=1, source_target_pairs={{0,4},{1,5},{2,6},{3,7},{4,8},{5,9},{6,10},{7,11},{8,12},{9,13},{1... | collective-permute-start | bytes 36872 | tf_op jit(solution)/shard_map/ppermute | solution.py:363
  28.5 3.9 %collective-permute-start.7 = (f32[160,128]{1,0:T(8,128)S(1)}, f32[160,128]{1,0:T(8,128)S(1)}, u32[]{:S(2)}, u32[]{:S(2)}) collective-permute-start(f32[160,128]{1,0:T(8,128)S(1)} %pad_maximum_fusion.1.r_0_), channel_id=1, source_target_pairs={{0,64},{64,0},{1,65},{65,1},{2,66},{66,2},{3,67},{67,3},{4,68},{68... | collective-permute-start | bytes 245768 | tf_op jit(solution)/shard_map/ppermute | solution.py:369
  40.7 1.5 %collective-permute-start.8 = (f32[288,128]{1,0:T(8,128)S(1)}, f32[288,128]{1,0:T(8,128)S(1)}, u32[]{:S(2)}, u32[]{:S(2)}) collective-permute-start(f32[288,128]{1,0:T(8,128)S(1)} %get-tuple-element.36), channel_id=1, source_target_pairs={{0,64},{64,0},{1,65},{65,1},{2,66},{66,2},{3,67},{67,3},{4,68},{68... | collective-permute-start | bytes 442376 | tf_op jit(solution)/shard_map/ppermute | solution.py:346
  42.2 8.6 %collective-permute-start.10 = (f32[64,128]{1,0:T(8,128)S(1)}, f32[64,128]{1,0:T(8,128)S(1)}, u32[]{:S(2)}, u32[]{:S(2)}) collective-permute-start(f32[64,128]{1,0:T(8,128)S(1)} %get-tuple-element.51), channel_id=1, source_target_pairs={{64,66},{65,67},{66,68},{67,69},{68,70},{69,71},{70,72},{71,73},{7... | collective-permute-start | bytes 98312 | tf_op jit(solution)/shard_map/ppermute | solution.py:363
  43.1 8.2 %collective-permute-start.11 = (f32[64,128]{1,0:T(8,128)S(1)}, f32[64,128]{1,0:T(8,128)S(1)}, u32[]{:S(2)}, u32[]{:S(2)}) collective-permute-start(f32[64,128]{1,0:T(8,128)S(1)} %get-tuple-element.52), channel_id=1, source_target_pairs={{64,65},{65,66},{66,67},{67,68},{68,69},{69,70},{70,71},{71,72},{7... | collective-permute-start | bytes 98312 | tf_op jit(solution)/shard_map/ppermute | solution.py:363
  43.1 8.2 %collective-permute-start.9 = (f32[64,128]{1,0:T(8,128)S(1)}, f32[64,128]{1,0:T(8,128)S(1)}, u32[]{:S(2)}, u32[]{:S(2)}) collective-permute-start(f32[64,128]{1,0:T(8,128)S(1)} %get-tuple-element.53), channel_id=1, source_target_pairs={{64,67},{65,68},{66,69},{67,70},{68,71},{69,72},{70,73},{71,74},{7... | collective-permute-start | bytes 98312 | tf_op jit(solution)/shard_map/ppermute | solution.py:363
  43.9 7.4 %collective-permute-start.12 = (f32[32,128]{1,0:T(8,128)S(1)}, f32[32,128]{1,0:T(8,128)S(1)}, u32[]{:S(2)}, u32[]{:S(2)}) collective-permute-start(f32[32,128]{1,0:T(8,128)S(1)} %get-tuple-element.48), channel_id=1, source_target_pairs={{64,96},{65,97},{66,98},{67,99},{68,100},{69,101},{70,102},{71,103... | collective-permute-start | bytes 49160 | tf_op jit(solution)/shard_map/ppermute | solution.py:363
  46.0 5.5 %collective-permute-start.13 = (f32[32,128]{1,0:T(8,128)S(1)}, f32[32,128]{1,0:T(8,128)S(1)}, u32[]{:S(2)}, u32[]{:S(2)}) collective-permute-start(f32[32,128]{1,0:T(8,128)S(1)} %get-tuple-element.50), channel_id=1, source_target_pairs={{64,95},{65,96},{66,97},{67,98},{68,99},{69,100},{70,101},{71,102}... | collective-permute-start | bytes 49160 | tf_op jit(solution)/shard_map/ppermute | solution.py:363
  50.8 5.9 %collective-permute-start.14 = (f32[32,128]{1,0:T(8,128)S(1)}, f32[32,128]{1,0:T(8,128)S(1)}, u32[]{:S(2)}, u32[]{:S(2)}) collective-permute-start(f32[32,128]{1,0:T(8,128)S(1)} %get-tuple-element.49), channel_id=1, source_target_pairs={{64,68},{65,69},{66,70},{67,71},{68,72},{69,73},{70,74},{71,75},{7... | collective-permute-start | bytes 49160 | tf_op jit(solution)/shard_map/ppermute | solution.py:363
  56.7 1.3 %collective-permute-start.15 = (f32[64,128]{1,0:T(8,128)S(1)}, f32[64,128]{1,0:T(8,128)S(1)}, u32[]{:S(2)}, u32[]{:S(2)}) collective-permute-start(f32[64,128]{1,0:T(8,128)S(1)} %pad_maximum_fusion.2.here), channel_id=1, source_target_pairs={{0,64},{64,0},{1,65},{65,1},{2,66},{66,2},{3,67},{67,3},{4,68},{68... | collective-permute-start | bytes 98312 | tf_op jit(solution)/shard_map/ppermute | solution.py:369

commit v5 on v4

--- a/solution.py
+++ b/solution.py
@@ -20,7 +20,8 @@
 SEND_VMEM = 24 * 1024 * 1024
 SEA_VMEM = 24 * 1024 * 1024
 LAST_VMEM = 4 * 1024 * 1024
-SEND_AHEAD = 3
+PAIR = 2
+SEND_AHEAD = 2
 SEA_AHEAD = 3
 
 
@@ -98,6 +99,11 @@
     return pltpu.make_async_copy(tiles.at[0, 0, i], weights.at[i], sems.at[i])
 
 
+def start_pair(tiles, weights, sems, n):
+    for i in range(PAIR):
+        tile_copy(tiles, weights, sems, n * PAIR + i).start()
+
+
 def own_targets(plane, chosen, dst, sem):
     offsets, slots, count = plane.shape
     me = lax.axis_index("blk")
@@ -119,32 +125,37 @@
             table[s * (BLK + 1) + d] = jnp.where(block == d, spread, 0.0).astype(jnp.bfloat16)
         table[s * (BLK + 1) + BLK] = jnp.zeros((rows, TILE), jnp.bfloat16)
     slots = weights.shape[1]
-
-    def one_offset(i, carry):
-        if ahead < weights.shape[0]:
-
-            @pl.when(i + ahead < weights.shape[0])
+    steps = weights.shape[0] // PAIR
+
+    def one_pair(n, carry):
+        if ahead < steps:
+
+            @pl.when(n + ahead < steps)
             def _():
-                tile_copy(tiles, weights, sems, i + ahead).start()
-
-        tile_copy(tiles, weights, sems, i).wait()
-        total = jnp.zeros((rows, TILE), jnp.float32)
-        for first in range(0, slots, GROUP):
-            left = []
-            for j in range(first, first + GROUP):
-                target = dst[0, i * slots + j]
-                left.append(table[src[i, j] * (BLK + 1) + jnp.where(target < 0, BLK, target)])
-            right = [weights[i, j] for j in range(first, first + GROUP)]
-            total = total + lax.dot_general(
-                jnp.concatenate(left, axis=1),
-                jnp.concatenate(right, axis=1),
-                (((1,), (1,)), ((), ())),
-                preferred_element_type=jnp.float32,
-            )
-        sums[i] = total
+                start_pair(tiles, weights, sems, n + ahead)
+
+        for i in range(PAIR):
+            tile_copy(tiles, weights, sems, n * PAIR + i).wait()
+        for i in range(PAIR):
+            i = n * PAIR + i
+            total = None
+            for first in range(0, slots, GROUP):
+                left = [weights[i, j] for j in range(first, first + GROUP)]
+                right = []
+                for j in range(first, first + GROUP):
+                    target = dst[0, i * slots + j]
+                    right.append(table[src[i, j] * (BLK + 1) + jnp.where(target < 0, BLK, target)])
+                part = lax.dot_general(
+                    jnp.concatenate(left, axis=1),
+                    jnp.concatenate(right, axis=1),
+                    (((1,), (1,)), ((), ())),
+                    preferred_element_type=jnp.float32,
+                )
+                total = part if total is None else total + part
+            sums[i] = total.T
         return carry
 
-    lax.fori_loop(0, weights.shape[0], one_offset, 0)
+    lax.fori_loop(0, steps, one_pair, 0)
 
 
 def write_message(sums, out, base, offset, slots, rows, halo, depth):
@@ -211,12 +222,13 @@
     @pl.when(section == 0)
     def _():
         copies = fetch([(state.at[0], v_state), (land, v_land), (tile_src.at[0, 0], src), (targets.at[0], plane)], sems)
-        for i in range(SEND_AHEAD):
-            tile_copy(tiles, weights, wsems, i).start()
+        start_pair(tiles, weights, wsems, 0)
         copies[3].wait()
         chosen_in = own_targets(plane, chosen, dst, sems.at[3])
         copies[0].wait()
         copies[1].wait()
+        for n in range(1, SEND_AHEAD):
+            start_pair(tiles, weights, wsems, n)
         lay_out(lambda c, at: v_state[c : c + 1, at], BLK, work, 0)
         lay_out(lambda c, at: v_land[:, at], 1, work, LAND)
         channels = [work[c * BLK : (c + 1) * BLK] for c in range(LAND + 1)]
@@ -255,12 +267,12 @@
     @pl.when(section == 1)
     def _():
         copies = fetch([(tile_src.at[0, 0], src), (targets.at[1], plane)], sems)
-        for i in range(SEA_AHEAD):
-            tile_copy(tiles, weights, wsems, i).start()
+        start_pair(tiles, weights, wsems, 0)
         edge[...] = jnp.zeros_like(edge)
         for c in copies:
             c.wait()
         chosen_in = own_targets(plane, chosen, dst, sems.at[2])
+        start_pair(tiles, weights, wsems, 1)
         rows = FLUX * BLK
         side = rows + len(FLUX_HALO) * BLK
         for c in range(TABLE):
@@ -302,6 +314,8 @@
             moved = sum(wx * a + wy * b for wx, wy, a, b in zip(grad_wx, grad_wy, moved_u, moved_v))
             height = height - 0.5 * moved + push_h
             flow_u, flow_v = next_u, next_v
+        for n in range(2, SEA_AHEAD):
+            start_pair(tiles, weights, wsems, n)
         new_temp = near(4) + 0.2 * near(LAND) * force(9) / mixed
         u, v = flow_u[:BLK], flow_v[:BLK]
         for r, field in enumerate([height[:BLK], u, v, new_temp]):

time: 58.7 us -> 55.7 us (0.949)
  starting transfers between devices: 35.4 us -> 33.8 us
  Pallas kernels: 10 us -> 8.61 us
    ppermute x2, starting transfers between devices: 8.97 us -> 7.36 us  [exchange(): crossed = lax.ppermute(handed, 'sec', swap)]
    pallas_call x1, Pallas kernels: 8.3 us -> 6.91 us  [body(): pl.pallas_call(lambda *r: sea_kernel(count, *r), name='sea_remap', out_sh...]
where the time goes in v5:
time: 55.7 us; the launch traced here: 55.6 us
  starting transfers between devices  33.8 us (61%)
  waiting for transfers between devices  13 us (23%)
  Pallas kernels  8.61 us (15%)
    ppermute x12, starting transfers between devices, exchange(): got.append(lax.ppermute(payload, AXES, pairs))  23.3 us
    ppermute x12, waiting for transfers between devices, exchange(): got.append(lax.ppermute(payload, AXES, pairs))  8.38 us
    ppermute x2, starting transfers between devices, exchange(): crossed = lax.ppermute(handed, 'sec', swap)  7.36 us
    pallas_call x1, Pallas kernels, body(): pl.pallas_call(lambda *r: sea_kernel(count, *r), name='sea_remap', out_sh...  6.91 us
    ppermute x2, starting transfers between devices, exchange(): return (here, lax.ppermute(here, 'sec', swap))  3.08 us
    ppermute x2, waiting for transfers between devices, exchange(): crossed = lax.ppermute(handed, 'sec', swap)  2.47 us
    ppermute x2, waiting for transfers between devices, exchange(): return (here, lax.ppermute(here, 'sec', swap))  2.12 us
  transfers between devices with their start and end apart: 16, of which 9 were waited for; matrix products, arithmetic and copies ran while one was open for 0% of the time, Pallas kernels for 0%

profile of v5, /device:TPU:1, one launch (start us, length us, event | category | flops | bytes accessed | tf_op | source)
XLA Modules:
  0.0 55.6 jit_solution(5272674898711464173)
XLA Ops:
  0.0 1.1 %flux_remap.1 = (f32[104,128]{1,0:T(8,128)S(1)}, f32[104,128]{1,0:T(8,128)S(1)}, f32[104,128]{1,0:T(8,128)S(1)}, f32[80,128]{1,0:T(8,128)S(1)}, f32[104,128]{1,0...) custom-call(f32[1,8,1024]{2,1,0:T(8,128)} %r_0_.1, ...), custom_call_target="tpu_custom_call" | custom-call | flops 201326592 | bytes 12582912 | tf_op jit(solution)/shard_map/flux_remap/pallas_call | solution.py:423
  1.1 7.3 %collective-permute-start = (f32[440,128]{1,0:T(8,128)S(1)}, f32[440,128]{1,0:T(8,128)S(1)}, u32[]{:S(2)}, u32[]{:S(2)}) collective-permute-start(f32[440,128]{1,0:T(8,128)S(1)} %get-tuple-element.26), channel_id=1, source_target_pairs={{0,64},{64,0},{1,65},{65,1},{2,66},{66,2},{3,67},{67,3},{4,68},{68... | collective-permute-start | bytes 675848 | tf_op jit(solution)/shard_map/ppermute | solution.py:360
  8.4 1.1 %collective-permute-done = f32[440,128]{1,0:T(8,128)S(1)} collective-permute-done((f32[440,128]{1,0:T(8,128)S(1)}, f32[440,128]{1,0:T(8,128)S(1)}, u32[]{:S(2)}, u32[]{:S(2)}) %collective-permute-start) | collective-permute-done | bytes 225312 | tf_op jit(solution)/shard_map/ppermute | solution.py:360
  9.5 8.6 %collective-permute-start.3 = (f32[160,128]{1,0:T(8,128)S(1)}, f32[160,128]{1,0:T(8,128)S(1)}, u32[]{:S(2)}, u32[]{:S(2)}) collective-permute-start(f32[160,128]{1,0:T(8,128)S(1)} %pad_maximum_fusion), channel_id=1, source_target_pairs={{0,1},{1,2},{2,3},{3,4},{4,5},{5,6},{6,7},{7,8},{8,9},{9,10},{10,1... | collective-permute-start | bytes 245768 | tf_op jit(solution)/shard_map/ppermute | solution.py:377
  18.1 0.0 collective-permute-start.1
  18.1 1.5 %collective-permute-start.2 = (f32[104,128]{1,0:T(8,128)S(1)}, f32[104,128]{1,0:T(8,128)S(1)}, u32[]{:S(2)}, u32[]{:S(2)}) collective-permute-start(f32[104,128]{1,0:T(8,128)S(1)} %get-tuple-element.45), channel_id=1, source_target_pairs={{0,2},{1,3},{2,4},{3,5},{4,6},{5,7},{6,8},{7,9},{8,10},{9,11},{10,... | collective-permute-start | bytes 159752 | tf_op jit(solution)/shard_map/ppermute | solution.py:377
  19.6 0.5 collective-permute-start.4
  20.1 4.1 %collective-permute-start.5 = (f32[24,128]{1,0:T(8,128)S(1)}, f32[24,128]{1,0:T(8,128)S(1)}, u32[]{:S(2)}, u32[]{:S(2)}) collective-permute-start(f32[24,128]{1,0:T(8,128)S(1)} %get-tuple-element.44), channel_id=1, source_target_pairs={{0,31},{1,32},{2,33},{3,34},{4,35},{5,36},{6,37},{7,38},{8,39},{9,... | collective-permute-start | bytes 36872 | tf_op jit(solution)/shard_map/ppermute | solution.py:377
  24.2 0.0 collective-permute-done.1
  24.2 0.2 collective-permute-start.6
  24.4 0.0 collective-permute-done.2
  24.4 0.0 collective-permute-done.3
  24.4 0.0 collective-permute-done.4
  24.5 2.4 %collective-permute-done.5 = f32[24,128]{1,0:T(8,128)S(1)} collective-permute-done((f32[24,128]{1,0:T(8,128)S(1)}, f32[24,128]{1,0:T(8,128)S(1)}, u32[]{:S(2)}, u32[]{:S(2)}) %collective-permute-start.5) | collective-permute-done | bytes 12320 | tf_op jit(solution)/shard_map/ppermute | solution.py:377
  26.9 0.0 collective-permute-done.6
  26.9 3.0 %collective-permute-start.7 = (f32[160,128]{1,0:T(8,128)S(1)}, f32[160,128]{1,0:T(8,128)S(1)}, u32[]{:S(2)}, u32[]{:S(2)}) collective-permute-start(f32[160,128]{1,0:T(8,128)S(1)} %pad_maximum_fusion.1.r_0_), channel_id=1, source_target_pairs={{0,64},{64,0},{1,65},{65,1},{2,66},{66,2},{3,67},{67,3},{4,68},{68... | collective-permute-start | bytes 245768 | tf_op jit(solution)/shard_map/ppermute | solution.py:383
  29.9 0.9 %collective-permute-done.7.r_1_ = f32[160,128]{1,0:T(8,128)S(1)} collective-permute-done((f32[160,128]{1,0:T(8,128)S(1)}, f32[160,128]{1,0:T(8,128)S(1)}, u32[]{:S(2)}, u32[]{:S(2)}) %collective-permute-start.7) | collective-permute-done | bytes 81952 | tf_op jit(solution)/shard_map/ppermute | solution.py:383
  30.8 6.9 %sea_remap.1 = (f32[64,128]{1,0:T(8,128)S(1)}, f32[64,128]{1,0:T(8,128)S(1)}, f32[64,128]{1,0:T(8,128)S(1)}, f32[32,128]{1,0:T(8,128)S(1)}, f32[64,128]{1,0:T(8,...) custom-call(f32[160,128]{1,0:T(8,128)S(1)} %pad_maximum_fusion.1.r_0_, ...), custom_call_target="tpu_custom_call" | custom-call | flops 201326592 | bytes 12582912 | tf_op jit(solution)/shard_map/sea_remap/pallas_call | solution.py:447
  37.7 0.1 collective-permute-start.8
  37.8 1.4 %collective-permute-done.8 = f32[288,128]{1,0:T(8,128)S(1)} collective-permute-done((f32[288,128]{1,0:T(8,128)S(1)}, f32[288,128]{1,0:T(8,128)S(1)}, u32[]{:S(2)}, u32[]{:S(2)}) %collective-permute-start.8) | collective-permute-done | bytes 147488 | tf_op jit(solution)/shard_map/ppermute | solution.py:360
  39.2 0.9 %collective-permute-start.10 = (f32[64,128]{1,0:T(8,128)S(1)}, f32[64,128]{1,0:T(8,128)S(1)}, u32[]{:S(2)}, u32[]{:S(2)}) collective-permute-start(f32[64,128]{1,0:T(8,128)S(1)} %get-tuple-element.51), channel_id=1, source_target_pairs={{64,66},{65,67},{66,68},{67,69},{68,70},{69,71},{70,72},{71,73},{7... | collective-permute-start | bytes 98312 | tf_op jit(solution)/shard_map/ppermute | solution.py:377
  40.1 0.0 collective-permute-start.11
  40.1 0.8 %collective-permute-start.9 = (f32[64,128]{1,0:T(8,128)S(1)}, f32[64,128]{1,0:T(8,128)S(1)}, u32[]{:S(2)}, u32[]{:S(2)}) collective-permute-start(f32[64,128]{1,0:T(8,128)S(1)} %get-tuple-element.53), channel_id=1, source_target_pairs={{64,67},{65,68},{66,69},{67,70},{68,71},{69,72},{70,73},{71,74},{7... | collective-permute-start | bytes 98312 | tf_op jit(solution)/shard_map/ppermute | solution.py:377
  40.9 2.1 %collective-permute-start.12 = (f32[32,128]{1,0:T(8,128)S(1)}, f32[32,128]{1,0:T(8,128)S(1)}, u32[]{:S(2)}, u32[]{:S(2)}) collective-permute-start(f32[32,128]{1,0:T(8,128)S(1)} %get-tuple-element.48), channel_id=1, source_target_pairs={{64,96},{65,97},{66,98},{67,99},{68,100},{69,101},{70,102},{71,103... | collective-permute-start | bytes 49160 | tf_op jit(solution)/shard_map/ppermute | solution.py:377
  43.0 4.7 %collective-permute-start.13 = (f32[32,128]{1,0:T(8,128)S(1)}, f32[32,128]{1,0:T(8,128)S(1)}, u32[]{:S(2)}, u32[]{:S(2)}) collective-permute-start(f32[32,128]{1,0:T(8,128)S(1)} %get-tuple-element.50), channel_id=1, source_target_pairs={{64,95},{65,96},{66,97},{67,98},{68,99},{69,100},{70,101},{71,102}... | collective-permute-start | bytes 49160 | tf_op jit(solution)/shard_map/ppermute | solution.py:377
  47.7 0.1 collective-permute-done.10
  47.8 0.0 collective-permute-start.14
  47.8 0.6 %collective-permute-done.11 = f32[64,128]{1,0:T(8,128)S(1)} collective-permute-done((f32[64,128]{1,0:T(8,128)S(1)}, f32[64,128]{1,0:T(8,128)S(1)}, u32[]{:S(2)}, u32[]{:S(2)}) %collective-permute-start.11) | collective-permute-done | bytes 32800 | tf_op jit(solution)/shard_map/ppermute | solution.py:377
  48.3 0.0 collective-permute-done.9
  48.3 0.0 collective-permute-done.12
  48.3 0.2 collective-permute-done.13
  48.5 5.1 %collective-permute-done.14 = f32[32,128]{1,0:T(8,128)S(1)} collective-permute-done((f32[32,128]{1,0:T(8,128)S(1)}, f32[32,128]{1,0:T(8,128)S(1)}, u32[]{:S(2)}, u32[]{:S(2)}) %collective-permute-start.14) | collective-permute-done | bytes 16416 | tf_op jit(solution)/shard_map/ppermute | solution.py:377
  53.7 0.1 collective-permute-start.15
  53.8 1.2 %collective-permute-done.15.there = f32[64,128]{1,0:T(8,128)S(1)} collective-permute-done((f32[64,128]{1,0:T(8,128)S(1)}, f32[64,128]{1,0:T(8,128)S(1)}, u32[]{:S(2)}, u32[]{:S(2)}) %collective-permute-start.15) | collective-permute-done | bytes 32800 | tf_op jit(solution)/shard_map/ppermute | solution.py:383
  55.0 0.6 %smooth.1 = f32[1,4,1024]{2,1,0:T(4,128)} custom-call(f32[64,128]{1,0:T(8,128)S(1)} %pad_maximum_fusion.2.here, f32[64,128]{1,0:T(8,128)S(1)} %collective-permute-done.15.there, f32[152,128]{1,0:T(8,128)S(1)} %get-tuple-element.42.keep), custom_call_target="tpu_custom_call" | custom-call | tf_op jit(solution)/shard_map/smooth/pallas_call | solution.py:468
  (15 shorter events, 0.1 us)
Async XLA Ops:
  1.1 8.4 %collective-permute-start = (f32[440,128]{1,0:T(8,128)S(1)}, f32[440,128]{1,0:T(8,128)S(1)}, u32[]{:S(2)}, u32[]{:S(2)}) collective-permute-start(f32[440,128]{1,0:T(8,128)S(1)} %get-tuple-element.26), channel_id=1, source_target_pairs={{0,64},{64,0},{1,65},{65,1},{2,66},{66,2},{3,67},{67,3},{4,68},{68... | collective-permute-start | bytes 675848 | tf_op jit(solution)/shard_map/ppermute | solution.py:360
  9.5 14.9 %collective-permute-start.3 = (f32[160,128]{1,0:T(8,128)S(1)}, f32[160,128]{1,0:T(8,128)S(1)}, u32[]{:S(2)}, u32[]{:S(2)}) collective-permute-start(f32[160,128]{1,0:T(8,128)S(1)} %pad_maximum_fusion), channel_id=1, source_target_pairs={{0,1},{1,2},{2,3},{3,4},{4,5},{5,6},{6,7},{7,8},{8,9},{9,10},{10,1... | collective-permute-start | bytes 245768 | tf_op jit(solution)/shard_map/ppermute | solution.py:377
  18.1 6.1 %collective-permute-start.1 = (f32[104,128]{1,0:T(8,128)S(1)}, f32[104,128]{1,0:T(8,128)S(1)}, u32[]{:S(2)}, u32[]{:S(2)}) collective-permute-start(f32[104,128]{1,0:T(8,128)S(1)} %get-tuple-element.47), channel_id=1, source_target_pairs={{0,3},{1,4},{2,5},{3,6},{4,7},{5,8},{6,9},{7,10},{8,11},{9,12},{10... | collective-permute-start | bytes 159752 | tf_op jit(solution)/shard_map/ppermute | solution.py:377
  18.1 6.3 %collective-permute-start.2 = (f32[104,128]{1,0:T(8,128)S(1)}, f32[104,128]{1,0:T(8,128)S(1)}, u32[]{:S(2)}, u32[]{:S(2)}) collective-permute-start(f32[104,128]{1,0:T(8,128)S(1)} %get-tuple-element.45), channel_id=1, source_target_pairs={{0,2},{1,3},{2,4},{3,5},{4,6},{5,7},{6,8},{7,9},{8,10},{9,11},{10,... | collective-permute-start | bytes 159752 | tf_op jit(solution)/shard_map/ppermute | solution.py:377
  19.6 4.8 %collective-permute-start.4 = (f32[80,128]{1,0:T(8,128)S(1)}, f32[80,128]{1,0:T(8,128)S(1)}, u32[]{:S(2)}, u32[]{:S(2)}) collective-permute-start(f32[80,128]{1,0:T(8,128)S(1)} %slice_select_fusion.3), channel_id=1, source_target_pairs={{0,32},{1,33},{2,34},{3,35},{4,36},{5,37},{6,38},{7,39},{8,40},{9,... | collective-permute-start | bytes 122888 | tf_op jit(solution)/shard_map/ppermute | solution.py:377
  20.1 6.8 %collective-permute-start.5 = (f32[24,128]{1,0:T(8,128)S(1)}, f32[24,128]{1,0:T(8,128)S(1)}, u32[]{:S(2)}, u32[]{:S(2)}) collective-permute-start(f32[24,128]{1,0:T(8,128)S(1)} %get-tuple-element.44), channel_id=1, source_target_pairs={{0,31},{1,32},{2,33},{3,34},{4,35},{5,36},{6,37},{7,38},{8,39},{9,... | collective-permute-start | bytes 36872 | tf_op jit(solution)/shard_map/ppermute | solution.py:377
  24.2 2.7 %collective-permute-start.6 = (f32[24,128]{1,0:T(8,128)S(1)}, f32[24,128]{1,0:T(8,128)S(1)}, u32[]{:S(2)}, u32[]{:S(2)}) collective-permute-start(f32[24,128]{1,0:T(8,128)S(1)} %get-tuple-element.43), channel_id=1, source_target_pairs={{0,4},{1,5},{2,6},{3,7},{4,8},{5,9},{6,10},{7,11},{8,12},{9,13},{1... | collective-permute-start | bytes 36872 | tf_op jit(solution)/shard_map/ppermute | solution.py:377
  26.9 3.9 %collective-permute-start.7 = (f32[160,128]{1,0:T(8,128)S(1)}, f32[160,128]{1,0:T(8,128)S(1)}, u32[]{:S(2)}, u32[]{:S(2)}) collective-permute-start(f32[160,128]{1,0:T(8,128)S(1)} %pad_maximum_fusion.1.r_0_), channel_id=1, source_target_pairs={{0,64},{64,0},{1,65},{65,1},{2,66},{66,2},{3,67},{67,3},{4,68},{68... | collective-permute-start | bytes 245768 | tf_op jit(solution)/shard_map/ppermute | solution.py:383
  37.7 1.5 %collective-permute-start.8 = (f32[288,128]{1,0:T(8,128)S(1)}, f32[288,128]{1,0:T(8,128)S(1)}, u32[]{:S(2)}, u32[]{:S(2)}) collective-permute-start(f32[288,128]{1,0:T(8,128)S(1)} %get-tuple-element.36), channel_id=1, source_target_pairs={{0,64},{64,0},{1,65},{65,1},{2,66},{66,2},{3,67},{67,3},{4,68},{68... | collective-permute-start | bytes 442376 | tf_op jit(solution)/shard_map/ppermute | solution.py:360
  39.2 8.6 %collective-permute-start.10 = (f32[64,128]{1,0:T(8,128)S(1)}, f32[64,128]{1,0:T(8,128)S(1)}, u32[]{:S(2)}, u32[]{:S(2)}) collective-permute-start(f32[64,128]{1,0:T(8,128)S(1)} %get-tuple-element.51), channel_id=1, source_target_pairs={{64,66},{65,67},{66,68},{67,69},{68,70},{69,71},{70,72},{71,73},{7... | collective-permute-start | bytes 98312 | tf_op jit(solution)/shard_map/ppermute | solution.py:377
  40.1 8.2 %collective-permute-start.11 = (f32[64,128]{1,0:T(8,128)S(1)}, f32[64,128]{1,0:T(8,128)S(1)}, u32[]{:S(2)}, u32[]{:S(2)}) collective-permute-start(f32[64,128]{1,0:T(8,128)S(1)} %get-tuple-element.52), channel_id=1, source_target_pairs={{64,65},{65,66},{66,67},{67,68},{68,69},{69,70},{70,71},{71,72},{7... | collective-permute-start | bytes 98312 | tf_op jit(solution)/shard_map/ppermute | solution.py:377
  40.1 8.2 %collective-permute-start.9 = (f32[64,128]{1,0:T(8,128)S(1)}, f32[64,128]{1,0:T(8,128)S(1)}, u32[]{:S(2)}, u32[]{:S(2)}) collective-permute-start(f32[64,128]{1,0:T(8,128)S(1)} %get-tuple-element.53), channel_id=1, source_target_pairs={{64,67},{65,68},{66,69},{67,70},{68,71},{69,72},{70,73},{71,74},{7... | collective-permute-start | bytes 98312 | tf_op jit(solution)/shard_map/ppermute | solution.py:377
  40.9 7.4 %collective-permute-start.12 = (f32[32,128]{1,0:T(8,128)S(1)}, f32[32,128]{1,0:T(8,128)S(1)}, u32[]{:S(2)}, u32[]{:S(2)}) collective-permute-start(f32[32,128]{1,0:T(8,128)S(1)} %get-tuple-element.48), channel_id=1, source_target_pairs={{64,96},{65,97},{66,98},{67,99},{68,100},{69,101},{70,102},{71,103... | collective-permute-start | bytes 49160 | tf_op jit(solution)/shard_map/ppermute | solution.py:377
  43.0 5.5 %collective-permute-start.13 = (f32[32,128]{1,0:T(8,128)S(1)}, f32[32,128]{1,0:T(8,128)S(1)}, u32[]{:S(2)}, u32[]{:S(2)}) collective-permute-start(f32[32,128]{1,0:T(8,128)S(1)} %get-tuple-element.50), channel_id=1, source_target_pairs={{64,95},{65,96},{66,97},{67,98},{68,99},{69,100},{70,101},{71,102}... | collective-permute-start | bytes 49160 | tf_op jit(solution)/shard_map/ppermute | solution.py:377
  47.8 5.9 %collective-permute-start.14 = (f32[32,128]{1,0:T(8,128)S(1)}, f32[32,128]{1,0:T(8,128)S(1)}, u32[]{:S(2)}, u32[]{:S(2)}) collective-permute-start(f32[32,128]{1,0:T(8,128)S(1)} %get-tuple-element.49), channel_id=1, source_target_pairs={{64,68},{65,69},{66,70},{67,71},{68,72},{69,73},{70,74},{71,75},{7... | collective-permute-start | bytes 49160 | tf_op jit(solution)/shard_map/ppermute | solution.py:377
  53.7 1.3 %collective-permute-start.15 = (f32[64,128]{1,0:T(8,128)S(1)}, f32[64,128]{1,0:T(8,128)S(1)}, u32[]{:S(2)}, u32[]{:S(2)}) collective-permute-start(f32[64,128]{1,0:T(8,128)S(1)} %pad_maximum_fusion.2.here), channel_id=1, source_target_pairs={{0,64},{64,0},{1,65},{65,1},{2,66},{66,2},{3,67},{67,3},{4,68},{68... | collective-permute-start | bytes 98312 | tf_op jit(solution)/shard_map/ppermute | solution.py:383

commit v6 on v5

--- a/solution.py
+++ b/solution.py
@@ -21,8 +21,8 @@
 SEA_VMEM = 24 * 1024 * 1024
 LAST_VMEM = 4 * 1024 * 1024
 PAIR = 2
-SEND_AHEAD = 2
-SEA_AHEAD = 3
+SEND_AHEAD = 3
+SEA_AHEAD = 4
 
 
 def offsets_of(count):
@@ -35,12 +35,12 @@
 
 def routes_of(count):
     half = count // 2
-    return [(3, -3), (2, -2), (half, half), (1, -1), (half - 1, half + 1), (4, -4)]
-
-
-SMALL = 4
-FAR = 2
+    return [(half, half), (half - 1, half + 1), (3, -3), (1, -1), (4, -4), (2, -2)]
+
+
+FAR = 0
 BESIDE = 3
+SMALL = (1, 4)
 SIDE = 56
 
 
@@ -116,7 +116,7 @@
     return copy
 
 
-def run_tiles(fields, tiles, weights, sems, ahead, src, dst, table, sums):
+def run_tiles(fields, tiles, weights, sems, ahead, src, dst, table, sums, awaited):
     rows = len(fields) * BLK
     block = lax.broadcasted_iota(jnp.int32, (rows, TILE), 0) & (BLK - 1)
     for s in range(BLK):
@@ -124,6 +124,8 @@
         for d in range(BLK):
             table[s * (BLK + 1) + d] = jnp.where(block == d, spread, 0.0).astype(jnp.bfloat16)
         table[s * (BLK + 1) + BLK] = jnp.zeros((rows, TILE), jnp.bfloat16)
+    for copy in awaited:
+        copy.wait()
     slots = weights.shape[1]
     steps = weights.shape[0] // PAIR
 
@@ -223,8 +225,6 @@
     def _():
         copies = fetch([(state.at[0], v_state), (land, v_land), (tile_src.at[0, 0], src), (targets.at[0], plane)], sems)
         start_pair(tiles, weights, wsems, 0)
-        copies[3].wait()
-        chosen_in = own_targets(plane, chosen, dst, sems.at[3])
         copies[0].wait()
         copies[1].wait()
         for n in range(1, SEND_AHEAD):
@@ -233,9 +233,9 @@
         lay_out(lambda c, at: v_land[:, at], 1, work, LAND)
         channels = [work[c * BLK : (c + 1) * BLK] for c in range(LAND + 1)]
         fields = compute_fluxes(channels[:LAND], channels[LAND])
-        copies[2].wait()
-        chosen_in.wait()
-        run_tiles(fields, tiles, weights, wsems, SEND_AHEAD, src, dst, table, sums)
+        copies[3].wait()
+        chosen_in = own_targets(plane, chosen, dst, sems.at[3])
+        run_tiles(fields, tiles, weights, wsems, SEND_AHEAD, src, dst, table, sums, [copies[2], chosen_in])
         write_messages(sums, outs, handed, count, FLUX * BLK, FLUX_HALO, 2)
 
     @pl.when(section == 1)
@@ -269,10 +269,6 @@
         copies = fetch([(tile_src.at[0, 0], src), (targets.at[1], plane)], sems)
         start_pair(tiles, weights, wsems, 0)
         edge[...] = jnp.zeros_like(edge)
-        for c in copies:
-            c.wait()
-        chosen_in = own_targets(plane, chosen, dst, sems.at[2])
-        start_pair(tiles, weights, wsems, 1)
         rows = FLUX * BLK
         side = rows + len(FLUX_HALO) * BLK
         for c in range(TABLE):
@@ -303,7 +299,7 @@
         mixed = 1.0 + softplus(near(7))
         drag = 0.3 * (1.0 - ice)
         push_u, push_v, push_h = drag * force_wide(0), drag * force_wide(1), 0.1 * force_wide(8)
-        for _ in range(SUBSTEPS):
+        for step in range(SUBSTEPS):
             slopes = spread(height)
             grad_x = sum(w * s for w, s in zip(grad_wx, slopes))
             grad_y = sum(w * s for w, s in zip(grad_wy, slopes))
@@ -314,14 +310,18 @@
             moved = sum(wx * a + wy * b for wx, wy, a, b in zip(grad_wx, grad_wy, moved_u, moved_v))
             height = height - 0.5 * moved + push_h
             flow_u, flow_v = next_u, next_v
+            if step == 0:
+                copies[1].wait()
+                chosen_in = own_targets(plane, chosen, dst, sems.at[2])
+                start_pair(tiles, weights, wsems, 1)
         for n in range(2, SEA_AHEAD):
             start_pair(tiles, weights, wsems, n)
         new_temp = near(4) + 0.2 * near(LAND) * force(9) / mixed
         u, v = flow_u[:BLK], flow_v[:BLK]
         for r, field in enumerate([height[:BLK], u, v, new_temp]):
             keep[r * BLK : (r + 1) * BLK] = field
-        chosen_in.wait()
-        run_tiles([new_temp, ice[:BLK], u, v], tiles, weights, wsems, SEA_AHEAD, src, dst, table, sums)
+        surface = [new_temp, ice[:BLK], u, v]
+        run_tiles(surface, tiles, weights, wsems, SEA_AHEAD, src, dst, table, sums, [copies[0], chosen_in])
         write_messages(sums, outs, handed, count, SURF * BLK, SURF_HALO, 1)
 
 
@@ -375,8 +375,8 @@
         pairs = [(source * count + i, source * count + (i + near) % count) for i in range(count)]
         pairs += [((1 - source) * count + i, (1 - source) * count + (i + far) % count) for i in range(count)]
         got.append(lax.ppermute(payload, AXES, pairs))
-    total = outs[0] + sum(g[:full] for n, g in enumerate(got[:SMALL]) if n != FAR)
-    parts = [total[:rows] + got[FAR], total[rows:] + sum(got[SMALL:])]
+    total = outs[0] + sum(g[:full] for n, g in enumerate(got) if n != FAR and n not in SMALL)
+    parts = [total[:rows] + got[FAR], total[rows:] + sum(got[n] for n in SMALL)]
     if side is not None:
         parts.append(got[BESIDE][full:])
     here = jnp.concatenate(parts)
@@ -402,7 +402,7 @@
         return pltpu.VMEM((rows, TILE), f32)
 
     def shapes_for(rows, halo):
-        sizes = [rows if n == FAR else halo if n >= SMALL else rows + halo for n in range(len(routes_of(count)))]
+        sizes = [rows if n == FAR else halo if n in SMALL else rows + halo for n in range(len(routes_of(count)))]
         return [shaped(size) for size in [rows + halo] + sizes + [sum(sizes)]]
 
     def remap_scratch(rows):

time: 55.7 us -> 55 us (0.987)
  starting transfers between devices: 33.8 us -> 33.1 us
    ppermute x12, starting transfers between devices: 23.3 us -> 22.7 us  [exchange(): got.append(lax.ppermute(payload, AXES, pairs))]
where the time goes in v6:
time: 55 us; the launch traced here: 54.9 us
  starting transfers between devices  33.1 us (60%)
  waiting for transfers between devices  13.3 us (24%)
  Pallas kernels  8.2 us (15%)
    ppermute x12, starting transfers between devices, exchange(): got.append(lax.ppermute(payload, AXES, pairs))  22.7 us
    ppermute x12, waiting for transfers between devices, exchange(): got.append(lax.ppermute(payload, AXES, pairs))  8.68 us
    ppermute x2, starting transfers between devices, exchange(): crossed = lax.ppermute(handed, 'sec', swap)  7.34 us
    pallas_call x1, Pallas kernels, body(): pl.pallas_call(lambda *r: sea_kernel(count, *r), name='sea_remap', out_sh...  6.51 us
    ppermute x2, starting transfers between devices, exchange(): return (here, lax.ppermute(here, 'sec', swap))  3.07 us
    ppermute x2, waiting for transfers between devices, exchange(): crossed = lax.ppermute(handed, 'sec', swap)  2.47 us
    ppermute x2, waiting for transfers between devices, exchange(): return (here, lax.ppermute(here, 'sec', swap))  2.12 us
  transfers between devices with their start and end apart: 16, of which 9 were waited for; matrix products, arithmetic and copies ran while one was open for 0% of the time, Pallas kernels for 0%

profile of v6, /device:TPU:1, one launch (start us, length us, event | category | flops | bytes accessed | tf_op | source)
XLA Modules:
  0.0 54.9 jit_solution(7094750780635549131)
XLA Ops:
  0.0 1.1 %flux_remap.1 = (f32[104,128]{1,0:T(8,128)S(1)}, f32[80,128]{1,0:T(8,128)S(1)}, f32[24,128]{1,0:T(8,128)S(1)}, f32[104,128]{1,0:T(8,128)S(1)}, f32[104,128]{1,0:...) custom-call(f32[1,8,1024]{2,1,0:T(8,128)} %r_0_.1, ...), custom_call_target="tpu_custom_call" | custom-call | flops 201326592 | bytes 12582912 | tf_op jit(solution)/shard_map/flux_remap/pallas_call | solution.py:423
  1.1 7.3 %collective-permute-start = (f32[440,128]{1,0:T(8,128)S(1)}, f32[440,128]{1,0:T(8,128)S(1)}, u32[]{:S(2)}, u32[]{:S(2)}) collective-permute-start(f32[440,128]{1,0:T(8,128)S(1)} %get-tuple-element.26), channel_id=1, source_target_pairs={{0,64},{64,0},{1,65},{65,1},{2,66},{66,2},{3,67},{67,3},{4,68},{68... | collective-permute-start | bytes 675848 | tf_op jit(solution)/shard_map/ppermute | solution.py:360
  8.3 1.1 %collective-permute-done = f32[440,128]{1,0:T(8,128)S(1)} collective-permute-done((f32[440,128]{1,0:T(8,128)S(1)}, f32[440,128]{1,0:T(8,128)S(1)}, u32[]{:S(2)}, u32[]{:S(2)}) %collective-permute-start) | collective-permute-done | bytes 225312 | tf_op jit(solution)/shard_map/ppermute | solution.py:360
  9.5 8.5 %collective-permute-start.2 = (f32[160,128]{1,0:T(8,128)S(1)}, f32[160,128]{1,0:T(8,128)S(1)}, u32[]{:S(2)}, u32[]{:S(2)}) collective-permute-start(f32[160,128]{1,0:T(8,128)S(1)} %pad_maximum_fusion), channel_id=1, source_target_pairs={{0,1},{1,2},{2,3},{3,4},{4,5},{5,6},{6,7},{7,8},{8,9},{9,10},{10,1... | collective-permute-start | bytes 245768 | tf_op jit(solution)/shard_map/ppermute | solution.py:377
  18.0 0.0 collective-permute-start.1
  18.1 1.5 %collective-permute-start.3 = (f32[104,128]{1,0:T(8,128)S(1)}, f32[104,128]{1,0:T(8,128)S(1)}, u32[]{:S(2)}, u32[]{:S(2)}) collective-permute-start(f32[104,128]{1,0:T(8,128)S(1)} %get-tuple-element.46), channel_id=1, source_target_pairs={{0,2},{1,3},{2,4},{3,5},{4,6},{5,7},{6,8},{7,9},{8,10},{9,11},{10,... | collective-permute-start | bytes 159752 | tf_op jit(solution)/shard_map/ppermute | solution.py:377
  19.5 0.5 collective-permute-start.4
  20.1 4.1 %collective-permute-start.5 = (f32[24,128]{1,0:T(8,128)S(1)}, f32[24,128]{1,0:T(8,128)S(1)}, u32[]{:S(2)}, u32[]{:S(2)}) collective-permute-start(f32[24,128]{1,0:T(8,128)S(1)} %get-tuple-element.44), channel_id=1, source_target_pairs={{0,31},{1,32},{2,33},{3,34},{4,35},{5,36},{6,37},{7,38},{8,39},{9,... | collective-permute-start | bytes 36872 | tf_op jit(solution)/shard_map/ppermute | solution.py:377
  24.2 0.0 collective-permute-done.1
  24.2 0.2 collective-permute-start.6
  24.4 0.0 collective-permute-done.3
  24.4 0.0 collective-permute-done.2
  24.4 0.0 collective-permute-done.4
  24.4 2.4 %collective-permute-done.5 = f32[24,128]{1,0:T(8,128)S(1)} collective-permute-done((f32[24,128]{1,0:T(8,128)S(1)}, f32[24,128]{1,0:T(8,128)S(1)}, u32[]{:S(2)}, u32[]{:S(2)}) %collective-permute-start.5) | collective-permute-done | bytes 12320 | tf_op jit(solution)/shard_map/ppermute | solution.py:377
  26.8 0.0 collective-permute-done.6
  26.9 3.0 %collective-permute-start.7 = (f32[160,128]{1,0:T(8,128)S(1)}, f32[160,128]{1,0:T(8,128)S(1)}, u32[]{:S(2)}, u32[]{:S(2)}) collective-permute-start(f32[160,128]{1,0:T(8,128)S(1)} %pad_maximum_fusion.1.r_0_), channel_id=1, source_target_pairs={{0,64},{64,0},{1,65},{65,1},{2,66},{66,2},{3,67},{67,3},{4,68},{68... | collective-permute-start | bytes 245768 | tf_op jit(solution)/shard_map/ppermute | solution.py:383
  29.9 0.9 %collective-permute-done.7.r_1_ = f32[160,128]{1,0:T(8,128)S(1)} collective-permute-done((f32[160,128]{1,0:T(8,128)S(1)}, f32[160,128]{1,0:T(8,128)S(1)}, u32[]{:S(2)}, u32[]{:S(2)}) %collective-permute-start.7) | collective-permute-done | bytes 81952 | tf_op jit(solution)/shard_map/ppermute | solution.py:383
  30.8 6.5 %sea_remap.1 = (f32[64,128]{1,0:T(8,128)S(1)}, f32[32,128]{1,0:T(8,128)S(1)}, f32[32,128]{1,0:T(8,128)S(1)}, f32[64,128]{1,0:T(8,128)S(1)}, f32[64,128]{1,0:T(8,...) custom-call(f32[160,128]{1,0:T(8,128)S(1)} %pad_maximum_fusion.1.r_0_, ...), custom_call_target="tpu_custom_call" | custom-call | flops 201326592 | bytes 12582912 | tf_op jit(solution)/shard_map/sea_remap/pallas_call | solution.py:447
  37.3 0.1 collective-permute-start.8
  37.4 1.4 %collective-permute-done.8 = f32[288,128]{1,0:T(8,128)S(1)} collective-permute-done((f32[288,128]{1,0:T(8,128)S(1)}, f32[288,128]{1,0:T(8,128)S(1)}, u32[]{:S(2)}, u32[]{:S(2)}) %collective-permute-start.8) | collective-permute-done | bytes 147488 | tf_op jit(solution)/shard_map/ppermute | solution.py:360
  38.8 0.1 collective-permute-start.10
  38.8 1.1 %collective-permute-start.11 = (f32[64,128]{1,0:T(8,128)S(1)}, f32[64,128]{1,0:T(8,128)S(1)}, u32[]{:S(2)}, u32[]{:S(2)}) collective-permute-start(f32[64,128]{1,0:T(8,128)S(1)} %get-tuple-element.52), channel_id=1, source_target_pairs={{64,66},{65,67},{66,68},{67,69},{68,70},{69,71},{70,72},{71,73},{7... | collective-permute-start | bytes 98312 | tf_op jit(solution)/shard_map/ppermute | solution.py:377
  40.0 0.0 collective-permute-start.9
  40.0 2.5 %collective-permute-start.12 = (f32[32,128]{1,0:T(8,128)S(1)}, f32[32,128]{1,0:T(8,128)S(1)}, u32[]{:S(2)}, u32[]{:S(2)}) collective-permute-start(f32[32,128]{1,0:T(8,128)S(1)} %get-tuple-element.48), channel_id=1, source_target_pairs={{64,96},{65,97},{66,98},{67,99},{68,100},{69,101},{70,102},{71,103... | collective-permute-start | bytes 49160 | tf_op jit(solution)/shard_map/ppermute | solution.py:377
  42.5 4.1 %collective-permute-start.13 = (f32[32,128]{1,0:T(8,128)S(1)}, f32[32,128]{1,0:T(8,128)S(1)}, u32[]{:S(2)}, u32[]{:S(2)}) collective-permute-start(f32[32,128]{1,0:T(8,128)S(1)} %get-tuple-element.50), channel_id=1, source_target_pairs={{64,95},{65,96},{66,97},{67,98},{68,99},{69,100},{70,101},{71,102}... | collective-permute-start | bytes 49160 | tf_op jit(solution)/shard_map/ppermute | solution.py:377
  46.6 0.4 collective-permute-done.10
  47.0 0.0 collective-permute-start.14
  47.0 0.6 %collective-permute-done.11 = f32[64,128]{1,0:T(8,128)S(1)} collective-permute-done((f32[64,128]{1,0:T(8,128)S(1)}, f32[64,128]{1,0:T(8,128)S(1)}, u32[]{:S(2)}, u32[]{:S(2)}) %collective-permute-start.11) | collective-permute-done | bytes 32800 | tf_op jit(solution)/shard_map/ppermute | solution.py:377
  47.6 0.1 collective-permute-done.9
  47.8 0.0 collective-permute-done.12
  47.8 0.0 collective-permute-done.13
  47.8 5.1 %collective-permute-done.14 = f32[32,128]{1,0:T(8,128)S(1)} collective-permute-done((f32[32,128]{1,0:T(8,128)S(1)}, f32[32,128]{1,0:T(8,128)S(1)}, u32[]{:S(2)}, u32[]{:S(2)}) %collective-permute-start.14) | collective-permute-done | bytes 16416 | tf_op jit(solution)/shard_map/ppermute | solution.py:377
  53.0 0.1 collective-permute-start.15
  53.1 1.2 %collective-permute-done.15.there = f32[64,128]{1,0:T(8,128)S(1)} collective-permute-done((f32[64,128]{1,0:T(8,128)S(1)}, f32[64,128]{1,0:T(8,128)S(1)}, u32[]{:S(2)}, u32[]{:S(2)}) %collective-permute-start.15) | collective-permute-done | bytes 32800 | tf_op jit(solution)/shard_map/ppermute | solution.py:383
  54.2 0.6 %smooth.1 = f32[1,4,1024]{2,1,0:T(4,128)} custom-call(f32[64,128]{1,0:T(8,128)S(1)} %pad_maximum_fusion.2.here, f32[64,128]{1,0:T(8,128)S(1)} %collective-permute-done.15.there, f32[152,128]{1,0:T(8,128)S(1)} %get-tuple-element.42.keep), custom_call_target="tpu_custom_call" | custom-call | tf_op jit(solution)/shard_map/smooth/pallas_call | solution.py:468
  (15 shorter events, 0.1 us)
Async XLA Ops:
  1.1 8.4 %collective-permute-start = (f32[440,128]{1,0:T(8,128)S(1)}, f32[440,128]{1,0:T(8,128)S(1)}, u32[]{:S(2)}, u32[]{:S(2)}) collective-permute-start(f32[440,128]{1,0:T(8,128)S(1)} %get-tuple-element.26), channel_id=1, source_target_pairs={{0,64},{64,0},{1,65},{65,1},{2,66},{66,2},{3,67},{67,3},{4,68},{68... | collective-permute-start | bytes 675848 | tf_op jit(solution)/shard_map/ppermute | solution.py:360
  9.5 14.9 %collective-permute-start.2 = (f32[160,128]{1,0:T(8,128)S(1)}, f32[160,128]{1,0:T(8,128)S(1)}, u32[]{:S(2)}, u32[]{:S(2)}) collective-permute-start(f32[160,128]{1,0:T(8,128)S(1)} %pad_maximum_fusion), channel_id=1, source_target_pairs={{0,1},{1,2},{2,3},{3,4},{4,5},{5,6},{6,7},{7,8},{8,9},{9,10},{10,1... | collective-permute-start | bytes 245768 | tf_op jit(solution)/shard_map/ppermute | solution.py:377
  18.0 6.1 %collective-permute-start.1 = (f32[104,128]{1,0:T(8,128)S(1)}, f32[104,128]{1,0:T(8,128)S(1)}, u32[]{:S(2)}, u32[]{:S(2)}) collective-permute-start(f32[104,128]{1,0:T(8,128)S(1)} %get-tuple-element.45), channel_id=1, source_target_pairs={{0,3},{1,4},{2,5},{3,6},{4,7},{5,8},{6,9},{7,10},{8,11},{9,12},{10... | collective-permute-start | bytes 159752 | tf_op jit(solution)/shard_map/ppermute | solution.py:377
  18.1 6.3 %collective-permute-start.3 = (f32[104,128]{1,0:T(8,128)S(1)}, f32[104,128]{1,0:T(8,128)S(1)}, u32[]{:S(2)}, u32[]{:S(2)}) collective-permute-start(f32[104,128]{1,0:T(8,128)S(1)} %get-tuple-element.46), channel_id=1, source_target_pairs={{0,2},{1,3},{2,4},{3,5},{4,6},{5,7},{6,8},{7,9},{8,10},{9,11},{10,... | collective-permute-start | bytes 159752 | tf_op jit(solution)/shard_map/ppermute | solution.py:377
  19.5 4.8 %collective-permute-start.4 = (f32[80,128]{1,0:T(8,128)S(1)}, f32[80,128]{1,0:T(8,128)S(1)}, u32[]{:S(2)}, u32[]{:S(2)}) collective-permute-start(f32[80,128]{1,0:T(8,128)S(1)} %slice_select_fusion.3), channel_id=1, source_target_pairs={{0,32},{1,33},{2,34},{3,35},{4,36},{5,37},{6,38},{7,39},{8,40},{9,... | collective-permute-start | bytes 122888 | tf_op jit(solution)/shard_map/ppermute | solution.py:377
  20.1 6.8 %collective-permute-start.5 = (f32[24,128]{1,0:T(8,128)S(1)}, f32[24,128]{1,0:T(8,128)S(1)}, u32[]{:S(2)}, u32[]{:S(2)}) collective-permute-start(f32[24,128]{1,0:T(8,128)S(1)} %get-tuple-element.44), channel_id=1, source_target_pairs={{0,31},{1,32},{2,33},{3,34},{4,35},{5,36},{6,37},{7,38},{8,39},{9,... | collective-permute-start | bytes 36872 | tf_op jit(solution)/shard_map/ppermute | solution.py:377
  24.2 2.7 %collective-permute-start.6 = (f32[24,128]{1,0:T(8,128)S(1)}, f32[24,128]{1,0:T(8,128)S(1)}, u32[]{:S(2)}, u32[]{:S(2)}) collective-permute-start(f32[24,128]{1,0:T(8,128)S(1)} %get-tuple-element.43), channel_id=1, source_target_pairs={{0,4},{1,5},{2,6},{3,7},{4,8},{5,9},{6,10},{7,11},{8,12},{9,13},{1... | collective-permute-start | bytes 36872 | tf_op jit(solution)/shard_map/ppermute | solution.py:377
  26.9 3.9 %collective-permute-start.7 = (f32[160,128]{1,0:T(8,128)S(1)}, f32[160,128]{1,0:T(8,128)S(1)}, u32[]{:S(2)}, u32[]{:S(2)}) collective-permute-start(f32[160,128]{1,0:T(8,128)S(1)} %pad_maximum_fusion.1.r_0_), channel_id=1, source_target_pairs={{0,64},{64,0},{1,65},{65,1},{2,66},{66,2},{3,67},{67,3},{4,68},{68... | collective-permute-start | bytes 245768 | tf_op jit(solution)/shard_map/ppermute | solution.py:383
  37.3 1.5 %collective-permute-start.8 = (f32[288,128]{1,0:T(8,128)S(1)}, f32[288,128]{1,0:T(8,128)S(1)}, u32[]{:S(2)}, u32[]{:S(2)}) collective-permute-start(f32[288,128]{1,0:T(8,128)S(1)} %get-tuple-element.36), channel_id=1, source_target_pairs={{0,64},{64,0},{1,65},{65,1},{2,66},{66,2},{3,67},{67,3},{4,68},{68... | collective-permute-start | bytes 442376 | tf_op jit(solution)/shard_map/ppermute | solution.py:360
  38.8 8.3 %collective-permute-start.10 = (f32[64,128]{1,0:T(8,128)S(1)}, f32[64,128]{1,0:T(8,128)S(1)}, u32[]{:S(2)}, u32[]{:S(2)}) collective-permute-start(f32[64,128]{1,0:T(8,128)S(1)} %get-tuple-element.51), channel_id=1, source_target_pairs={{64,65},{65,66},{66,67},{67,68},{68,69},{69,70},{70,71},{71,72},{7... | collective-permute-start | bytes 98312 | tf_op jit(solution)/shard_map/ppermute | solution.py:377
  38.8 8.8 %collective-permute-start.11 = (f32[64,128]{1,0:T(8,128)S(1)}, f32[64,128]{1,0:T(8,128)S(1)}, u32[]{:S(2)}, u32[]{:S(2)}) collective-permute-start(f32[64,128]{1,0:T(8,128)S(1)} %get-tuple-element.52), channel_id=1, source_target_pairs={{64,66},{65,67},{66,68},{67,69},{68,70},{69,71},{70,72},{71,73},{7... | collective-permute-start | bytes 98312 | tf_op jit(solution)/shard_map/ppermute | solution.py:377
  40.0 7.8 %collective-permute-start.9 = (f32[64,128]{1,0:T(8,128)S(1)}, f32[64,128]{1,0:T(8,128)S(1)}, u32[]{:S(2)}, u32[]{:S(2)}) collective-permute-start(f32[64,128]{1,0:T(8,128)S(1)} %get-tuple-element.53), channel_id=1, source_target_pairs={{64,67},{65,68},{66,69},{67,70},{68,71},{69,72},{70,73},{71,74},{7... | collective-permute-start | bytes 98312 | tf_op jit(solution)/shard_map/ppermute | solution.py:377
  40.0 7.8 %collective-permute-start.12 = (f32[32,128]{1,0:T(8,128)S(1)}, f32[32,128]{1,0:T(8,128)S(1)}, u32[]{:S(2)}, u32[]{:S(2)}) collective-permute-start(f32[32,128]{1,0:T(8,128)S(1)} %get-tuple-element.48), channel_id=1, source_target_pairs={{64,96},{65,97},{66,98},{67,99},{68,100},{69,101},{70,102},{71,103... | collective-permute-start | bytes 49160 | tf_op jit(solution)/shard_map/ppermute | solution.py:377
  42.5 5.3 %collective-permute-start.13 = (f32[32,128]{1,0:T(8,128)S(1)}, f32[32,128]{1,0:T(8,128)S(1)}, u32[]{:S(2)}, u32[]{:S(2)}) collective-permute-start(f32[32,128]{1,0:T(8,128)S(1)} %get-tuple-element.50), channel_id=1, source_target_pairs={{64,95},{65,96},{66,97},{67,98},{68,99},{69,100},{70,101},{71,102}... | collective-permute-start | bytes 49160 | tf_op jit(solution)/shard_map/ppermute | solution.py:377
  47.0 5.9 %collective-permute-start.14 = (f32[32,128]{1,0:T(8,128)S(1)}, f32[32,128]{1,0:T(8,128)S(1)}, u32[]{:S(2)}, u32[]{:S(2)}) collective-permute-start(f32[32,128]{1,0:T(8,128)S(1)} %get-tuple-element.49), channel_id=1, source_target_pairs={{64,68},{65,69},{66,70},{67,71},{68,72},{69,73},{70,74},{71,75},{7... | collective-permute-start | bytes 49160 | tf_op jit(solution)/shard_map/ppermute | solution.py:377
  53.0 1.3 %collective-permute-start.15 = (f32[64,128]{1,0:T(8,128)S(1)}, f32[64,128]{1,0:T(8,128)S(1)}, u32[]{:S(2)}, u32[]{:S(2)}) collective-permute-start(f32[64,128]{1,0:T(8,128)S(1)} %pad_maximum_fusion.2.here), channel_id=1, source_target_pairs={{0,64},{64,0},{1,65},{65,1},{2,66},{66,2},{3,67},{67,3},{4,68},{68... | collective-permute-start | bytes 98312 | tf_op jit(solution)/shard_map/ppermute | solution.py:383

commit v7 on v6

--- a/solution.py
+++ b/solution.py
@@ -116,14 +116,21 @@
     return copy
 
 
-def run_tiles(fields, tiles, weights, sems, ahead, src, dst, table, sums, awaited):
+def run_tiles(fields, tiles, weights, sems, ahead, src, dst, table, lines, sums, awaited):
     rows = len(fields) * BLK
     block = lax.broadcasted_iota(jnp.int32, (rows, TILE), 0) & (BLK - 1)
-    for s in range(BLK):
-        spread = jnp.concatenate([jnp.broadcast_to(f[s : s + 1], (BLK, TILE)) for f in fields], axis=0)
+    for f, field in enumerate(fields):
+        lines[f * BLK : (f + 1) * BLK] = field
+
+    def one_source(s, carry):
+        line = lines[pl.ds(s, len(fields), stride=BLK)]
+        spread = jnp.concatenate([jnp.broadcast_to(line[f : f + 1], (BLK, TILE)) for f in range(len(fields))], axis=0)
         for d in range(BLK):
             table[s * (BLK + 1) + d] = jnp.where(block == d, spread, 0.0).astype(jnp.bfloat16)
         table[s * (BLK + 1) + BLK] = jnp.zeros((rows, TILE), jnp.bfloat16)
+        return carry
+
+    lax.fori_loop(0, BLK, one_source, 0)
     for copy in awaited:
         copy.wait()
     slots = weights.shape[1]
@@ -218,7 +225,7 @@
 
 def send_kernel(count, state, links, coef, land, tile_src, targets, tiles, *refs):
     outs, (handed, low, own) = refs[:7], refs[7:10]
-    (weights, table, sums, src, plane, chosen, dst, v_state, v_links, v_coef, v_land, work, wsems, sems) = refs[10:]
+    (weights, table, lines, sums, src, plane, chosen, dst, v_state, v_links, v_coef, v_land, work, wsems, sems) = refs[10:]
     section = lax.axis_index("sec")
 
     @pl.when(section == 0)
@@ -235,7 +242,7 @@
         fields = compute_fluxes(channels[:LAND], channels[LAND])
         copies[3].wait()
         chosen_in = own_targets(plane, chosen, dst, sems.at[3])
-        run_tiles(fields, tiles, weights, wsems, SEND_AHEAD, src, dst, table, sums, [copies[2], chosen_in])
+        run_tiles(fields, tiles, weights, wsems, SEND_AHEAD, src, dst, table, lines, sums, [copies[2], chosen_in])
         write_messages(sums, outs, handed, count, FLUX * BLK, FLUX_HALO, 2)
 
     @pl.when(section == 1)
@@ -253,7 +260,7 @@
 
 def sea_kernel(count, here, there, own, links, coef, land, tile_src, targets, tiles, *refs):
     outs, (handed, keep) = refs[:7], refs[7:9]
-    (weights, table, sums, src, plane, chosen, dst, v_links, v_coef, v_land, edge, wsems, sems) = refs[9:]
+    (weights, table, lines, sums, src, plane, chosen, dst, v_links, v_coef, v_land, edge, wsems, sems) = refs[9:]
     section = lax.axis_index("sec")
 
     @pl.when(section == 0)
@@ -321,7 +328,7 @@
         for r, field in enumerate([height[:BLK], u, v, new_temp]):
             keep[r * BLK : (r + 1) * BLK] = field
         surface = [new_temp, ice[:BLK], u, v]
-        run_tiles(surface, tiles, weights, wsems, SEA_AHEAD, src, dst, table, sums, [copies[0], chosen_in])
+        run_tiles(surface, tiles, weights, wsems, SEA_AHEAD, src, dst, table, lines, sums, [copies[0], chosen_in])
         write_messages(sums, outs, handed, count, SURF * BLK, SURF_HALO, 1)
 
 
@@ -409,6 +416,7 @@
         return [
             pltpu.VMEM((recv_count, slots, TILE, TILE), jnp.bfloat16),
             pltpu.VMEM((BLK * (BLK + 1), rows, TILE), jnp.bfloat16),
+            pltpu.VMEM((rows + BLK, TILE), f32),
             pltpu.VMEM((recv_count, rows, TILE), f32),
             pltpu.SMEM((recv_count, slots), i32),
             pltpu.VMEM((recv_count, slots, count), i32),

time: 55 us -> 54.8 us (level)
  no operation moved by 1% of the time
where the time goes in v7:
time: 54.8 us; the launch traced here: 54.7 us
  starting transfers between devices  32.9 us (60%)
  waiting for transfers between devices  13.3 us (24%)
  Pallas kernels  8.21 us (15%)
    ppermute x12, starting transfers between devices, exchange(): got.append(lax.ppermute(payload, AXES, pairs))  22.7 us
    ppermute x12, waiting for transfers between devices, exchange(): got.append(lax.ppermute(payload, AXES, pairs))  8.68 us
    ppermute x2, starting transfers between devices, exchange(): crossed = lax.ppermute(handed, 'sec', swap)  7.13 us
    pallas_call x1, Pallas kernels, body(): pl.pallas_call(lambda *r: sea_kernel(count, *r), name='sea_remap', out_sh...  6.52 us
    ppermute x2, starting transfers between devices, exchange(): return (here, lax.ppermute(here, 'sec', swap))  3.08 us
    ppermute x2, waiting for transfers between devices, exchange(): crossed = lax.ppermute(handed, 'sec', swap)  2.47 us
    ppermute x2, waiting for transfers between devices, exchange(): return (here, lax.ppermute(here, 'sec', swap))  2.12 us
  transfers between devices with their start and end apart: 16, of which 9 were waited for; matrix products, arithmetic and copies ran while one was open for 0% of the time, Pallas kernels for 0%

profile of v7, /device:TPU:1, one launch (start us, length us, event | category | flops | bytes accessed | tf_op | source)
XLA Modules:
  0.0 54.7 jit_solution(15827088591092984785)
XLA Ops:
  0.0 1.1 %flux_remap.1 = (f32[104,128]{1,0:T(8,128)S(1)}, f32[80,128]{1,0:T(8,128)S(1)}, f32[24,128]{1,0:T(8,128)S(1)}, f32[104,128]{1,0:T(8,128)S(1)}, f32[104,128]{1,0:...) custom-call(f32[1,8,1024]{2,1,0:T(8,128)} %r_0_.1, ...), custom_call_target="tpu_custom_call" | custom-call | flops 201326592 | bytes 12582912 | tf_op jit(solution)/shard_map/flux_remap/pallas_call | solution.py:431
  1.1 7.0 %collective-permute-start = (f32[440,128]{1,0:T(8,128)S(1)}, f32[440,128]{1,0:T(8,128)S(1)}, u32[]{:S(2)}, u32[]{:S(2)}) collective-permute-start(f32[440,128]{1,0:T(8,128)S(1)} %get-tuple-element.26), channel_id=1, source_target_pairs={{0,64},{64,0},{1,65},{65,1},{2,66},{66,2},{3,67},{67,3},{4,68},{68... | collective-permute-start | bytes 675848 | tf_op jit(solution)/shard_map/ppermute | solution.py:367
  8.1 1.1 %collective-permute-done = f32[440,128]{1,0:T(8,128)S(1)} collective-permute-done((f32[440,128]{1,0:T(8,128)S(1)}, f32[440,128]{1,0:T(8,128)S(1)}, u32[]{:S(2)}, u32[]{:S(2)}) %collective-permute-start) | collective-permute-done | bytes 225312 | tf_op jit(solution)/shard_map/ppermute | solution.py:367
  9.3 8.6 %collective-permute-start.2 = (f32[160,128]{1,0:T(8,128)S(1)}, f32[160,128]{1,0:T(8,128)S(1)}, u32[]{:S(2)}, u32[]{:S(2)}) collective-permute-start(f32[160,128]{1,0:T(8,128)S(1)} %pad_maximum_fusion), channel_id=1, source_target_pairs={{0,1},{1,2},{2,3},{3,4},{4,5},{5,6},{6,7},{7,8},{8,9},{9,10},{10,1... | collective-permute-start | bytes 245768 | tf_op jit(solution)/shard_map/ppermute | solution.py:384
  17.8 0.0 collective-permute-start.1
  17.8 1.5 %collective-permute-start.3 = (f32[104,128]{1,0:T(8,128)S(1)}, f32[104,128]{1,0:T(8,128)S(1)}, u32[]{:S(2)}, u32[]{:S(2)}) collective-permute-start(f32[104,128]{1,0:T(8,128)S(1)} %get-tuple-element.46), channel_id=1, source_target_pairs={{0,2},{1,3},{2,4},{3,5},{4,6},{5,7},{6,8},{7,9},{8,10},{9,11},{10,... | collective-permute-start | bytes 159752 | tf_op jit(solution)/shard_map/ppermute | solution.py:384
  19.3 0.5 collective-permute-start.4
  19.9 4.1 %collective-permute-start.5 = (f32[24,128]{1,0:T(8,128)S(1)}, f32[24,128]{1,0:T(8,128)S(1)}, u32[]{:S(2)}, u32[]{:S(2)}) collective-permute-start(f32[24,128]{1,0:T(8,128)S(1)} %get-tuple-element.44), channel_id=1, source_target_pairs={{0,31},{1,32},{2,33},{3,34},{4,35},{5,36},{6,37},{7,38},{8,39},{9,... | collective-permute-start | bytes 36872 | tf_op jit(solution)/shard_map/ppermute | solution.py:384
  24.0 0.0 collective-permute-done.1
  24.0 0.2 collective-permute-start.6
  24.2 0.0 collective-permute-done.3
  24.2 0.0 collective-permute-done.2
  24.2 0.0 collective-permute-done.4
  24.2 2.4 %collective-permute-done.5 = f32[24,128]{1,0:T(8,128)S(1)} collective-permute-done((f32[24,128]{1,0:T(8,128)S(1)}, f32[24,128]{1,0:T(8,128)S(1)}, u32[]{:S(2)}, u32[]{:S(2)}) %collective-permute-start.5) | collective-permute-done | bytes 12320 | tf_op jit(solution)/shard_map/ppermute | solution.py:384
  26.6 0.0 collective-permute-done.6
  26.7 3.0 %collective-permute-start.7 = (f32[160,128]{1,0:T(8,128)S(1)}, f32[160,128]{1,0:T(8,128)S(1)}, u32[]{:S(2)}, u32[]{:S(2)}) collective-permute-start(f32[160,128]{1,0:T(8,128)S(1)} %pad_maximum_fusion.1.r_0_), channel_id=1, source_target_pairs={{0,64},{64,0},{1,65},{65,1},{2,66},{66,2},{3,67},{67,3},{4,68},{68... | collective-permute-start | bytes 245768 | tf_op jit(solution)/shard_map/ppermute | solution.py:390
  29.7 0.9 %collective-permute-done.7.r_1_ = f32[160,128]{1,0:T(8,128)S(1)} collective-permute-done((f32[160,128]{1,0:T(8,128)S(1)}, f32[160,128]{1,0:T(8,128)S(1)}, u32[]{:S(2)}, u32[]{:S(2)}) %collective-permute-start.7) | collective-permute-done | bytes 81952 | tf_op jit(solution)/shard_map/ppermute | solution.py:390
  30.6 6.5 %sea_remap.1 = (f32[64,128]{1,0:T(8,128)S(1)}, f32[32,128]{1,0:T(8,128)S(1)}, f32[32,128]{1,0:T(8,128)S(1)}, f32[64,128]{1,0:T(8,128)S(1)}, f32[64,128]{1,0:T(8,...) custom-call(f32[160,128]{1,0:T(8,128)S(1)} %pad_maximum_fusion.1.r_0_, ...), custom_call_target="tpu_custom_call" | custom-call | flops 201326592 | bytes 12582912 | tf_op jit(solution)/shard_map/sea_remap/pallas_call | solution.py:455
  37.1 0.1 collective-permute-start.8
  37.2 1.4 %collective-permute-done.8 = f32[288,128]{1,0:T(8,128)S(1)} collective-permute-done((f32[288,128]{1,0:T(8,128)S(1)}, f32[288,128]{1,0:T(8,128)S(1)}, u32[]{:S(2)}, u32[]{:S(2)}) %collective-permute-start.8) | collective-permute-done | bytes 147488 | tf_op jit(solution)/shard_map/ppermute | solution.py:367
  38.6 0.1 collective-permute-start.10
  38.7 1.1 %collective-permute-start.11 = (f32[64,128]{1,0:T(8,128)S(1)}, f32[64,128]{1,0:T(8,128)S(1)}, u32[]{:S(2)}, u32[]{:S(2)}) collective-permute-start(f32[64,128]{1,0:T(8,128)S(1)} %get-tuple-element.52), channel_id=1, source_target_pairs={{64,66},{65,67},{66,68},{67,69},{68,70},{69,71},{70,72},{71,73},{7... | collective-permute-start | bytes 98312 | tf_op jit(solution)/shard_map/ppermute | solution.py:384
  39.8 0.0 collective-permute-start.9
  39.8 2.5 %collective-permute-start.12 = (f32[32,128]{1,0:T(8,128)S(1)}, f32[32,128]{1,0:T(8,128)S(1)}, u32[]{:S(2)}, u32[]{:S(2)}) collective-permute-start(f32[32,128]{1,0:T(8,128)S(1)} %get-tuple-element.48), channel_id=1, source_target_pairs={{64,96},{65,97},{66,98},{67,99},{68,100},{69,101},{70,102},{71,103... | collective-permute-start | bytes 49160 | tf_op jit(solution)/shard_map/ppermute | solution.py:384
  42.3 4.1 %collective-permute-start.13 = (f32[32,128]{1,0:T(8,128)S(1)}, f32[32,128]{1,0:T(8,128)S(1)}, u32[]{:S(2)}, u32[]{:S(2)}) collective-permute-start(f32[32,128]{1,0:T(8,128)S(1)} %get-tuple-element.50), channel_id=1, source_target_pairs={{64,95},{65,96},{66,97},{67,98},{68,99},{69,100},{70,101},{71,102}... | collective-permute-start | bytes 49160 | tf_op jit(solution)/shard_map/ppermute | solution.py:384
  46.5 0.4 collective-permute-done.10
  46.8 0.0 collective-permute-start.14
  46.8 0.6 %collective-permute-done.11 = f32[64,128]{1,0:T(8,128)S(1)} collective-permute-done((f32[64,128]{1,0:T(8,128)S(1)}, f32[64,128]{1,0:T(8,128)S(1)}, u32[]{:S(2)}, u32[]{:S(2)}) %collective-permute-start.11) | collective-permute-done | bytes 32800 | tf_op jit(solution)/shard_map/ppermute | solution.py:384
  47.4 0.1 collective-permute-done.9
  47.6 0.0 collective-permute-done.12
  47.6 0.0 collective-permute-done.13
  47.6 5.1 %collective-permute-done.14 = f32[32,128]{1,0:T(8,128)S(1)} collective-permute-done((f32[32,128]{1,0:T(8,128)S(1)}, f32[32,128]{1,0:T(8,128)S(1)}, u32[]{:S(2)}, u32[]{:S(2)}) %collective-permute-start.14) | collective-permute-done | bytes 16416 | tf_op jit(solution)/shard_map/ppermute | solution.py:384
  52.8 0.1 collective-permute-start.15
  52.9 1.2 %collective-permute-done.15.there = f32[64,128]{1,0:T(8,128)S(1)} collective-permute-done((f32[64,128]{1,0:T(8,128)S(1)}, f32[64,128]{1,0:T(8,128)S(1)}, u32[]{:S(2)}, u32[]{:S(2)}) %collective-permute-start.15) | collective-permute-done | bytes 32800 | tf_op jit(solution)/shard_map/ppermute | solution.py:390
  54.1 0.6 %smooth.1 = f32[1,4,1024]{2,1,0:T(4,128)} custom-call(f32[64,128]{1,0:T(8,128)S(1)} %pad_maximum_fusion.2.here, f32[64,128]{1,0:T(8,128)S(1)} %collective-permute-done.15.there, f32[152,128]{1,0:T(8,128)S(1)} %get-tuple-element.42.keep), custom_call_target="tpu_custom_call" | custom-call | tf_op jit(solution)/shard_map/smooth/pallas_call | solution.py:476
  (15 shorter events, 0.1 us)
Async XLA Ops:
  1.1 8.2 %collective-permute-start = (f32[440,128]{1,0:T(8,128)S(1)}, f32[440,128]{1,0:T(8,128)S(1)}, u32[]{:S(2)}, u32[]{:S(2)}) collective-permute-start(f32[440,128]{1,0:T(8,128)S(1)} %get-tuple-element.26), channel_id=1, source_target_pairs={{0,64},{64,0},{1,65},{65,1},{2,66},{66,2},{3,67},{67,3},{4,68},{68... | collective-permute-start | bytes 675848 | tf_op jit(solution)/shard_map/ppermute | solution.py:367
  9.3 14.9 %collective-permute-start.2 = (f32[160,128]{1,0:T(8,128)S(1)}, f32[160,128]{1,0:T(8,128)S(1)}, u32[]{:S(2)}, u32[]{:S(2)}) collective-permute-start(f32[160,128]{1,0:T(8,128)S(1)} %pad_maximum_fusion), channel_id=1, source_target_pairs={{0,1},{1,2},{2,3},{3,4},{4,5},{5,6},{6,7},{7,8},{8,9},{9,10},{10,1... | collective-permute-start | bytes 245768 | tf_op jit(solution)/shard_map/ppermute | solution.py:384
  17.8 6.1 %collective-permute-start.1 = (f32[104,128]{1,0:T(8,128)S(1)}, f32[104,128]{1,0:T(8,128)S(1)}, u32[]{:S(2)}, u32[]{:S(2)}) collective-permute-start(f32[104,128]{1,0:T(8,128)S(1)} %get-tuple-element.45), channel_id=1, source_target_pairs={{0,3},{1,4},{2,5},{3,6},{4,7},{5,8},{6,9},{7,10},{8,11},{9,12},{10... | collective-permute-start | bytes 159752 | tf_op jit(solution)/shard_map/ppermute | solution.py:384
  17.8 6.3 %collective-permute-start.3 = (f32[104,128]{1,0:T(8,128)S(1)}, f32[104,128]{1,0:T(8,128)S(1)}, u32[]{:S(2)}, u32[]{:S(2)}) collective-permute-start(f32[104,128]{1,0:T(8,128)S(1)} %get-tuple-element.46), channel_id=1, source_target_pairs={{0,2},{1,3},{2,4},{3,5},{4,6},{5,7},{6,8},{7,9},{8,10},{9,11},{10,... | collective-permute-start | bytes 159752 | tf_op jit(solution)/shard_map/ppermute | solution.py:384
  19.3 4.8 %collective-permute-start.4 = (f32[80,128]{1,0:T(8,128)S(1)}, f32[80,128]{1,0:T(8,128)S(1)}, u32[]{:S(2)}, u32[]{:S(2)}) collective-permute-start(f32[80,128]{1,0:T(8,128)S(1)} %slice_select_fusion.3), channel_id=1, source_target_pairs={{0,32},{1,33},{2,34},{3,35},{4,36},{5,37},{6,38},{7,39},{8,40},{9,... | collective-permute-start | bytes 122888 | tf_op jit(solution)/shard_map/ppermute | solution.py:384
  19.9 6.8 %collective-permute-start.5 = (f32[24,128]{1,0:T(8,128)S(1)}, f32[24,128]{1,0:T(8,128)S(1)}, u32[]{:S(2)}, u32[]{:S(2)}) collective-permute-start(f32[24,128]{1,0:T(8,128)S(1)} %get-tuple-element.44), channel_id=1, source_target_pairs={{0,31},{1,32},{2,33},{3,34},{4,35},{5,36},{6,37},{7,38},{8,39},{9,... | collective-permute-start | bytes 36872 | tf_op jit(solution)/shard_map/ppermute | solution.py:384
  24.0 2.7 %collective-permute-start.6 = (f32[24,128]{1,0:T(8,128)S(1)}, f32[24,128]{1,0:T(8,128)S(1)}, u32[]{:S(2)}, u32[]{:S(2)}) collective-permute-start(f32[24,128]{1,0:T(8,128)S(1)} %get-tuple-element.43), channel_id=1, source_target_pairs={{0,4},{1,5},{2,6},{3,7},{4,8},{5,9},{6,10},{7,11},{8,12},{9,13},{1... | collective-permute-start | bytes 36872 | tf_op jit(solution)/shard_map/ppermute | solution.py:384
  26.7 3.9 %collective-permute-start.7 = (f32[160,128]{1,0:T(8,128)S(1)}, f32[160,128]{1,0:T(8,128)S(1)}, u32[]{:S(2)}, u32[]{:S(2)}) collective-permute-start(f32[160,128]{1,0:T(8,128)S(1)} %pad_maximum_fusion.1.r_0_), channel_id=1, source_target_pairs={{0,64},{64,0},{1,65},{65,1},{2,66},{66,2},{3,67},{67,3},{4,68},{68... | collective-permute-start | bytes 245768 | tf_op jit(solution)/shard_map/ppermute | solution.py:390
  37.1 1.5 %collective-permute-start.8 = (f32[288,128]{1,0:T(8,128)S(1)}, f32[288,128]{1,0:T(8,128)S(1)}, u32[]{:S(2)}, u32[]{:S(2)}) collective-permute-start(f32[288,128]{1,0:T(8,128)S(1)} %get-tuple-element.36), channel_id=1, source_target_pairs={{0,64},{64,0},{1,65},{65,1},{2,66},{66,2},{3,67},{67,3},{4,68},{68... | collective-permute-start | bytes 442376 | tf_op jit(solution)/shard_map/ppermute | solution.py:367
  38.6 8.3 %collective-permute-start.10 = (f32[64,128]{1,0:T(8,128)S(1)}, f32[64,128]{1,0:T(8,128)S(1)}, u32[]{:S(2)}, u32[]{:S(2)}) collective-permute-start(f32[64,128]{1,0:T(8,128)S(1)} %get-tuple-element.51), channel_id=1, source_target_pairs={{64,65},{65,66},{66,67},{67,68},{68,69},{69,70},{70,71},{71,72},{7... | collective-permute-start | bytes 98312 | tf_op jit(solution)/shard_map/ppermute | solution.py:384
  38.7 8.8 %collective-permute-start.11 = (f32[64,128]{1,0:T(8,128)S(1)}, f32[64,128]{1,0:T(8,128)S(1)}, u32[]{:S(2)}, u32[]{:S(2)}) collective-permute-start(f32[64,128]{1,0:T(8,128)S(1)} %get-tuple-element.52), channel_id=1, source_target_pairs={{64,66},{65,67},{66,68},{67,69},{68,70},{69,71},{70,72},{71,73},{7... | collective-permute-start | bytes 98312 | tf_op jit(solution)/shard_map/ppermute | solution.py:384
  39.8 7.8 %collective-permute-start.9 = (f32[64,128]{1,0:T(8,128)S(1)}, f32[64,128]{1,0:T(8,128)S(1)}, u32[]{:S(2)}, u32[]{:S(2)}) collective-permute-start(f32[64,128]{1,0:T(8,128)S(1)} %get-tuple-element.53), channel_id=1, source_target_pairs={{64,67},{65,68},{66,69},{67,70},{68,71},{69,72},{70,73},{71,74},{7... | collective-permute-start | bytes 98312 | tf_op jit(solution)/shard_map/ppermute | solution.py:384
  39.8 7.8 %collective-permute-start.12 = (f32[32,128]{1,0:T(8,128)S(1)}, f32[32,128]{1,0:T(8,128)S(1)}, u32[]{:S(2)}, u32[]{:S(2)}) collective-permute-start(f32[32,128]{1,0:T(8,128)S(1)} %get-tuple-element.48), channel_id=1, source_target_pairs={{64,96},{65,97},{66,98},{67,99},{68,100},{69,101},{70,102},{71,103... | collective-permute-start | bytes 49160 | tf_op jit(solution)/shard_map/ppermute | solution.py:384
  42.3 5.3 %collective-permute-start.13 = (f32[32,128]{1,0:T(8,128)S(1)}, f32[32,128]{1,0:T(8,128)S(1)}, u32[]{:S(2)}, u32[]{:S(2)}) collective-permute-start(f32[32,128]{1,0:T(8,128)S(1)} %get-tuple-element.50), channel_id=1, source_target_pairs={{64,95},{65,96},{66,97},{67,98},{68,99},{69,100},{70,101},{71,102}... | collective-permute-start | bytes 49160 | tf_op jit(solution)/shard_map/ppermute | solution.py:384
  46.8 5.9 %collective-permute-start.14 = (f32[32,128]{1,0:T(8,128)S(1)}, f32[32,128]{1,0:T(8,128)S(1)}, u32[]{:S(2)}, u32[]{:S(2)}) collective-permute-start(f32[32,128]{1,0:T(8,128)S(1)} %get-tuple-element.49), channel_id=1, source_target_pairs={{64,68},{65,69},{66,70},{67,71},{68,72},{69,73},{70,74},{71,75},{7... | collective-permute-start | bytes 49160 | tf_op jit(solution)/shard_map/ppermute | solution.py:384
  52.8 1.3 %collective-permute-start.15 = (f32[64,128]{1,0:T(8,128)S(1)}, f32[64,128]{1,0:T(8,128)S(1)}, u32[]{:S(2)}, u32[]{:S(2)}) collective-permute-start(f32[64,128]{1,0:T(8,128)S(1)} %pad_maximum_fusion.2.here), channel_id=1, source_target_pairs={{0,64},{64,0},{1,65},{65,1},{2,66},{66,2},{3,67},{67,3},{4,68},{68... | collective-permute-start | bytes 98312 | tf_op jit(solution)/shard_map/ppermute | solution.py:390

commit v8 on v7

--- a/solution.py
+++ b/solution.py
@@ -306,7 +306,12 @@
         mixed = 1.0 + softplus(near(7))
         drag = 0.3 * (1.0 - ice)
         push_u, push_v, push_h = drag * force_wide(0), drag * force_wide(1), 0.1 * force_wide(8)
-        for step in range(SUBSTEPS):
+        copies[1].wait()
+        chosen_in = own_targets(plane, chosen, dst, sems.at[2])
+        start_pair(tiles, weights, wsems, 1)
+
+        def substep(_, fields):
+            height, flow_u, flow_v = fields
             slopes = spread(height)
             grad_x = sum(w * s for w, s in zip(grad_wx, slopes))
             grad_y = sum(w * s for w, s in zip(grad_wy, slopes))
@@ -315,12 +320,9 @@
             moved_u = spread(depth * next_u)
             moved_v = spread(depth * next_v)
             moved = sum(wx * a + wy * b for wx, wy, a, b in zip(grad_wx, grad_wy, moved_u, moved_v))
-            height = height - 0.5 * moved + push_h
-            flow_u, flow_v = next_u, next_v
-            if step == 0:
-                copies[1].wait()
-                chosen_in = own_targets(plane, chosen, dst, sems.at[2])
-                start_pair(tiles, weights, wsems, 1)
+            return height - 0.5 * moved + push_h, next_u, next_v
+
+        height, flow_u, flow_v = lax.fori_loop(0, SUBSTEPS, substep, (height, flow_u, flow_v))
         for n in range(2, SEA_AHEAD):
             start_pair(tiles, weights, wsems, n)
         new_temp = near(4) + 0.2 * near(LAND) * force(9) / mixed

time: 54.8 us -> 54.8 us (level)
  no operation moved by 1% of the time
where the time goes in v8:
time: 54.8 us; the launch traced here: 54.7 us
  starting transfers between devices  32.9 us (60%)
  waiting for transfers between devices  13.3 us (24%)
  Pallas kernels  8.21 us (15%)
    ppermute x12, starting transfers between devices, exchange(): got.append(lax.ppermute(payload, AXES, pairs))  22.7 us
    ppermute x12, waiting for transfers between devices, exchange(): got.append(lax.ppermute(payload, AXES, pairs))  8.69 us
    ppermute x2, starting transfers between devices, exchange(): crossed = lax.ppermute(handed, 'sec', swap)  7.13 us
    pallas_call x1, Pallas kernels, body(): pl.pallas_call(lambda *r: sea_kernel(count, *r), name='sea_remap', out_sh...  6.52 us
    ppermute x2, starting transfers between devices, exchange(): return (here, lax.ppermute(here, 'sec', swap))  3.08 us
    ppermute x2, waiting for transfers between devices, exchange(): crossed = lax.ppermute(handed, 'sec', swap)  2.47 us
    ppermute x2, waiting for transfers between devices, exchange(): return (here, lax.ppermute(here, 'sec', swap))  2.12 us
  transfers between devices with their start and end apart: 16, of which 9 were waited for; matrix products, arithmetic and copies ran while one was open for 0% of the time, Pallas kernels for 0%

profile of v8, /device:TPU:1, one launch (start us, length us, event | category | flops | bytes accessed | tf_op | source)
XLA Modules:
  0.0 54.7 jit_solution(6363125358721593628)
XLA Ops:
  0.0 1.1 %flux_remap.1 = (f32[104,128]{1,0:T(8,128)S(1)}, f32[80,128]{1,0:T(8,128)S(1)}, f32[24,128]{1,0:T(8,128)S(1)}, f32[104,128]{1,0:T(8,128)S(1)}, f32[104,128]{1,0:...) custom-call(f32[1,8,1024]{2,1,0:T(8,128)} %r_0_.1, ...), custom_call_target="tpu_custom_call" | custom-call | flops 201326592 | bytes 12582912 | tf_op jit(solution)/shard_map/flux_remap/pallas_call | solution.py:433
  1.1 7.0 %collective-permute-start = (f32[440,128]{1,0:T(8,128)S(1)}, f32[440,128]{1,0:T(8,128)S(1)}, u32[]{:S(2)}, u32[]{:S(2)}) collective-permute-start(f32[440,128]{1,0:T(8,128)S(1)} %get-tuple-element.26), channel_id=1, source_target_pairs={{0,64},{64,0},{1,65},{65,1},{2,66},{66,2},{3,67},{67,3},{4,68},{68... | collective-permute-start | bytes 675848 | tf_op jit(solution)/shard_map/ppermute | solution.py:369
  8.1 1.1 %collective-permute-done = f32[440,128]{1,0:T(8,128)S(1)} collective-permute-done((f32[440,128]{1,0:T(8,128)S(1)}, f32[440,128]{1,0:T(8,128)S(1)}, u32[]{:S(2)}, u32[]{:S(2)}) %collective-permute-start) | collective-permute-done | bytes 225312 | tf_op jit(solution)/shard_map/ppermute | solution.py:369
  9.3 8.6 %collective-permute-start.2 = (f32[160,128]{1,0:T(8,128)S(1)}, f32[160,128]{1,0:T(8,128)S(1)}, u32[]{:S(2)}, u32[]{:S(2)}) collective-permute-start(f32[160,128]{1,0:T(8,128)S(1)} %pad_maximum_fusion), channel_id=1, source_target_pairs={{0,1},{1,2},{2,3},{3,4},{4,5},{5,6},{6,7},{7,8},{8,9},{9,10},{10,1... | collective-permute-start | bytes 245768 | tf_op jit(solution)/shard_map/ppermute | solution.py:386
  17.9 0.0 collective-permute-start.1
  17.9 1.5 %collective-permute-start.3 = (f32[104,128]{1,0:T(8,128)S(1)}, f32[104,128]{1,0:T(8,128)S(1)}, u32[]{:S(2)}, u32[]{:S(2)}) collective-permute-start(f32[104,128]{1,0:T(8,128)S(1)} %get-tuple-element.46), channel_id=1, source_target_pairs={{0,2},{1,3},{2,4},{3,5},{4,6},{5,7},{6,8},{7,9},{8,10},{9,11},{10,... | collective-permute-start | bytes 159752 | tf_op jit(solution)/shard_map/ppermute | solution.py:386
  19.3 0.5 collective-permute-start.4
  19.9 4.1 %collective-permute-start.5 = (f32[24,128]{1,0:T(8,128)S(1)}, f32[24,128]{1,0:T(8,128)S(1)}, u32[]{:S(2)}, u32[]{:S(2)}) collective-permute-start(f32[24,128]{1,0:T(8,128)S(1)} %get-tuple-element.44), channel_id=1, source_target_pairs={{0,31},{1,32},{2,33},{3,34},{4,35},{5,36},{6,37},{7,38},{8,39},{9,... | collective-permute-start | bytes 36872 | tf_op jit(solution)/shard_map/ppermute | solution.py:386
  24.0 0.0 collective-permute-done.1
  24.0 0.2 collective-permute-start.6
  24.2 0.0 collective-permute-done.3
  24.2 0.0 collective-permute-done.2
  24.2 0.0 collective-permute-done.4
  24.2 2.4 %collective-permute-done.5 = f32[24,128]{1,0:T(8,128)S(1)} collective-permute-done((f32[24,128]{1,0:T(8,128)S(1)}, f32[24,128]{1,0:T(8,128)S(1)}, u32[]{:S(2)}, u32[]{:S(2)}) %collective-permute-start.5) | collective-permute-done | bytes 12320 | tf_op jit(solution)/shard_map/ppermute | solution.py:386
  26.6 0.0 collective-permute-done.6
  26.7 3.0 %collective-permute-start.7 = (f32[160,128]{1,0:T(8,128)S(1)}, f32[160,128]{1,0:T(8,128)S(1)}, u32[]{:S(2)}, u32[]{:S(2)}) collective-permute-start(f32[160,128]{1,0:T(8,128)S(1)} %pad_maximum_fusion.1.r_0_), channel_id=1, source_target_pairs={{0,64},{64,0},{1,65},{65,1},{2,66},{66,2},{3,67},{67,3},{4,68},{68... | collective-permute-start | bytes 245768 | tf_op jit(solution)/shard_map/ppermute | solution.py:392
  29.7 0.9 %collective-permute-done.7.r_1_ = f32[160,128]{1,0:T(8,128)S(1)} collective-permute-done((f32[160,128]{1,0:T(8,128)S(1)}, f32[160,128]{1,0:T(8,128)S(1)}, u32[]{:S(2)}, u32[]{:S(2)}) %collective-permute-start.7) | collective-permute-done | bytes 81952 | tf_op jit(solution)/shard_map/ppermute | solution.py:392
  30.6 6.5 %sea_remap.1 = (f32[64,128]{1,0:T(8,128)S(1)}, f32[32,128]{1,0:T(8,128)S(1)}, f32[32,128]{1,0:T(8,128)S(1)}, f32[64,128]{1,0:T(8,128)S(1)}, f32[64,128]{1,0:T(8,...) custom-call(f32[160,128]{1,0:T(8,128)S(1)} %pad_maximum_fusion.1.r_0_, ...), custom_call_target="tpu_custom_call" | custom-call | flops 201326592 | bytes 12582912 | tf_op jit(solution)/shard_map/sea_remap/pallas_call | solution.py:457
  37.1 0.1 collective-permute-start.8
  37.2 1.4 %collective-permute-done.8 = f32[288,128]{1,0:T(8,128)S(1)} collective-permute-done((f32[288,128]{1,0:T(8,128)S(1)}, f32[288,128]{1,0:T(8,128)S(1)}, u32[]{:S(2)}, u32[]{:S(2)}) %collective-permute-start.8) | collective-permute-done | bytes 147488 | tf_op jit(solution)/shard_map/ppermute | solution.py:369
  38.6 0.1 collective-permute-start.10
  38.7 1.1 %collective-permute-start.11 = (f32[64,128]{1,0:T(8,128)S(1)}, f32[64,128]{1,0:T(8,128)S(1)}, u32[]{:S(2)}, u32[]{:S(2)}) collective-permute-start(f32[64,128]{1,0:T(8,128)S(1)} %get-tuple-element.52), channel_id=1, source_target_pairs={{64,66},{65,67},{66,68},{67,69},{68,70},{69,71},{70,72},{71,73},{7... | collective-permute-start | bytes 98312 | tf_op jit(solution)/shard_map/ppermute | solution.py:386
  39.8 0.0 collective-permute-start.9
  39.8 2.5 %collective-permute-start.12 = (f32[32,128]{1,0:T(8,128)S(1)}, f32[32,128]{1,0:T(8,128)S(1)}, u32[]{:S(2)}, u32[]{:S(2)}) collective-permute-start(f32[32,128]{1,0:T(8,128)S(1)} %get-tuple-element.48), channel_id=1, source_target_pairs={{64,96},{65,97},{66,98},{67,99},{68,100},{69,101},{70,102},{71,103... | collective-permute-start | bytes 49160 | tf_op jit(solution)/shard_map/ppermute | solution.py:386
  42.3 4.1 %collective-permute-start.13 = (f32[32,128]{1,0:T(8,128)S(1)}, f32[32,128]{1,0:T(8,128)S(1)}, u32[]{:S(2)}, u32[]{:S(2)}) collective-permute-start(f32[32,128]{1,0:T(8,128)S(1)} %get-tuple-element.50), channel_id=1, source_target_pairs={{64,95},{65,96},{66,97},{67,98},{68,99},{69,100},{70,101},{71,102}... | collective-permute-start | bytes 49160 | tf_op jit(solution)/shard_map/ppermute | solution.py:386
  46.4 0.4 collective-permute-done.10
  46.8 0.0 collective-permute-start.14
  46.8 0.6 %collective-permute-done.11 = f32[64,128]{1,0:T(8,128)S(1)} collective-permute-done((f32[64,128]{1,0:T(8,128)S(1)}, f32[64,128]{1,0:T(8,128)S(1)}, u32[]{:S(2)}, u32[]{:S(2)}) %collective-permute-start.11) | collective-permute-done | bytes 32800 | tf_op jit(solution)/shard_map/ppermute | solution.py:386
  47.4 0.1 collective-permute-done.9
  47.6 0.0 collective-permute-done.12
  47.6 0.0 collective-permute-done.13
  47.6 5.1 %collective-permute-done.14 = f32[32,128]{1,0:T(8,128)S(1)} collective-permute-done((f32[32,128]{1,0:T(8,128)S(1)}, f32[32,128]{1,0:T(8,128)S(1)}, u32[]{:S(2)}, u32[]{:S(2)}) %collective-permute-start.14) | collective-permute-done | bytes 16416 | tf_op jit(solution)/shard_map/ppermute | solution.py:386
  52.8 0.1 collective-permute-start.15
  52.9 1.2 %collective-permute-done.15.there = f32[64,128]{1,0:T(8,128)S(1)} collective-permute-done((f32[64,128]{1,0:T(8,128)S(1)}, f32[64,128]{1,0:T(8,128)S(1)}, u32[]{:S(2)}, u32[]{:S(2)}) %collective-permute-start.15) | collective-permute-done | bytes 32800 | tf_op jit(solution)/shard_map/ppermute | solution.py:392
  54.1 0.6 %smooth.1 = f32[1,4,1024]{2,1,0:T(4,128)} custom-call(f32[64,128]{1,0:T(8,128)S(1)} %pad_maximum_fusion.2.here, f32[64,128]{1,0:T(8,128)S(1)} %collective-permute-done.15.there, f32[152,128]{1,0:T(8,128)S(1)} %get-tuple-element.42.keep), custom_call_target="tpu_custom_call" | custom-call | tf_op jit(solution)/shard_map/smooth/pallas_call | solution.py:478
  (15 shorter events, 0.1 us)
Async XLA Ops:
  1.1 8.2 %collective-permute-start = (f32[440,128]{1,0:T(8,128)S(1)}, f32[440,128]{1,0:T(8,128)S(1)}, u32[]{:S(2)}, u32[]{:S(2)}) collective-permute-start(f32[440,128]{1,0:T(8,128)S(1)} %get-tuple-element.26), channel_id=1, source_target_pairs={{0,64},{64,0},{1,65},{65,1},{2,66},{66,2},{3,67},{67,3},{4,68},{68... | collective-permute-start | bytes 675848 | tf_op jit(solution)/shard_map/ppermute | solution.py:369
  9.3 14.9 %collective-permute-start.2 = (f32[160,128]{1,0:T(8,128)S(1)}, f32[160,128]{1,0:T(8,128)S(1)}, u32[]{:S(2)}, u32[]{:S(2)}) collective-permute-start(f32[160,128]{1,0:T(8,128)S(1)} %pad_maximum_fusion), channel_id=1, source_target_pairs={{0,1},{1,2},{2,3},{3,4},{4,5},{5,6},{6,7},{7,8},{8,9},{9,10},{10,1... | collective-permute-start | bytes 245768 | tf_op jit(solution)/shard_map/ppermute | solution.py:386
  17.9 6.1 %collective-permute-start.1 = (f32[104,128]{1,0:T(8,128)S(1)}, f32[104,128]{1,0:T(8,128)S(1)}, u32[]{:S(2)}, u32[]{:S(2)}) collective-permute-start(f32[104,128]{1,0:T(8,128)S(1)} %get-tuple-element.45), channel_id=1, source_target_pairs={{0,3},{1,4},{2,5},{3,6},{4,7},{5,8},{6,9},{7,10},{8,11},{9,12},{10... | collective-permute-start | bytes 159752 | tf_op jit(solution)/shard_map/ppermute | solution.py:386
  17.9 6.3 %collective-permute-start.3 = (f32[104,128]{1,0:T(8,128)S(1)}, f32[104,128]{1,0:T(8,128)S(1)}, u32[]{:S(2)}, u32[]{:S(2)}) collective-permute-start(f32[104,128]{1,0:T(8,128)S(1)} %get-tuple-element.46), channel_id=1, source_target_pairs={{0,2},{1,3},{2,4},{3,5},{4,6},{5,7},{6,8},{7,9},{8,10},{9,11},{10,... | collective-permute-start | bytes 159752 | tf_op jit(solution)/shard_map/ppermute | solution.py:386
  19.3 4.8 %collective-permute-start.4 = (f32[80,128]{1,0:T(8,128)S(1)}, f32[80,128]{1,0:T(8,128)S(1)}, u32[]{:S(2)}, u32[]{:S(2)}) collective-permute-start(f32[80,128]{1,0:T(8,128)S(1)} %slice_select_fusion.3), channel_id=1, source_target_pairs={{0,32},{1,33},{2,34},{3,35},{4,36},{5,37},{6,38},{7,39},{8,40},{9,... | collective-permute-start | bytes 122888 | tf_op jit(solution)/shard_map/ppermute | solution.py:386
  19.9 6.8 %collective-permute-start.5 = (f32[24,128]{1,0:T(8,128)S(1)}, f32[24,128]{1,0:T(8,128)S(1)}, u32[]{:S(2)}, u32[]{:S(2)}) collective-permute-start(f32[24,128]{1,0:T(8,128)S(1)} %get-tuple-element.44), channel_id=1, source_target_pairs={{0,31},{1,32},{2,33},{3,34},{4,35},{5,36},{6,37},{7,38},{8,39},{9,... | collective-permute-start | bytes 36872 | tf_op jit(solution)/shard_map/ppermute | solution.py:386
  24.0 2.7 %collective-permute-start.6 = (f32[24,128]{1,0:T(8,128)S(1)}, f32[24,128]{1,0:T(8,128)S(1)}, u32[]{:S(2)}, u32[]{:S(2)}) collective-permute-start(f32[24,128]{1,0:T(8,128)S(1)} %get-tuple-element.43), channel_id=1, source_target_pairs={{0,4},{1,5},{2,6},{3,7},{4,8},{5,9},{6,10},{7,11},{8,12},{9,13},{1... | collective-permute-start | bytes 36872 | tf_op jit(solution)/shard_map/ppermute | solution.py:386
  26.7 3.9 %collective-permute-start.7 = (f32[160,128]{1,0:T(8,128)S(1)}, f32[160,128]{1,0:T(8,128)S(1)}, u32[]{:S(2)}, u32[]{:S(2)}) collective-permute-start(f32[160,128]{1,0:T(8,128)S(1)} %pad_maximum_fusion.1.r_0_), channel_id=1, source_target_pairs={{0,64},{64,0},{1,65},{65,1},{2,66},{66,2},{3,67},{67,3},{4,68},{68... | collective-permute-start | bytes 245768 | tf_op jit(solution)/shard_map/ppermute | solution.py:392
  37.1 1.5 %collective-permute-start.8 = (f32[288,128]{1,0:T(8,128)S(1)}, f32[288,128]{1,0:T(8,128)S(1)}, u32[]{:S(2)}, u32[]{:S(2)}) collective-permute-start(f32[288,128]{1,0:T(8,128)S(1)} %get-tuple-element.36), channel_id=1, source_target_pairs={{0,64},{64,0},{1,65},{65,1},{2,66},{66,2},{3,67},{67,3},{4,68},{68... | collective-permute-start | bytes 442376 | tf_op jit(solution)/shard_map/ppermute | solution.py:369
  38.6 8.3 %collective-permute-start.10 = (f32[64,128]{1,0:T(8,128)S(1)}, f32[64,128]{1,0:T(8,128)S(1)}, u32[]{:S(2)}, u32[]{:S(2)}) collective-permute-start(f32[64,128]{1,0:T(8,128)S(1)} %get-tuple-element.51), channel_id=1, source_target_pairs={{64,65},{65,66},{66,67},{67,68},{68,69},{69,70},{70,71},{71,72},{7... | collective-permute-start | bytes 98312 | tf_op jit(solution)/shard_map/ppermute | solution.py:386
  38.7 8.8 %collective-permute-start.11 = (f32[64,128]{1,0:T(8,128)S(1)}, f32[64,128]{1,0:T(8,128)S(1)}, u32[]{:S(2)}, u32[]{:S(2)}) collective-permute-start(f32[64,128]{1,0:T(8,128)S(1)} %get-tuple-element.52), channel_id=1, source_target_pairs={{64,66},{65,67},{66,68},{67,69},{68,70},{69,71},{70,72},{71,73},{7... | collective-permute-start | bytes 98312 | tf_op jit(solution)/shard_map/ppermute | solution.py:386
  39.8 7.8 %collective-permute-start.9 = (f32[64,128]{1,0:T(8,128)S(1)}, f32[64,128]{1,0:T(8,128)S(1)}, u32[]{:S(2)}, u32[]{:S(2)}) collective-permute-start(f32[64,128]{1,0:T(8,128)S(1)} %get-tuple-element.53), channel_id=1, source_target_pairs={{64,67},{65,68},{66,69},{67,70},{68,71},{69,72},{70,73},{71,74},{7... | collective-permute-start | bytes 98312 | tf_op jit(solution)/shard_map/ppermute | solution.py:386
  39.8 7.8 %collective-permute-start.12 = (f32[32,128]{1,0:T(8,128)S(1)}, f32[32,128]{1,0:T(8,128)S(1)}, u32[]{:S(2)}, u32[]{:S(2)}) collective-permute-start(f32[32,128]{1,0:T(8,128)S(1)} %get-tuple-element.48), channel_id=1, source_target_pairs={{64,96},{65,97},{66,98},{67,99},{68,100},{69,101},{70,102},{71,103... | collective-permute-start | bytes 49160 | tf_op jit(solution)/shard_map/ppermute | solution.py:386
  42.3 5.3 %collective-permute-start.13 = (f32[32,128]{1,0:T(8,128)S(1)}, f32[32,128]{1,0:T(8,128)S(1)}, u32[]{:S(2)}, u32[]{:S(2)}) collective-permute-start(f32[32,128]{1,0:T(8,128)S(1)} %get-tuple-element.50), channel_id=1, source_target_pairs={{64,95},{65,96},{66,97},{67,98},{68,99},{69,100},{70,101},{71,102}... | collective-permute-start | bytes 49160 | tf_op jit(solution)/shard_map/ppermute | solution.py:386
  46.8 5.9 %collective-permute-start.14 = (f32[32,128]{1,0:T(8,128)S(1)}, f32[32,128]{1,0:T(8,128)S(1)}, u32[]{:S(2)}, u32[]{:S(2)}) collective-permute-start(f32[32,128]{1,0:T(8,128)S(1)} %get-tuple-element.49), channel_id=1, source_target_pairs={{64,68},{65,69},{66,70},{67,71},{68,72},{69,73},{70,74},{71,75},{7... | collective-permute-start | bytes 49160 | tf_op jit(solution)/shard_map/ppermute | solution.py:386
  52.8 1.3 %collective-permute-start.15 = (f32[64,128]{1,0:T(8,128)S(1)}, f32[64,128]{1,0:T(8,128)S(1)}, u32[]{:S(2)}, u32[]{:S(2)}) collective-permute-start(f32[64,128]{1,0:T(8,128)S(1)} %pad_maximum_fusion.2.here), channel_id=1, source_target_pairs={{0,64},{64,0},{1,65},{65,1},{2,66},{66,2},{3,67},{67,3},{4,68},{68... | collective-permute-start | bytes 98312 | tf_op jit(solution)/shard_map/ppermute | solution.py:392
